TPU v7x, 128 devices: a whole 4x4x4 slice. The times are simulated.
128 devices in a mesh: gx: 32 (over z, x, core), gz: 4 (over y).
Axes of the slice: x: 4, y: 4, z: 4, core: 2. Of those that a mesh axis runs over, the one named last changes fastest.
Arguments:
- thermal_state: float32 [256, 64, 512], P('gx', None, 'gz'), may hold values from -6 to 6
- heat_spread_factor: float32 [256, 64, 512], P('gx', None, 'gz'), may hold values from 0.25 to 2
- heating_input: float32 [256, 64, 512], P('gx', None, 'gz'), may hold values from -400 to 400
Outputs:
- next_temperature: float32 [256, 64, 512], P('gx', None, 'gz')
All inputs are finite; a program needn't handle non-finite values.
Results may differ from a plain program's by a relative error of at most 0.0003.
Values sent between devices are 32-bit elements; how exact they have to be, the bound alone decides.
No kernel may reach another device: no remote copies, remote signals or barrier semaphores. Data moves between devices by JAX's collectives and lax.ppermute only.
A program may use at most 64 MiB of HBM per device.

v0:
```python
import jax
import jax.numpy as jnp
from jax import lax
from jax.sharding import PartitionSpec as P

SHARD_SPAN_WIDTH = 8
SHARD_SPAN_TALL = 128


half_theta = 0.5


def with_halo(block, sides, width):
    for axis, dim in sides:
        count = lax.axis_size(axis)
        forward = [(i, i + 1) for i in range(count - 1)]
        backward = [(target, source) for source, target in forward]
        low = lax.ppermute(
            lax.slice_in_dim(block, block.shape[dim] - width, None, axis=dim), axis, forward
        )
        high = lax.ppermute(lax.slice_in_dim(block, 0, width, axis=dim), axis, backward)
        block = jnp.concatenate([low, block, high], axis=dim)
    return block


def from_behind(block, axis, distance):
    devices = range(lax.axis_size(axis))
    route = [(i - distance, i) for i in devices if i - distance in devices]
    return lax.ppermute(block, axis, route)


def cut_range(values, start, stop, direction):
    return lax.slice_in_dim(values, start, stop, axis=direction % values.ndim)


def from_below(values, stride, direction):
    position = direction % values.ndim
    extent = values.shape[position]
    retained = cut_range(values, 0, extent - stride, direction)
    padding = jnp.zeros_like(cut_range(values, 0, stride, direction))
    return jnp.concatenate([padding, retained], axis=position)


def from_above(values, stride, direction):
    position = direction % values.ndim
    extent = values.shape[position]
    retained = cut_range(values, stride, extent, direction)
    padding = jnp.zeros_like(cut_range(values, 0, stride, direction))
    return jnp.concatenate([retained, padding], axis=position)


def eliminate(
    lower_band,
    upper_band,
    values,
    low_lower,
    low_upper,
    low_values,
    high_lower,
    high_upper,
    high_values,
):
    denominator = 1.0 - lower_band * low_upper - upper_band * high_lower
    new_lower = -lower_band * low_lower
    new_upper = -upper_band * high_upper
    new_values = values - lower_band * low_values - upper_band * high_values
    return (new_lower / denominator, new_upper / denominator, new_values / denominator)


def reduce_levels(lower_band, upper_band, values, direction):
    extent = lower_band.shape[direction % lower_band.ndim]
    stride = 1
    while stride < extent:
        lower_band, upper_band, values = eliminate(
            lower_band,
            upper_band,
            values,
            from_below(lower_band, stride, direction),
            from_below(upper_band, stride, direction),
            from_below(values, stride, direction),
            from_above(lower_band, stride, direction),
            from_above(upper_band, stride, direction),
            from_above(values, stride, direction),
        )
        stride = stride * 2
    return values


def axis_flux_parts(temp_pad, cond_pad, ratio, direction):
    extent = temp_pad.shape[direction] - 2
    face_all = 0.5 * (
        cut_range(cond_pad, 0, extent + 1, direction)
        + cut_range(cond_pad, 1, extent + 2, direction)
    )
    face_low = cut_range(face_all, 0, extent, direction)
    face_high = cut_range(face_all, 1, extent + 1, direction)
    centre = cut_range(temp_pad, 1, extent + 1, direction)
    lower_cell = cut_range(temp_pad, 0, extent, direction)
    upper_cell = cut_range(temp_pad, 2, extent + 2, direction)
    explicit = ratio * (face_high * (upper_cell - centre) - face_low * (centre - lower_cell))
    lower_band = -half_theta * ratio * face_low
    upper_band = -half_theta * ratio * face_high
    main_band = 1.0 - lower_band - upper_band
    return (explicit, lower_band, main_band, upper_band)


def edge_row(values, index, direction):
    return jnp.squeeze(cut_range(values, index, index + 1, direction), axis=direction % values.ndim)


def split_rows(lower_band, main_band, upper_band, values, direction):
    position = direction % values.ndim
    extent = values.shape[position]
    inner_lower = cut_range(lower_band, 1, extent - 1, direction)
    inner_main = cut_range(main_band, 1, extent - 1, direction)
    inner_upper = cut_range(upper_band, 1, extent - 1, direction)
    low_source = jnp.concatenate(
        [
            cut_range(lower_band, 1, 2, direction),
            jnp.zeros_like(cut_range(lower_band, 2, extent - 1, direction)),
        ],
        axis=position,
    )
    high_source = jnp.concatenate(
        [
            jnp.zeros_like(cut_range(upper_band, 1, extent - 2, direction)),
            cut_range(upper_band, extent - 2, extent - 1, direction),
        ],
        axis=position,
    )
    diagonals_together = jnp.stack(
        [cut_range(values, 1, extent - 1, direction), low_source, high_source]
    )
    solved = reduce_levels(
        inner_lower / inner_main,
        inner_upper / inner_main,
        diagonals_together / inner_main,
        direction,
    )
    inner_y, inner_g, inner_h = (solved[0], solved[1], solved[2])
    head_lower = edge_row(lower_band, 0, direction)
    head_upper = edge_row(upper_band, 0, direction)
    head_main = edge_row(main_band, 0, direction) - head_upper * edge_row(inner_g, 0, direction)
    head_off = -head_upper * edge_row(inner_h, 0, direction)
    head_values = edge_row(values, 0, direction) - head_upper * edge_row(inner_y, 0, direction)
    tail_lower = edge_row(lower_band, extent - 1, direction)
    tail_upper = edge_row(upper_band, extent - 1, direction)
    tail_main = edge_row(main_band, extent - 1, direction) - tail_lower * edge_row(
        inner_h, extent - 3, direction
    )
    tail_off = -tail_lower * edge_row(inner_g, extent - 3, direction)
    tail_values = edge_row(values, extent - 1, direction) - tail_lower * edge_row(
        inner_y, extent - 3, direction
    )
    reduced = jnp.stack(
        [
            jnp.stack([head_lower / head_main, tail_off / tail_main]),
            jnp.stack([head_off / head_main, tail_upper / tail_main]),
            jnp.stack([head_values / head_main, tail_values / tail_main]),
        ]
    )
    return (reduced, inner_y, inner_g, inner_h)


def assemble(boundary, inner_y, inner_g, inner_h, direction):
    position = direction % inner_y.ndim
    head_value = jnp.expand_dims(boundary[0], position)
    tail_value = jnp.expand_dims(boundary[1], position)
    inner = inner_y - head_value * inner_g - tail_value * inner_h
    return jnp.concatenate([head_value, inner, tail_value], axis=position)


def per_device(thermal_state, heat_spread_factor, heating_input):
    diagonals_together = jnp.stack([thermal_state, heat_spread_factor])
    widened = with_halo(diagonals_together, (("gx", 1), ("gz", 3)), 1)
    row_with_ghosts = [(0, 0), (1, 1), (0, 0)]
    width_known_flux, width_subdiagonal, width_diagonal, width_superdiagonal = axis_flux_parts(
        widened[0, :, :, 1:-1],
        widened[1, :, :, 1:-1],
        16.0 * SHARD_SPAN_WIDTH * SHARD_SPAN_WIDTH,
        0,
    )
    row_known_flux, row_subdiagonal, row_diagonal, row_superdiagonal = axis_flux_parts(
        jnp.pad(thermal_state, row_with_ghosts),
        jnp.pad(heat_spread_factor, row_with_ghosts),
        2.0,
        1,
    )
    height_known_flux, height_subdiagonal, height_diagonal, height_superdiagonal = axis_flux_parts(
        widened[0, 1:-1], widened[1, 1:-1], 0.5 * SHARD_SPAN_TALL * SHARD_SPAN_TALL, 2
    )
    right_side = width_known_flux + row_known_flux + height_known_flux + heating_input
    x_reduced, x_inner_y, x_inner_g, x_inner_h = split_rows(
        width_subdiagonal, width_diagonal, width_superdiagonal, right_side, -3
    )
    groups = lax.axis_size("gx")
    row_extent_count = thermal_state.shape[1]
    height_extent_count = thermal_state.shape[2]
    line_count = row_extent_count * height_extent_count
    packed = x_reduced.reshape(3, 2, groups, line_count // groups)
    line_block = lax.all_to_all(packed, "gx", split_axis=2, concat_axis=1, tiled=True)
    answer = reduce_levels(line_block[0], line_block[1], line_block[2], -3)
    boundary = lax.all_to_all(answer, "gx", split_axis=0, concat_axis=1, tiled=True)
    x_boundary = boundary.reshape(2, row_extent_count, height_extent_count)
    step_one = assemble(x_boundary, x_inner_y, x_inner_g, x_inner_h, -3)
    step_two = reduce_levels(
        row_subdiagonal / row_diagonal, row_superdiagonal / row_diagonal, step_one / row_diagonal, 1
    )
    z_reduced, z_inner_y, z_inner_g, z_inner_h = split_rows(
        height_subdiagonal, height_diagonal, height_superdiagonal, step_two, -1
    )
    group_count = lax.axis_size("gz")
    incoming = jnp.zeros((2,) + z_reduced.shape[2:], jnp.float32)
    for sweep_turn in range(group_count):
        carry_upper, carry_values = (incoming[0], incoming[1])
        denominator = 1.0 - z_reduced[0, 0] * carry_upper
        head_upper = z_reduced[1, 0] / denominator
        head_values = (z_reduced[2, 0] - z_reduced[0, 0] * carry_values) / denominator
        denominator = 1.0 - z_reduced[0, 1] * head_upper
        tail_upper = z_reduced[1, 1] / denominator
        tail_values = (z_reduced[2, 1] - z_reduced[0, 1] * head_values) / denominator
        if sweep_turn + 1 < group_count:
            incoming = from_behind(jnp.stack([tail_upper, tail_values]), "gz", 1)
    next_head = jnp.zeros_like(tail_values)
    for sweep_turn in range(group_count):
        tail_value = tail_values - tail_upper * next_head
        head_value = head_values - head_upper * tail_value
        if sweep_turn + 1 < group_count:
            next_head = from_behind(head_value, "gz", -1)
    z_boundary = jnp.stack([head_value, tail_value])
    closing_update = assemble(z_boundary, z_inner_y, z_inner_g, z_inner_h, -1)
    return thermal_state + closing_update


def solution(mesh):
    in_specs = (P("gx", None, "gz"), P("gx", None, "gz"), P("gx", None, "gz"))
    out_specs = P("gx", None, "gz")
    return jax.shard_map(
        per_device, mesh=mesh, in_specs=in_specs, out_specs=out_specs, check_vma=False
    )
```

profile of v0, /device:TPU:0, one launch (start us, length us, event | category | flops | bytes accessed | tf_op | source)
XLA Modules:
  0.0 129.9 jit_solution(3935269888984965669)
XLA Ops:
  0.9 1.3 collective-permute-start.1
  2.2 3.2 %collective-permute-start = (f32[2,1,64,128]{3,2,1,0:T(8,128)S(1)}, f32[2,1,64,128]{3,2,1,0:T(8,128)S(1)}, u32[]{:S(2)}, u32[]{:S(2)}) collective-permute-start(f32[2,1,64,128]{3,2,1,0:T(8,128)S(1)} %get-tuple-element.104), channel_id=1, source_target_pairs={{0,4},{4,8},{8,12},{12,16},{16,20},{20,24},{24,28},{28,32},{32,36}... | collective-permute-start | bytes 196616 | tf_op jit(solution)/shard_map/ppermute | solution.py:18
  6.3 1.1 fusion.102
  7.3 1.3 %copy.697 = f32[2,10,64,1]{2,0,3,1:T(2,128)S(1)} copy(f32[2,10,64,1]{3,2,1,0:T(8,128)} %get-tuple-element.92) | data formatting | bytes 10240 | tf_op jit(solution)/shard_map/slice | solution.py:21
  8.7 1.3 collective-permute-start.3
  10.8 5.1 %collective-permute-start.2 = (f32[2,10,64,1]{2,0,3,1:T(2,128)}, f32[2,10,64,1]{2,0,3,1:T(2,128)}, u32[]{:S(2)}, u32[]{:S(2)}) collective-permute-start(f32[2,10,64,1]{2,0,3,1:T(2,128)} %copy.696), channel_id=1, source_target_pairs={{0,1},{1,2},{2,3},{4,5},{5,6},{6,7},{8,9},{9,10},{10,11},{12,13},{... | collective-permute-start | bytes 15368 | tf_op jit(solution)/shard_map/ppermute | solution.py:18
  19.5 1.8 %copy.699 = f32[2,10,64,1]{3,2,1,0:T(8,128)} copy(f32[2,10,64,1]{2,0,3,1:T(2,128)} %collective-permute-done.3) | data formatting | bytes 10240 | tf_op jit(solution)/shard_map/ppermute | solution.py:21
  21.3 1.9 %copy.698 = f32[2,10,64,1]{3,2,1,0:T(8,128)} copy(f32[2,10,64,1]{2,0,3,1:T(2,128)} %collective-permute-done.2) | data formatting | bytes 10240 | tf_op jit(solution)/shard_map/ppermute | solution.py:18
  23.2 1.7 %fusion = (f32[8,64,130]{2,1,0:T(8,128)S(1)}, f32[8,64,130]{2,1,0:T(8,128)S(1)}) fusion(f32[2,10,64,1]{3,2,1,0:T(8,128)} %copy.699, f32[2,10,64,1]{3,2,1,0:T(8,128)} %copy.698, f32[2,1,64,128]{3,2,1,0:T(8,128)S(1)} %collective-permute-done.1, f32[2,1,64,128]{3,2,1,0:T(8,128)S(1)} %copy-done.37, f32[1,8,64,128]{3,2,1,0:T(8,128)S(1)} %bitcast.318, ...), kind=kLoop, calls=%fused_computation.16 | loop fusion | flops 665600 | bytes 1198080 | tf_op jit(solution)/shard_map/squeeze | solution.py:190
  30.6 1.0 slice_divide_fusion.7
  33.5 12.3 %all-to-all-start = ((f32[3,2,32,256]{3,1,0,2:T(2,128)}), f32[3,2,32,256]{3,1,0,2:T(2,128)}, u32[]{:S(2)}, u32[]{:S(2)}) async-start(f32[3,2,32,256]{3,1,0,2:T(2,128)} %copy.700), calls=%async_computation | async-start | bytes 393216 | tf_op jit(solution)/shard_map/all_to_all | solution.py:201
  45.8 1.0 slice_divide_fusion.2
  55.2 1.6 %fusion.134 = (f32[1,32,2,1,256]{4,2,0,1,3:T(2,128)}, f32[1,32,2,1,256]{4,2,0,1,3:T(2,128)S(1)}, f32[1,32,2,1,256]{4,2,0,1,3:T(2,128)}) fusion(f32[3,32,2,1,256]{4,2,0,1,3:T(2,128)} %bitcast.18), kind=kLoop, calls=%fused_computation.306 | loop fusion | bytes 393216 | tf_op jit(solution)/shard_map/slice | solution.py:202
  56.8 0.9 squeeze.70
  58.5 0.9 squeeze.71
  64.3 7.5 %all-to-all-start.1 = ((f32[64,1,256]{2,1,0:T(1,128)}), f32[64,1,256]{2,1,0:T(1,128)S(1)}, u32[]{:S(2)}, u32[]{:S(2)}) async-start(f32[64,1,256]{2,1,0:T(1,128)} %subtract_divide_fusion.16), calls=%async_computation.1 | async-start | bytes 131072 | tf_op jit(solution)/shard_map/all_to_all | solution.py:203
  71.8 1.9 %pad_bitcast_fusion = (f32[1,8,64,126]{3,2,1,0:T(8,128)}, f32[1,8,64,126]{3,2,1,0:T(8,128)}) fusion(f32[8,64,1]{2,1,0:T(8,128)} %slice.1061, f32[8,64,1]{2,1,0:T(8,128)} %slice.1060), kind=kLoop, calls=%fused_computation.99 | loop fusion | bytes 520192 | tf_op jit(solution)/shard_map/stack | solution.py:131
  73.7 5.6 %all-to-all-done.1 = f32[64,1,256]{2,1,0:T(1,128)S(1)} async-done(((f32[64,1,256]{2,1,0:T(1,128)}), f32[64,1,256]{2,1,0:T(1,128)S(1)}, u32[]{:S(2)}, u32[]{:S(2)}) %all-to-all-start.1) | async-done | bytes 65568 | tf_op jit(solution)/shard_map/all_to_all | solution.py:203
  79.9 1.2 fusion.41
  96.1 2.9 %collective-permute-start.4 = (f32[2,8,64]{2,1,0:T(8,128)S(1)}, f32[2,8,64]{2,1,0:T(8,128)S(1)}, u32[]{:S(2)}, u32[]{:S(2)}) collective-permute-start(f32[2,8,64]{2,1,0:T(8,128)S(1)} %pad_maximum_fusion.13), channel_id=1, source_target_pairs={{0,1},{1,2},{2,3},{4,5},{5,6},{6,7},{8,9},{9,10},{10,11},{12,13},{... | collective-permute-start | bytes 12296 | tf_op jit(solution)/shard_map/ppermute | solution.py:29
  99.0 1.3 %collective-permute-done.4 = f32[2,8,64]{2,1,0:T(8,128)S(1)} collective-permute-done((f32[2,8,64]{2,1,0:T(8,128)S(1)}, f32[2,8,64]{2,1,0:T(8,128)S(1)}, u32[]{:S(2)}, u32[]{:S(2)}) %collective-permute-start.4) | collective-permute-done | bytes 4128 | tf_op jit(solution)/shard_map/ppermute | solution.py:29
  100.4 4.2 %collective-permute-start.5 = (f32[2,8,64]{2,1,0:T(8,128)S(1)}, f32[2,8,64]{2,1,0:T(8,128)S(1)}, u32[]{:S(2)}, u32[]{:S(2)}) collective-permute-start(f32[2,8,64]{2,1,0:T(8,128)S(1)} %pad_maximum_fusion.14), channel_id=1, source_target_pairs={{0,1},{1,2},{2,3},{4,5},{5,6},{6,7},{8,9},{9,10},{10,11},{12,13},{... | collective-permute-start | bytes 12296 | tf_op jit(solution)/shard_map/ppermute | solution.py:29
  104.6 1.3 %collective-permute-done.5 = f32[2,8,64]{2,1,0:T(8,128)S(1)} collective-permute-done((f32[2,8,64]{2,1,0:T(8,128)S(1)}, f32[2,8,64]{2,1,0:T(8,128)S(1)}, u32[]{:S(2)}, u32[]{:S(2)}) %collective-permute-start.5) | collective-permute-done | bytes 4128 | tf_op jit(solution)/shard_map/ppermute | solution.py:29
  106.0 4.2 %collective-permute-start.6 = (f32[2,8,64]{2,1,0:T(8,128)S(1)}, f32[2,8,64]{2,1,0:T(8,128)S(1)}, u32[]{:S(2)}, u32[]{:S(2)}) collective-permute-start(f32[2,8,64]{2,1,0:T(8,128)S(1)} %pad_maximum_fusion.15), channel_id=1, source_target_pairs={{0,1},{1,2},{2,3},{4,5},{5,6},{6,7},{8,9},{9,10},{10,11},{12,13},{... | collective-permute-start | bytes 12296 | tf_op jit(solution)/shard_map/ppermute | solution.py:29
  110.2 1.3 %collective-permute-done.6 = f32[2,8,64]{2,1,0:T(8,128)S(1)} collective-permute-done((f32[2,8,64]{2,1,0:T(8,128)S(1)}, f32[2,8,64]{2,1,0:T(8,128)S(1)}, u32[]{:S(2)}, u32[]{:S(2)}) %collective-permute-start.6) | collective-permute-done | bytes 4128 | tf_op jit(solution)/shard_map/ppermute | solution.py:29
  111.6 1.3 collective-permute-start.7
  112.9 4.5 %collective-permute-done.7 = f32[8,64]{1,0:T(8,128)S(1)} collective-permute-done((f32[8,64]{1,0:T(8,128)S(1)}, f32[8,64]{1,0:T(8,128)S(1)}, u32[]{:S(2)}, u32[]{:S(2)}) %collective-permute-start.7) | collective-permute-done | bytes 2080 | tf_op jit(solution)/shard_map/ppermute | solution.py:29
  117.3 1.3 collective-permute-start.8
  118.6 4.3 %collective-permute-done.8 = f32[8,64]{1,0:T(8,128)S(1)} collective-permute-done((f32[8,64]{1,0:T(8,128)S(1)}, f32[8,64]{1,0:T(8,128)S(1)}, u32[]{:S(2)}, u32[]{:S(2)}) %collective-permute-start.8) | collective-permute-done | bytes 2080 | tf_op jit(solution)/shard_map/ppermute | solution.py:29
  123.0 1.3 collective-permute-start.9
  124.3 4.2 %collective-permute-done.9 = f32[8,64]{1,0:T(8,128)S(1)} collective-permute-done((f32[8,64]{1,0:T(8,128)S(1)}, f32[8,64]{1,0:T(8,128)S(1)}, u32[]{:S(2)}, u32[]{:S(2)}) %collective-permute-start.9) | collective-permute-done | bytes 2080 | tf_op jit(solution)/shard_map/ppermute | solution.py:29
  129.0 0.9 maximum_add_fusion
  (263 shorter events, 42.8 us)
Async XLA Ops:
  0.0 5.4 %copy-start.1 = (f32[8,64,128]{2,1,0:T(8,128)S(1)}, f32[8,64,128]{2,1,0:T(8,128)}, u32[]{:S(2)}) copy-start(f32[8,64,128]{2,1,0:T(8,128)} %param.4) | copy-start | bytes 786436
  0.9 4.6 %collective-permute-start.1 = (f32[2,1,64,128]{3,2,1,0:T(8,128)S(1)}, f32[2,1,64,128]{3,2,1,0:T(8,128)S(1)}, u32[]{:S(2)}, u32[]{:S(2)}) collective-permute-start(f32[2,1,64,128]{3,2,1,0:T(8,128)S(1)} %get-tuple-element.105), channel_id=1, source_target_pairs={{4,0},{8,4},{12,8},{16,12},{20,16},{24,20},{28,24},{32,28},{36,32}... | collective-permute-start | bytes 196616 | tf_op jit(solution)/shard_map/ppermute | solution.py:21
  2.2 4.1 %copy-start = (f32[8,64,128]{2,1,0:T(8,128)S(1)}, f32[8,64,128]{2,1,0:T(8,128)}, u32[]{:S(2)}) copy-start(f32[8,64,128]{2,1,0:T(8,128)} %param.3) | copy-start | bytes 786436
  2.2 4.1 %collective-permute-start = (f32[2,1,64,128]{3,2,1,0:T(8,128)S(1)}, f32[2,1,64,128]{3,2,1,0:T(8,128)S(1)}, u32[]{:S(2)}, u32[]{:S(2)}) collective-permute-start(f32[2,1,64,128]{3,2,1,0:T(8,128)S(1)} %get-tuple-element.104), channel_id=1, source_target_pairs={{0,4},{4,8},{8,12},{12,16},{16,20},{20,24},{24,28},{28,32},{32,36}... | collective-permute-start | bytes 196616 | tf_op jit(solution)/shard_map/ppermute | solution.py:18
  5.4 21.6 %copy-start.6 = (f32[8,65,128]{2,1,0:T(8,128)}, f32[8,65,128]{2,1,0:T(8,128)S(1)}, u32[]{:S(2)}) copy-start(f32[8,65,128]{2,1,0:T(8,128)S(1)} %add_multiply_fusion) | copy-start | bytes 798724
  6.2 9.7 %copy-start.36 = (f32[2,1,64,128]{3,2,1,0:T(8,128)}, f32[2,1,64,128]{3,2,1,0:T(8,128)S(1)}, u32[]{:S(2)}) copy-start(f32[2,1,64,128]{3,2,1,0:T(8,128)S(1)} %collective-permute-done) | copy-start | bytes 196612
  8.7 10.8 %collective-permute-start.3 = (f32[2,10,64,1]{2,0,3,1:T(2,128)S(1)}, f32[2,10,64,1]{2,0,3,1:T(2,128)}, u32[]{:S(2)}, u32[]{:S(2)}) collective-permute-start(f32[2,10,64,1]{2,0,3,1:T(2,128)S(1)} %copy.697), channel_id=1, source_target_pairs={{1,0},{2,1},{3,2},{5,4},{6,5},{7,6},{9,8},{10,9},{11,10},{13,12},{... | collective-permute-start | bytes 15368 | tf_op jit(solution)/shard_map/ppermute | solution.py:21
  10.8 10.5 %collective-permute-start.2 = (f32[2,10,64,1]{2,0,3,1:T(2,128)}, f32[2,10,64,1]{2,0,3,1:T(2,128)}, u32[]{:S(2)}, u32[]{:S(2)}) collective-permute-start(f32[2,10,64,1]{2,0,3,1:T(2,128)} %copy.696), channel_id=1, source_target_pairs={{0,1},{1,2},{2,3},{4,5},{5,6},{6,7},{8,9},{9,10},{10,11},{12,13},{... | collective-permute-start | bytes 15368 | tf_op jit(solution)/shard_map/ppermute | solution.py:18
  16.3 2.6 %copy-start.32 = (f32[8,64,128]{2,1,0:T(8,128)}, f32[8,64,128]{2,1,0:T(8,128)S(1)}, u32[]{:S(2)}) copy-start(f32[8,64,128]{2,1,0:T(8,128)S(1)} %get-tuple-element.111) | copy-start | bytes 786436
  21.3 1.9 %copy-start.37 = (f32[2,1,64,128]{3,2,1,0:T(8,128)S(1)}, f32[2,1,64,128]{3,2,1,0:T(8,128)}, u32[]{:S(2)}) copy-start(f32[2,1,64,128]{3,2,1,0:T(8,128)} %copy-done.36) | copy-start | bytes 196612
  25.3 20.6 %copy-start.8 = (f32[8,64,128]{2,1,0:T(8,128)}, f32[8,64,128]{2,1,0:T(8,128)S(1)}, u32[]{:S(2)}) copy-start(f32[8,64,128]{2,1,0:T(8,128)S(1)} %get-tuple-element.99) | copy-start | bytes 786436
  26.1 1.0 copy-start.42
  27.9 1.0 copy-start.31
  30.6 1.9 %copy-start.14 = (f32[3,6,64,128]{3,2,1,0:T(8,128)}, f32[3,6,64,128]{3,2,1,0:T(8,128)S(1)}, u32[]{:S(2)}) copy-start(f32[3,6,64,128]{3,2,1,0:T(8,128)S(1)} %subtract_divide_fusion.7) | copy-start | bytes 1769476
  33.5 21.7 %all-to-all-start = ((f32[3,2,32,256]{3,1,0,2:T(2,128)}), f32[3,2,32,256]{3,1,0,2:T(2,128)}, u32[]{:S(2)}, u32[]{:S(2)}) async-start(f32[3,2,32,256]{3,1,0,2:T(2,128)} %copy.700), calls=%async_computation | async-start | bytes 393216 | tf_op jit(solution)/shard_map/all_to_all | solution.py:201
  64.3 15.0 %all-to-all-start.1 = ((f32[64,1,256]{2,1,0:T(1,128)}), f32[64,1,256]{2,1,0:T(1,128)S(1)}, u32[]{:S(2)}, u32[]{:S(2)}) async-start(f32[64,1,256]{2,1,0:T(1,128)} %subtract_divide_fusion.16), calls=%async_computation.1 | async-start | bytes 131072 | tf_op jit(solution)/shard_map/all_to_all | solution.py:203
  79.9 1.3 copy-start.7
  83.3 1.0 copy-start.19
  83.4 1.0 copy-start.15
  83.4 1.0 copy-start.18
  84.6 1.0 copy-start.17
  85.9 1.0 copy-start.21
  89.8 1.0 copy-start.27
  91.2 1.0 copy-start.29
  92.5 1.0 copy-start.13
  92.5 1.1 copy-start.35
  96.1 4.3 %collective-permute-start.4 = (f32[2,8,64]{2,1,0:T(8,128)S(1)}, f32[2,8,64]{2,1,0:T(8,128)S(1)}, u32[]{:S(2)}, u32[]{:S(2)}) collective-permute-start(f32[2,8,64]{2,1,0:T(8,128)S(1)} %pad_maximum_fusion.13), channel_id=1, source_target_pairs={{0,1},{1,2},{2,3},{4,5},{5,6},{6,7},{8,9},{9,10},{10,11},{12,13},{... | collective-permute-start | bytes 12296 | tf_op jit(solution)/shard_map/ppermute | solution.py:29
  100.4 5.5 %collective-permute-start.5 = (f32[2,8,64]{2,1,0:T(8,128)S(1)}, f32[2,8,64]{2,1,0:T(8,128)S(1)}, u32[]{:S(2)}, u32[]{:S(2)}) collective-permute-start(f32[2,8,64]{2,1,0:T(8,128)S(1)} %pad_maximum_fusion.14), channel_id=1, source_target_pairs={{0,1},{1,2},{2,3},{4,5},{5,6},{6,7},{8,9},{9,10},{10,11},{12,13},{... | collective-permute-start | bytes 12296 | tf_op jit(solution)/shard_map/ppermute | solution.py:29
  106.0 5.5 %collective-permute-start.6 = (f32[2,8,64]{2,1,0:T(8,128)S(1)}, f32[2,8,64]{2,1,0:T(8,128)S(1)}, u32[]{:S(2)}, u32[]{:S(2)}) collective-permute-start(f32[2,8,64]{2,1,0:T(8,128)S(1)} %pad_maximum_fusion.15), channel_id=1, source_target_pairs={{0,1},{1,2},{2,3},{4,5},{5,6},{6,7},{8,9},{9,10},{10,11},{12,13},{... | collective-permute-start | bytes 12296 | tf_op jit(solution)/shard_map/ppermute | solution.py:29
  111.6 5.8 %collective-permute-start.7 = (f32[8,64]{1,0:T(8,128)S(1)}, f32[8,64]{1,0:T(8,128)S(1)}, u32[]{:S(2)}, u32[]{:S(2)}) collective-permute-start(f32[8,64]{1,0:T(8,128)S(1)} %get-tuple-element.13), channel_id=1, source_target_pairs={{1,0},{2,1},{3,2},{5,4},{6,5},{7,6},{9,8},{10,9},{11,10},{13,12},{... | collective-permute-start | bytes 6152 | tf_op jit(solution)/shard_map/ppermute | solution.py:29
  117.3 5.6 %collective-permute-start.8 = (f32[8,64]{1,0:T(8,128)S(1)}, f32[8,64]{1,0:T(8,128)S(1)}, u32[]{:S(2)}, u32[]{:S(2)}) collective-permute-start(f32[8,64]{1,0:T(8,128)S(1)} %multiply_subtract_fusion.24), channel_id=1, source_target_pairs={{1,0},{2,1},{3,2},{5,4},{6,5},{7,6},{9,8},{10,9},{11,10},{13,12},{... | collective-permute-start | bytes 6152 | tf_op jit(solution)/shard_map/ppermute | solution.py:29
  123.0 5.5 %collective-permute-start.9 = (f32[8,64]{1,0:T(8,128)S(1)}, f32[8,64]{1,0:T(8,128)S(1)}, u32[]{:S(2)}, u32[]{:S(2)}) collective-permute-start(f32[8,64]{1,0:T(8,128)S(1)} %multiply_subtract_fusion.23), channel_id=1, source_target_pairs={{1,0},{2,1},{3,2},{5,4},{6,5},{7,6},{9,8},{10,9},{11,10},{13,12},{... | collective-permute-start | bytes 6152 | tf_op jit(solution)/shard_map/ppermute | solution.py:29
  (26 other events, 21.8 us)
where the time goes:
time: 132 us; the launch traced here: 130 us
  starting transfers between devices  45.8 us (35%)
  local copies, waits for them, and re-layouts  37.5 us (28%)
  waiting for transfers between devices  23.4 us (18%)
  other arithmetic  21.7 us (16%)
  between operations  1.4 us (1%)
    ppermute x6, waiting for transfers between devices, from_behind(): return lax.ppermute(block, axis, route)  17.1 us
    ppermute x6, starting transfers between devices, from_behind(): return lax.ppermute(block, axis, route)  15.1 us
    unnamed x92, local copies, waits for them, and re-layouts  14.1 us
    all_to_all x1, starting transfers between devices, per_device(): lax.all_to_all(packed, 'gx', split_axis=2, concat_axis=1, tiled=True)  12.3 us
    ppermute x2, starting transfers between devices, with_halo(): lax.ppermute(lax.slice_in_dim(block, block.shape[dim] - width, None, axis...  8.3 us
    slice x67, local copies, waits for them, and re-layouts, cut_range(): return lax.slice_in_dim(values, start, stop, axis=direction % values.ndim)  8.29 us
    all_to_all x1, starting transfers between devices, per_device(): lax.all_to_all(answer, 'gx', split_axis=0, concat_axis=1, tiled=True)  7.5 us
    div x22, other arithmetic, eliminate(): new_values / denominator  6.27 us
  transfers between devices with their start and end apart: 12, of which 8 were waited for; matrix products, arithmetic and copies ran while one was open for 10% of the time, Pallas kernels for 0%

commit v1 on v0

v1 whole, which is shorter than its diff:
```python
import functools

import jax
import jax.numpy as jnp
from jax import lax
from jax.experimental import pallas as pl
from jax.experimental.pallas import tpu as pltpu
from jax.sharding import PartitionSpec as P

NX, NY, NZ = 8, 64, 128
ROWS = NX * NY
HALF = NY // 2
CX = 0.25 * 16.0 * NX * NX
CY = 0.25 * 2.0
CZ = 0.25 * 0.5 * NZ * NZ
F32 = jnp.float32
VMEM_LIMIT = 24 * 1024 * 1024
HIGHEST = lax.Precision.HIGHEST


def call(kernel, outs, *args, scratch=(), flops=0, name=None):
    shapes = [jax.ShapeDtypeStruct(s, F32) for s in outs]
    nbytes = sum(4 * a.size for a in args) + sum(4 * s.size for s in shapes)
    return pl.pallas_call(
        kernel,
        out_shape=shapes,
        in_specs=[pl.BlockSpec(memory_space=pltpu.VMEM) for _ in args],
        out_specs=[pl.BlockSpec(memory_space=pltpu.VMEM) for _ in outs],
        scratch_shapes=[pltpu.VMEM(s, F32) for s in scratch],
        compiler_params=pltpu.CompilerParams(vmem_limit_bytes=VMEM_LIMIT),
        cost_estimate=pl.CostEstimate(flops=flops, bytes_accessed=nbytes, transcendentals=0),
        name=name,
    )(*args)


def lanes_to_rows(select, block):
    return lax.dot_general(
        select, block, (((1,), (1,)), ((), ())), precision=HIGHEST, preferred_element_type=F32
    )


def rows_to_lanes(rows, select):
    return lax.dot_general(
        rows, select, (((0,), (0,)), ((), ())), precision=HIGHEST, preferred_element_type=F32
    )


def selector(entries):
    row = lax.broadcasted_iota(jnp.int32, (8, NZ), 0)
    lane = lax.broadcasted_iota(jnp.int32, (8, NZ), 1)
    hit = None
    for r, l in entries:
        one = (row == r) if l is None else ((row == r) & (lane == l))
        hit = one if hit is None else (hit | one)
    return jnp.where(hit, 1.0, 0.0).astype(F32)


def reduce_chain(e, c, r):
    n = len(e)
    e_h, r_h = e[0], r[0]
    s, w, rr = e[1], c[0], r[1]
    parts = []
    for j in range(1, n - 1):
        inv = 1.0 / (s + w + c[j])
        a, m = w * inv, c[j] * inv
        parts.append((a, m, rr * inv))
        e_h = e_h + a * s
        r_h = r_h + a * rr
        s = e[j + 1] + m * s
        rr = r[j + 1] + m * rr
        w = m * w
    return (e_h, s, w, r_h, rr), parts


def expand_chain(first, last, parts):
    values = [last]
    for a, m, q in reversed(parts):
        values.append(q + a * first + m * values[-1])
    values.append(first)
    return values[::-1]


def solve_chain(e, c, r):
    n = len(e)
    s, rr = e[0], r[0]
    parts = []
    for j in range(n - 1):
        inv = 1.0 / (s + c[j])
        m = c[j] * inv
        parts.append((m, rr * inv))
        s = e[j + 1] + m * s
        rr = r[j + 1] + m * rr
    values = [rr / s]
    for m, q in reversed(parts):
        values.append(q + m * values[-1])
    return values[::-1]


def chain_of(blocks, scale):
    e, c, r = [], [], []
    for i, b in enumerate(blocks):
        e += [b[0], b[1]]
        r += [b[3], b[4]]
        c.append(b[2])
        if i + 1 < len(blocks):
            c.append(scale * (b[6] + blocks[i + 1][5]))
    return e, c, r


def edges_kernel(u_ref, k_ref, out_ref):
    u = u_ref[...].reshape(ROWS, NZ)
    k = k_ref[...].reshape(ROWS, NZ)
    out_ref[...] = lanes_to_rows(selector([(0, 0), (1, NZ - 1)]), u) + lanes_to_rows(
        selector([(2, 0), (3, NZ - 1)]), k
    )


def local_kernel(u_ref, k_ref, f_ref, rp_ref, a_ref, m_ref, inv_ref, ew_ref):
    row = lax.broadcasted_iota(jnp.int32, (NY, NZ), 0)
    lane = lax.broadcasted_iota(jnp.int32, (NY, NZ), 1)
    for x in range(NX):
        u, k = u_ref[x], k_ref[x]
        flux_y = (CY * (k + pltpu.roll(k, NY - 1, 0))) * (pltpu.roll(u, NY - 1, 0) - u)
        flux_y = jnp.where(row == NY - 1, -(CY * k) * u, flux_y)
        low_y = jnp.where(row == 0, (CY * k) * u, pltpu.roll(flux_y, 1, 0))
        flux_z = (CZ * (k + pltpu.roll(k, NZ - 1, 1))) * (pltpu.roll(u, NZ - 1, 1) - u)
        flux_z = jnp.where(lane == NZ - 1, 0.0, flux_z)
        low_z = pltpu.roll(flux_z, 1, 1)
        rp_ref[x] = u + (flux_y - low_y) + (flux_z - low_z) + 0.5 * f_ref[x]
    s = jnp.ones((NY, NZ), F32)
    e_h = s
    w = CX * (k_ref[0] + k_ref[1])
    for j in range(1, NX - 1):
        c = CX * (k_ref[j] + k_ref[j + 1])
        inv = 1.0 / (s + w + c)
        a, m = w * inv, c * inv
        inv_ref[j - 1], a_ref[j - 1], m_ref[j - 1] = inv, a, m
        e_h = e_h + a * s
        s = 1.0 + m * s
        w = m * w
    ew_ref[0], ew_ref[1], ew_ref[2] = e_h, s, w


def halo_kernel(own_ref, one_ref, two_ref, rp_ref, a_ref, m_ref, ew_ref, k_ref, keep_ref, send_ref, rr_ref, fix_ref):
    g = lax.axis_index("gz")
    core = lax.rem(lax.axis_index("gx"), 2)
    odd = lax.rem(g, 2) == 1
    own, one, two = own_ref[...], one_ref[...], two_ref[...]
    low = jnp.where(odd, one, two) * jnp.where(g > 0, 1.0, 0.0)
    high = jnp.where(odd, two, one) * jnp.where(g < 3, 1.0, 0.0)
    at_low = CZ * (low[3:4] + own[2:3]) * (low[1:2] - own[0:1])
    at_high = CZ * (high[2:3] + own[3:4]) * (high[0:1] - own[1:2])
    row = lax.broadcasted_iota(jnp.int32, (8, ROWS), 0)
    both = jnp.where(row == 0, at_low, jnp.where(row == 1, at_high, 0.0))
    fix_ref[...] = rows_to_lanes(both, selector([(0, 0), (1, NZ - 1)])).reshape(NX, NY, NZ)
    for which, out in ((core, keep_ref), (1 - core, send_ref)):
        ys = pl.ds(pl.multiple_of(which * HALF, HALF), HALF)
        r_h = rp_ref[0, ys] + fix_ref[0, ys]
        rr = rp_ref[1, ys] + fix_ref[1, ys]
        for j in range(1, NX - 1):
            rr_ref[j - 1, ys] = rr
            r_h = r_h + a_ref[j - 1, ys] * rr
            rr = (rp_ref[j + 1, ys] + fix_ref[j + 1, ys]) + m_ref[j - 1, ys] * rr
        for i in range(3):
            out[i] = ew_ref[i, ys]
        out[3], out[4] = r_h, rr
        out[5], out[6] = k_ref[0, ys], k_ref[NX - 1, ys]


def core_kernel(own_ref, got_ref, out_ref, parts_ref):
    first = lax.rem(lax.axis_index("gx"), 2) == 0
    low = [jnp.where(first, own_ref[i], got_ref[i]) for i in range(7)]
    high = [jnp.where(first, got_ref[i], own_ref[i]) for i in range(7)]
    port, parts = reduce_chain(*chain_of([low, high], CX))
    for i, v in enumerate(port):
        out_ref[i] = v
    out_ref[5], out_ref[6] = low[5], high[6]
    for j, p in enumerate(parts):
        for i in range(3):
            parts_ref[3 * j + i] = p[i]


def ordered(me, refs, held):
    for i, ref in enumerate(refs):
        held[jnp.bitwise_xor(me, i)] = ref[...]
    return held


def chips_kernel(own_ref, one_ref, two_ref, three_ref, out_ref, parts_ref, held):
    me = lax.rem(lax.axis_index("gx") // 2, 4)
    ordered(me, (own_ref, one_ref, two_ref, three_ref), held)
    blocks = [[held[b, i] for i in range(7)] for b in range(4)]
    port, parts = reduce_chain(*chain_of(blocks, CX))
    for i, v in enumerate(port):
        out_ref[i] = v
    out_ref[5], out_ref[6] = blocks[0][5], blocks[3][6]
    for j, p in enumerate(parts):
        for i in range(3):
            parts_ref[3 * j + i] = p[i]


def back_kernel(own_ref, one_ref, two_ref, three_ref, chips_ref, cores_ref, keep_ref, send_ref, held, nodes):
    index = lax.axis_index("gx")
    core, x, z = lax.rem(index, 2), lax.rem(index // 2, 4), index // 8
    ordered(z, (own_ref, one_ref, two_ref, three_ref), held)
    blocks = [[held[b, i] for i in range(7)] for b in range(4)]
    e, c, r = chain_of(blocks, CX)
    e[0] = e[0] + CX * blocks[0][5]
    e[-1] = e[-1] + CX * blocks[3][6]
    for i, v in enumerate(solve_chain(e, c, r)):
        nodes[i] = v
    first, last = nodes[2 * z], nodes[2 * z + 1]
    parts = [tuple(chips_ref[3 * j + i] for i in range(3)) for j in range(6)]
    for i, v in enumerate(expand_chain(first, last, parts)):
        nodes[i] = v
    first, last = nodes[2 * x], nodes[2 * x + 1]
    parts = [tuple(cores_ref[3 * j + i] for i in range(3)) for j in range(2)]
    v = expand_chain(first, last, parts)
    even = core == 0
    keep_ref[0], keep_ref[1] = jnp.where(even, v[0], v[2]), jnp.where(even, v[1], v[3])
    send_ref[0], send_ref[1] = jnp.where(even, v[2], v[0]), jnp.where(even, v[3], v[1])


def prepare_kernel(u_ref, k_ref, a_ref, m_ref, inv_ref, rr_ref, base_ref, g_ref, h_ref, my_ref, iy_ref):
    base_ref[0] = -u_ref[0]
    base_ref[NX - 1] = -u_ref[NX - 1]
    y = jnp.zeros((NY, NZ), F32)
    g = y
    h = jnp.ones((NY, NZ), F32)
    for j in range(NX - 2, 0, -1):
        m = m_ref[j - 1]
        y = rr_ref[j - 1] * inv_ref[j - 1] + m * y
        g = a_ref[j - 1] + m * g
        h = m * h
        base_ref[j], g_ref[j - 1], h_ref[j - 1] = y - u_ref[j], g, h
    k2 = k_ref.reshape(ROWS, NZ)
    at = lambda y: k2[pl.ds(y, NX, stride=NY), :]
    mid = HALF
    ends = []
    for start, step in ((0, 1), (NY - 1, -1)):
        k = at(start)
        ends.append([1.0 + CY * k, k, start, step])
    while any(e[2] != mid for e in ends):
        for e in ends:
            s, k, y, step = e
            if y == mid:
                continue
            k_next = at(y + step)
            c = CY * (k + k_next)
            inv = 1.0 / (s + c)
            m = c * inv
            my_ref[y], iy_ref[y] = m, inv
            e[0] = (0.0 if y + step == mid else 1.0) + m * s
            e[1], e[2] = k_next, y + step
    iy_ref[mid] = 1.0 / (1.0 + ends[0][0] + ends[1][0])
    my_ref[mid] = jnp.zeros((NX, NZ), F32)


def z_levels(k, r):
    lane = lax.broadcasted_iota(jnp.int32, k.shape, 1)
    up = CZ * (k + pltpu.roll(k, NZ - 1, 1))
    low = pltpu.roll(up, 1, 1)
    top = up
    e = jnp.ones(k.shape, F32)
    s = 1
    while s < NZ:
        inv = 1.0 / (e + low + up)
        has_low, has_up = lane >= s + 1, lane <= NZ - 2 - s
        share = e * inv
        low_in, up_in = jnp.where(has_low, low, 0.0), jnp.where(has_up, up, 0.0)
        e = e + low_in * pltpu.roll(share, s, 1) + up_in * pltpu.roll(share, NZ - s, 1)
        if r is not None:
            q = r * inv
            r = r + low_in * pltpu.roll(q, s, 1) + up_in * pltpu.roll(q, NZ - s, 1)
        new_low = jnp.where(has_low, low * pltpu.roll(low * inv, s, 1), low)
        up = jnp.where(has_up, up * pltpu.roll(up * inv, NZ - s, 1), up)
        low = new_low
        s *= 2
    inv = 1.0 / (e + low + up)
    first, last = lane == 0, lane == NZ - 1
    if r is not None:
        return jnp.where(first | last, 0.0, r * inv)
    g = jnp.where(first, 1.0, jnp.where(last, 0.0, low * inv))
    h = jnp.where(first, 0.0, jnp.where(last, 1.0, up * inv))
    return g, h, jnp.where(lane == NZ - 2, top * g, 0.0)


STEP = 32


def z_ports_kernel(k_ref, after_ref, g_ref, h_ref, port_ref, t_ref):
    del after_ref
    k2 = k_ref.reshape(ROWS, NZ)
    g2, h2 = g_ref.reshape(ROWS, NZ), h_ref.reshape(ROWS, NZ)

    def body(i, carry):
        y = i * STEP
        k = jnp.concatenate([k2[pl.ds(y + n, NX, stride=NY), :] for n in range(STEP)], axis=0)
        g, h, w = z_levels(k, None)
        at = pl.ds(pl.multiple_of(y * NX, NX * STEP), NX * STEP)
        g2[at, :], h2[at, :] = g, h
        t_ref[0, at, :], t_ref[1, at, :] = k, w
        return carry

    lax.fori_loop(0, NY // STEP, body, 0)
    port_ref[...] = (
        lanes_to_rows(selector([(0, None)]), g2[...])
        + lanes_to_rows(selector([(1, None)]), h2[...])
        + lanes_to_rows(selector([(2, None)]), t_ref[1])
        + lanes_to_rows(selector([(5, 0), (6, NZ - 1)]), t_ref[0])
    )


def y_kernel(keep_ref, got_ref, base_ref, gx_ref, hx_ref, my_ref, iy_ref, g_ref, h_ref, port_ref, v_ref, out_ref, b_ref, s_ref, d_ref):
    core = lax.rem(lax.axis_index("gx"), 2)
    for i in range(2):
        b_ref[i, pl.ds(pl.multiple_of(core * HALF, HALF), HALF)] = keep_ref[i]
        b_ref[i, pl.ds(pl.multiple_of((1 - core) * HALF, HALF), HALF)] = got_ref[i]
    first, last = b_ref[0], b_ref[1]
    s_ref[0:NY, :] = base_ref[0] + first
    for j in range(1, NX - 1):
        s_ref[j * NY : (j + 1) * NY, :] = base_ref[j] + gx_ref[j - 1] * first + hx_ref[j - 1] * last
    s_ref[(NX - 1) * NY : NX * NY, :] = base_ref[NX - 1] + last
    at = lambda y: s_ref[pl.ds(y, NX, stride=NY), :]
    mid = HALF
    low, high = at(0), at(NY - 1)
    for n in range(mid):
        y = n
        v_ref[y] = low * iy_ref[y]
        low = (at(y + 1) if y + 1 < mid else 0.0) + my_ref[y] * low
        y = NY - 1 - n
        if y > mid:
            v_ref[y] = high * iy_ref[y]
            high = (at(y - 1) if y - 1 > mid else 0.0) + my_ref[y] * high
    v = (at(mid) + low + high) * iy_ref[mid]
    low = high = v

    def emit(y, v):
        v_ref[y] = v
        d_ref[0, y * NX : (y + 1) * NX, :] = g_ref[y] * v
        d_ref[1, y * NX : (y + 1) * NX, :] = h_ref[y] * v

    emit(mid, v)
    for n in range(1, mid + 1):
        y = mid - n
        low = v_ref[y] + my_ref[y] * low
        emit(y, low)
        y = mid + n
        if y < NY:
            high = v_ref[y] + my_ref[y] * high
            emit(y, high)
    out_ref[...] = (
        port_ref[...]
        + lanes_to_rows(selector([(3, None)]), d_ref[0])
        + lanes_to_rows(selector([(4, None)]), d_ref[1])
    )


def z_local_kernel(k_ref, v_ref, y_ref):
    k2 = k_ref.reshape(ROWS, NZ)
    v2, y2 = v_ref.reshape(ROWS, NZ), y_ref.reshape(ROWS, NZ)

    def body(i, carry):
        y = i * STEP
        k = jnp.concatenate([k2[pl.ds(y + n, NX, stride=NY), :] for n in range(STEP)], axis=0)
        at = pl.ds(pl.multiple_of(y * NX, NX * STEP), NX * STEP)
        y2[at, :] = z_levels(k, v2[at, :])
        return carry

    lax.fori_loop(0, NY // STEP, body, 0)


def final_kernel(own_ref, one_ref, two_ref, three_ref, y_ref, g_ref, h_ref, u_ref, out_ref, held, nodes, b_ref):
    me = lax.axis_index("gz")
    ordered(me, (own_ref, one_ref, two_ref, three_ref), held)
    blocks = [[held[b, i : i + 1, :] for i in range(7)] for b in range(4)]
    e, c, r = chain_of(blocks, CZ)
    e[0] = e[0] + CZ * blocks[0][5]
    e[-1] = e[-1] + CZ * blocks[3][6]
    values = solve_chain(e, c, r)
    first, last = values[0], values[1]
    for b in range(1, 4):
        first = jnp.where(me == b, values[2 * b], first)
        last = jnp.where(me == b, values[2 * b + 1], last)
    row = lax.broadcasted_iota(jnp.int32, (8, ROWS), 0)
    both = jnp.where(row == 0, first, jnp.where(row == 1, last, 0.0))
    b_ref[0] = rows_to_lanes(both, selector([(0, None)]))
    b_ref[1] = rows_to_lanes(both, selector([(1, None)]))
    u2, out2 = u_ref.reshape(ROWS, NZ), out_ref.reshape(ROWS, NZ)
    for y in range(NY):
        at = pl.ds(y, NX, stride=NY)
        ys = slice(y * NX, (y + 1) * NX)
        out2[at, :] = u2[at, :] + 2.0 * (
            y_ref[y] + g_ref[y] * b_ref[0, ys, :] + h_ref[y] * b_ref[1, ys, :]
        )


def swap(block, axis, mask):
    n = lax.axis_size(axis)
    return lax.ppermute(block, axis, [(i, i ^ mask) for i in range(n)])


def per_device(u, k, f):
    edges, = call(edges_kernel, [(8, ROWS)], u, k, name="edges")
    one, two = swap(edges, "gz", 1), swap(edges, "gz", 3)
    rp, a, m, inv, ew = call(
        local_kernel,
        [(NX, NY, NZ), (NX - 2, NY, NZ), (NX - 2, NY, NZ), (NX - 2, NY, NZ), (3, NY, NZ)],
        u, k, f, name="local",
    )
    keep, send, rr = call(
        halo_kernel,
        [(7, HALF, NZ), (7, HALF, NZ), (NX - 2, NY, NZ)],
        edges, one, two, rp, a, m, ew, k, scratch=[(NX, NY, NZ)], name="halo",
    )
    got = swap(send, "gx", 1)
    chip, core_parts = call(core_kernel, [(7, HALF, NZ), (6, HALF, NZ)], keep, got, name="core")
    x_got = [swap(chip, "gx", 2 * i) for i in (1, 2, 3)]
    base, gx, hx, my, iy = call(
        prepare_kernel,
        [(NX, NY, NZ), (NX - 2, NY, NZ), (NX - 2, NY, NZ), (NY, NX, NZ), (NY, NX, NZ)],
        u, k, a, m, inv, rr, name="prepare",
    )
    group, chip_parts = call(
        chips_kernel, [(7, HALF, NZ), (18, HALF, NZ)], chip, *x_got, scratch=[(4, 7, HALF, NZ)], name="chips"
    )
    z_got = [swap(group, "gx", 8 * i) for i in (1, 2, 3)]
    gz, hz, port = call(
        z_ports_kernel,
        [(NY, NX, NZ), (NY, NX, NZ), (8, ROWS)],
        k, group, scratch=[(2, ROWS, NZ)], name="z_ports",
    )
    keep, send = call(
        back_kernel,
        [(2, HALF, NZ), (2, HALF, NZ)],
        group, *z_got, chip_parts, core_parts,
        scratch=[(4, 7, HALF, NZ), (8, HALF, NZ)], name="back",
    )
    got = swap(send, "gx", 1)
    v, message = call(
        y_kernel,
        [(NY, NX, NZ), (8, ROWS)],
        keep, got, base, gx, hx, my, iy, gz, hz, port,
        scratch=[(2, NY, NZ), (ROWS, NZ), (2, ROWS, NZ)], name="y_solve",
    )
    l_got = [swap(message, "gz", i) for i in (1, 2, 3)]
    yz, = call(z_local_kernel, [(NY, NX, NZ)], k, v, name="z_local")
    out, = call(
        final_kernel,
        [(NX, NY, NZ)],
        message, *l_got, yz, gz, hz, u,
        scratch=[(4, 8, ROWS), (8, ROWS), (2, ROWS, NZ)], name="final",
    )
    return out


def solution(mesh):
    spec = P("gx", None, "gz")
    return jax.shard_map(
        per_device, mesh=mesh, in_specs=(spec, spec, spec), out_specs=spec, check_vma=False
    )
```

time: 132 us -> 52.5 us (0.40); the launches traced: 130 us -> 52.3 us
  local copies, waits for them, and re-layouts: 37.5 us -> 2.58 us
  starting transfers between devices: 45.8 us -> 19.1 us
  other arithmetic: 21.7 us -> 0 us
  Pallas kernels: 0 us -> 12.6 us
  waiting for transfers between devices: 23.4 us -> 17.9 us
    all_to_all x2 -> x0, starting transfers between devices: 19.8 us -> none  [the longest x1 12.3 us: per_device(): lax.all_to_all(packed, 'gx', split_axis=2, concat_axis=1, tiled=True)]
    div x56 -> x0, other arithmetic: 13.9 us -> none  [the longest x22 6.27 us: eliminate(): new_values / denominator]
    slice x74 -> x0, local copies, waits for them, and re-layouts: 13.1 us -> none  [the longest x67 8.29 us: cut_range(): return lax.slice_in_dim(values, start, stop, axis=direction % values.ndim)]
    pallas_call x0 -> x11, Pallas kernels: none -> 12.6 us  [call(): pl.pallas_call(kernel, out_shape=shapes, in_specs=[pl.BlockSpec(memory_sp...]
    unnamed x92 -> x10, local copies, waits for them, and re-layouts: 14.1 us -> 2.58 us
    ppermute x10 -> x13, starting transfers between devices: 26 us -> 19.1 us  [swap(): return lax.ppermute(block, axis, [(i, i ^ mask) for i in range(n)])]
    all_to_all x2 -> x0, waiting for transfers between devices: 5.57 us -> none  [the longest x1 5.57 us: per_device(): lax.all_to_all(answer, 'gx', split_axis=0, concat_axis=1, tiled=True)]
    another operation x10 -> x0, local copies, waits for them, and re-layouts: 3.97 us -> none  [the longest x4 2.76 us: split_rows(): jnp.stack([cut_range(values, 1, extent - 1, direction), low_source, high_...]
  transfers between devices with their start and end apart: 12 -> 13, of which waited for: 8 -> 7; matrix products, arithmetic and copies ran while one was open for 10% -> 0% of each run, Pallas kernels for 0% -> 17%
where the time goes in v1:
time: 52.5 us; the launch traced here: 52.3 us
  starting transfers between devices  19.1 us (36%)
  waiting for transfers between devices  17.9 us (34%)
  Pallas kernels  12.6 us (24%)
  local copies, waits for them, and re-layouts  2.58 us (5%)
    ppermute x13, starting transfers between devices, swap(): return lax.ppermute(block, axis, [(i, i ^ mask) for i in range(n)])  19.1 us
    ppermute x13, waiting for transfers between devices, swap(): return lax.ppermute(block, axis, [(i, i ^ mask) for i in range(n)])  17.9 us
    pallas_call x11, Pallas kernels, call(): pl.pallas_call(kernel, out_shape=shapes, in_specs=[pl.BlockSpec(memory_sp...  12.6 us
    unnamed x10, local copies, waits for them, and re-layouts  2.58 us
  transfers between devices with their start and end apart: 13, of which 7 were waited for; matrix products, arithmetic and copies ran while one was open for 0% of the time, Pallas kernels for 17%

profile of v1, /device:TPU:0, one launch (start us, length us, event | category | flops | bytes accessed | tf_op | source)
XLA Modules:
  0.0 52.3 jit_solution(15600815412276490186)
XLA Ops:
  0.0 0.9 %copy-done = f32[8,64,128]{2,1,0:T(8,128)S(1)} copy-done((f32[8,64,128]{2,1,0:T(8,128)S(1)}, f32[8,64,128]{2,1,0:T(8,128)}, u32[]{:S(2)}) %copy-start) | copy-done | bytes 262168
  1.0 0.9 %copy-done.2 = f32[8,64,128]{2,1,0:T(8,128)S(1)} copy-done((f32[8,64,128]{2,1,0:T(8,128)S(1)}, f32[8,64,128]{2,1,0:T(8,128)}, u32[]{:S(2)}) %copy-start.2) | copy-done | bytes 262168
  1.9 0.5 edges.1.own_ref
  2.4 1.7 %collective-permute-start = (f32[8,512]{1,0:T(8,128)S(1)}, f32[8,512]{1,0:T(8,128)S(1)}, u32[]{:S(2)}, u32[]{:S(2)}) collective-permute-start(f32[8,512]{1,0:T(8,128)S(1)} %edges.1.own_ref), channel_id=1, source_target_pairs={{0,1},{1,0},{2,3},{3,2},{4,5},{5,4},{6,7},{7,6},{8,9},{9,8},{10,11... | collective-permute-start | bytes 49160 | tf_op jit(solution)/shard_map/ppermute | solution.py:400
  4.1 2.2 %collective-permute-start.1 = (f32[8,512]{1,0:T(8,128)S(1)}, f32[8,512]{1,0:T(8,128)S(1)}, u32[]{:S(2)}, u32[]{:S(2)}) collective-permute-start(f32[8,512]{1,0:T(8,128)S(1)} %edges.1.own_ref), channel_id=1, source_target_pairs={{0,3},{1,2},{2,1},{3,0},{4,7},{5,6},{6,5},{7,4},{8,11},{9,10},{10,... | collective-permute-start | bytes 49160 | tf_op jit(solution)/shard_map/ppermute | solution.py:400
  6.3 0.5 %local.1 = (f32[8,64,128]{2,1,0:T(8,128)S(1)}, f32[6,64,128]{2,1,0:T(8,128)S(1)}, f32[6,64,128]{2,1,0:T(8,128)S(1)}, f32[6,64,128]{2,1,0:T(8,128)S(1)}, f32[3,64,128]{2,1,0:T(8,128)S(1)}) custom-call(f32[8,64,128]{2,1,0:T(8,128)S(1)} %copy-done.2, f32[8,64,128]{2,1,0:T(8,128)S(1)} %copy-done, f32[8,64,128]{2,1,0:T(8,128)S(1)} %copy-done.4), custom_call_target="tpu_custom_call" | custom-call | bytes 1736704 | tf_op jit(solution)/shard_map/local/pallas_call | solution.py:24
  6.8 2.2 %collective-permute-done.1.two_ref = f32[8,512]{1,0:T(8,128)S(1)} collective-permute-done((f32[8,512]{1,0:T(8,128)S(1)}, f32[8,512]{1,0:T(8,128)S(1)}, u32[]{:S(2)}, u32[]{:S(2)}) %collective-permute-start.1) | collective-permute-done | bytes 16416 | tf_op jit(solution)/shard_map/ppermute | solution.py:400
  9.0 0.5 halo.1
  9.5 0.1 collective-permute-start.2
  9.6 1.3 %collective-permute-done.2.got_ref = f32[7,32,128]{2,1,0:T(8,128)S(1)} collective-permute-done((f32[7,32,128]{2,1,0:T(8,128)S(1)}, f32[7,32,128]{2,1,0:T(8,128)S(1)}, u32[]{:S(2)}, u32[]{:S(2)}) %collective-permute-start.2) | collective-permute-done | bytes 114720 | tf_op jit(solution)/shard_map/ppermute | solution.py:400
  11.0 1.6 %collective-permute-start.3 = (f32[7,32,128]{2,1,0:T(8,128)S(1)}, f32[7,32,128]{2,1,0:T(8,128)S(1)}, u32[]{:S(2)}, u32[]{:S(2)}) collective-permute-start(f32[7,32,128]{2,1,0:T(8,128)S(1)} %get-tuple-element.35.own_ref), channel_id=1, source_target_pairs={{0,8},{4,12},{8,0},{12,4},{16,24},{20,28},{24,16},{28,20},{32,40},... | collective-permute-start | bytes 344072 | tf_op jit(solution)/shard_map/ppermute | solution.py:400
  12.6 2.7 %collective-permute-start.4 = (f32[7,32,128]{2,1,0:T(8,128)S(1)}, f32[7,32,128]{2,1,0:T(8,128)S(1)}, u32[]{:S(2)}, u32[]{:S(2)}) collective-permute-start(f32[7,32,128]{2,1,0:T(8,128)S(1)} %get-tuple-element.35.own_ref), channel_id=1, source_target_pairs={{0,16},{4,20},{8,24},{12,28},{16,0},{20,4},{24,8},{28,12},{32,48},... | collective-permute-start | bytes 344072 | tf_op jit(solution)/shard_map/ppermute | solution.py:400
  15.3 0.5 collective-permute-start.5
  15.8 0.8 %collective-permute-done.3.one_ref = f32[7,32,128]{2,1,0:T(8,128)S(1)} collective-permute-done((f32[7,32,128]{2,1,0:T(8,128)S(1)}, f32[7,32,128]{2,1,0:T(8,128)S(1)}, u32[]{:S(2)}, u32[]{:S(2)}) %collective-permute-start.3) | collective-permute-done | bytes 114720 | tf_op jit(solution)/shard_map/ppermute | solution.py:400
  16.6 4.5 %collective-permute-done.4.two_ref = f32[7,32,128]{2,1,0:T(8,128)S(1)} collective-permute-done((f32[7,32,128]{2,1,0:T(8,128)S(1)}, f32[7,32,128]{2,1,0:T(8,128)S(1)}, u32[]{:S(2)}, u32[]{:S(2)}) %collective-permute-start.4) | collective-permute-done | bytes 114720 | tf_op jit(solution)/shard_map/ppermute | solution.py:400
  21.0 2.1 %collective-permute-done.5.three_ref = f32[7,32,128]{2,1,0:T(8,128)S(1)} collective-permute-done((f32[7,32,128]{2,1,0:T(8,128)S(1)}, f32[7,32,128]{2,1,0:T(8,128)S(1)}, u32[]{:S(2)}, u32[]{:S(2)}) %collective-permute-start.5) | collective-permute-done | bytes 114720 | tf_op jit(solution)/shard_map/ppermute | solution.py:400
  23.1 0.1 chips.1
  23.3 2.0 %collective-permute-start.6 = (f32[7,32,128]{2,1,0:T(8,128)S(1)}, f32[7,32,128]{2,1,0:T(8,128)S(1)}, u32[]{:S(2)}, u32[]{:S(2)}) collective-permute-start(f32[7,32,128]{2,1,0:T(8,128)S(1)} %get-tuple-element.36.own_ref.after_ref), channel_id=1, source_target_pairs={{0,32},{4,36},{8,40},{12,44},{16,48},{20,52},{24,56},{28,60},{32,0... | collective-permute-start | bytes 344072 | tf_op jit(solution)/shard_map/ppermute | solution.py:400
  25.2 3.6 %collective-permute-start.7 = (f32[7,32,128]{2,1,0:T(8,128)S(1)}, f32[7,32,128]{2,1,0:T(8,128)S(1)}, u32[]{:S(2)}, u32[]{:S(2)}) collective-permute-start(f32[7,32,128]{2,1,0:T(8,128)S(1)} %get-tuple-element.36.own_ref.after_ref), channel_id=1, source_target_pairs={{0,64},{4,68},{8,72},{12,76},{16,80},{20,84},{24,88},{28,92},{32,9... | collective-permute-start | bytes 344072 | tf_op jit(solution)/shard_map/ppermute | solution.py:400
  28.8 0.0 collective-permute-start.8
  28.8 5.3 %collective-permute-done.7.two_ref = f32[7,32,128]{2,1,0:T(8,128)S(1)} collective-permute-done((f32[7,32,128]{2,1,0:T(8,128)S(1)}, f32[7,32,128]{2,1,0:T(8,128)S(1)}, u32[]{:S(2)}, u32[]{:S(2)}) %collective-permute-start.7) | collective-permute-done | bytes 114720 | tf_op jit(solution)/shard_map/ppermute | solution.py:400
  34.1 1.8 %collective-permute-done.8.three_ref = f32[7,32,128]{2,1,0:T(8,128)S(1)} collective-permute-done((f32[7,32,128]{2,1,0:T(8,128)S(1)}, f32[7,32,128]{2,1,0:T(8,128)S(1)}, u32[]{:S(2)}, u32[]{:S(2)}) %collective-permute-start.8) | collective-permute-done | bytes 114720 | tf_op jit(solution)/shard_map/ppermute | solution.py:400
  35.9 0.2 back.1
  36.1 0.1 collective-permute-start.9
  36.2 0.7 %copy-done.3 = f32[8,64,128]{2,1,0:T(8,128)S(1)} copy-done((f32[8,64,128]{2,1,0:T(8,128)S(1)}, f32[8,64,128]{2,1,0:T(8,128)}, u32[]{:S(2)}) %copy-start.3) | copy-done | bytes 262168
  36.9 0.4 prepare.1
  37.2 3.9 %z_ports.1 = (f32[64,8,128]{2,1,0:T(8,128)S(1)}, f32[64,8,128]{2,1,0:T(8,128)S(1)}, f32[8,512]{1,0:T(8,128)S(1)}) custom-call(f32[8,64,128]{2,1,0:T(8,128)S(1)} %copy-done.1, f32[7,32,128]{2,1,0:T(8,128)S(1)} %get-tuple-element.36.own_ref.after_ref), custom_call_target="tpu_custom_call" | custom-call | bytes 917504 | tf_op jit(solution)/shard_map/z_ports/pallas_call | solution.py:24
  41.2 0.8 %y_solve.1 = (f32[64,8,128]{2,1,0:T(8,128)S(1)}, f32[8,512]{1,0:T(8,128)S(1)}) custom-call(f32[2,32,128]{2,1,0:T(8,128)S(1)} %get-tuple-element.39.keep_ref, f32[2,32,128]{2,1,0:T(8,128)S(1)} %collective-permute-done.9.got_ref, f32[8,64,128]{2,1,0:T(8,128)S(1)} %get-tuple-element.43.base_ref, f32[6,64,128]{2,1,0:T(8,128)S(1)} %get-tuple-element.44.gx_ref, ...), custom_call_target="tpu_custom_call" | custom-call | bytes 2064384 | tf_op jit(solution)/shard_map/y_solve/pallas_call | solution.py:24
  42.0 3.7 %collective-permute-start.11 = (f32[8,512]{1,0:T(8,128)S(1)}, f32[8,512]{1,0:T(8,128)S(1)}, u32[]{:S(2)}, u32[]{:S(2)}) collective-permute-start(f32[8,512]{1,0:T(8,128)S(1)} %get-tuple-element.51.own_ref), channel_id=1, source_target_pairs={{0,2},{1,3},{2,0},{3,1},{4,6},{5,7},{6,4},{7,5},{8,10},{9,11},{10,... | collective-permute-start | bytes 49160 | tf_op jit(solution)/shard_map/ppermute | solution.py:400
  45.6 1.1 %collective-permute-start.12 = (f32[8,512]{1,0:T(8,128)S(1)}, f32[8,512]{1,0:T(8,128)S(1)}, u32[]{:S(2)}, u32[]{:S(2)}) collective-permute-start(f32[8,512]{1,0:T(8,128)S(1)} %get-tuple-element.51.own_ref), channel_id=1, source_target_pairs={{0,3},{1,2},{2,1},{3,0},{4,7},{5,6},{6,5},{7,4},{8,11},{9,10},{10,... | collective-permute-start | bytes 49160 | tf_op jit(solution)/shard_map/ppermute | solution.py:400
  46.7 3.9 %z_local.1.y_ref = f32[64,8,128]{2,1,0:T(8,128)S(1)} custom-call(f32[8,64,128]{2,1,0:T(8,128)S(1)} %copy-done.1, f32[64,8,128]{2,1,0:T(8,128)S(1)} %get-tuple-element.52.v_ref), custom_call_target="tpu_custom_call" | custom-call | bytes 786432 | tf_op jit(solution)/shard_map/z_local/pallas_call | solution.py:24
  50.7 1.6 %final.1 = f32[8,64,128]{2,1,0:T(8,128)} custom-call(f32[8,512]{1,0:T(8,128)S(1)} %get-tuple-element.51.own_ref, f32[8,512]{1,0:T(8,128)S(1)} %collective-permute-done.10.one_ref, f32[8,512]{1,0:T(8,128)S(1)} %collective-permute-done.11.two_ref, f32[8,512]{1,0:T(8,128)S(1)} %collective-permute-done.12.three_ref, f32[64,8,128]{2,1,0:T(8,128)S(1)} %z_local.1.y_ref, ...), custom_call_target="tpu_custom_call" | custom-call | bytes 1376256 | tf_op jit(solution)/shard_map/final/pallas_call | solution.py:24
  (15 shorter events, 0.1 us)
Async XLA Ops:
  0.0 0.9 %copy-start = (f32[8,64,128]{2,1,0:T(8,128)S(1)}, f32[8,64,128]{2,1,0:T(8,128)}, u32[]{:S(2)}) copy-start(f32[8,64,128]{2,1,0:T(8,128)} %k_ref.11) | copy-start | bytes 786436
  1.0 0.9 %copy-start.2 = (f32[8,64,128]{2,1,0:T(8,128)S(1)}, f32[8,64,128]{2,1,0:T(8,128)}, u32[]{:S(2)}) copy-start(f32[8,64,128]{2,1,0:T(8,128)} %u_ref.7) | copy-start | bytes 786436
  1.9 4.4 %copy-start.4 = (f32[8,64,128]{2,1,0:T(8,128)S(1)}, f32[8,64,128]{2,1,0:T(8,128)}, u32[]{:S(2)}) copy-start(f32[8,64,128]{2,1,0:T(8,128)} %f_ref.1) | copy-start | bytes 786436
  2.4 6.6 %copy-start.1 = (f32[8,64,128]{2,1,0:T(8,128)S(1)}, f32[8,64,128]{2,1,0:T(8,128)}, u32[]{:S(2)}) copy-start(f32[8,64,128]{2,1,0:T(8,128)} %k_ref.11) | copy-start | bytes 786436
  2.4 4.4 %collective-permute-start = (f32[8,512]{1,0:T(8,128)S(1)}, f32[8,512]{1,0:T(8,128)S(1)}, u32[]{:S(2)}, u32[]{:S(2)}) collective-permute-start(f32[8,512]{1,0:T(8,128)S(1)} %edges.1.own_ref), channel_id=1, source_target_pairs={{0,1},{1,0},{2,3},{3,2},{4,5},{5,4},{6,7},{7,6},{8,9},{9,8},{10,11... | collective-permute-start | bytes 49160 | tf_op jit(solution)/shard_map/ppermute | solution.py:400
  4.1 4.9 %collective-permute-start.1 = (f32[8,512]{1,0:T(8,128)S(1)}, f32[8,512]{1,0:T(8,128)S(1)}, u32[]{:S(2)}, u32[]{:S(2)}) collective-permute-start(f32[8,512]{1,0:T(8,128)S(1)} %edges.1.own_ref), channel_id=1, source_target_pairs={{0,3},{1,2},{2,1},{3,0},{4,7},{5,6},{6,5},{7,4},{8,11},{9,10},{10,... | collective-permute-start | bytes 49160 | tf_op jit(solution)/shard_map/ppermute | solution.py:400
  9.5 1.4 %collective-permute-start.2 = (f32[7,32,128]{2,1,0:T(8,128)S(1)}, f32[7,32,128]{2,1,0:T(8,128)S(1)}, u32[]{:S(2)}, u32[]{:S(2)}) collective-permute-start(f32[7,32,128]{2,1,0:T(8,128)S(1)} %get-tuple-element.34), channel_id=1, source_target_pairs={{0,4},{4,0},{8,12},{12,8},{16,20},{20,16},{24,28},{28,24},{32,36},... | collective-permute-start | bytes 344072 | tf_op jit(solution)/shard_map/ppermute | solution.py:400
  11.0 5.6 %collective-permute-start.3 = (f32[7,32,128]{2,1,0:T(8,128)S(1)}, f32[7,32,128]{2,1,0:T(8,128)S(1)}, u32[]{:S(2)}, u32[]{:S(2)}) collective-permute-start(f32[7,32,128]{2,1,0:T(8,128)S(1)} %get-tuple-element.35.own_ref), channel_id=1, source_target_pairs={{0,8},{4,12},{8,0},{12,4},{16,24},{20,28},{24,16},{28,20},{32,40},... | collective-permute-start | bytes 344072 | tf_op jit(solution)/shard_map/ppermute | solution.py:400
  12.6 8.5 %collective-permute-start.4 = (f32[7,32,128]{2,1,0:T(8,128)S(1)}, f32[7,32,128]{2,1,0:T(8,128)S(1)}, u32[]{:S(2)}, u32[]{:S(2)}) collective-permute-start(f32[7,32,128]{2,1,0:T(8,128)S(1)} %get-tuple-element.35.own_ref), channel_id=1, source_target_pairs={{0,16},{4,20},{8,24},{12,28},{16,0},{20,4},{24,8},{28,12},{32,48},... | collective-permute-start | bytes 344072 | tf_op jit(solution)/shard_map/ppermute | solution.py:400
  15.3 7.8 %collective-permute-start.5 = (f32[7,32,128]{2,1,0:T(8,128)S(1)}, f32[7,32,128]{2,1,0:T(8,128)S(1)}, u32[]{:S(2)}, u32[]{:S(2)}) collective-permute-start(f32[7,32,128]{2,1,0:T(8,128)S(1)} %get-tuple-element.35.own_ref), channel_id=1, source_target_pairs={{0,24},{4,28},{8,16},{12,20},{16,8},{20,12},{24,0},{28,4},{32,56},... | collective-permute-start | bytes 344072 | tf_op jit(solution)/shard_map/ppermute | solution.py:400
  23.3 5.6 %collective-permute-start.6 = (f32[7,32,128]{2,1,0:T(8,128)S(1)}, f32[7,32,128]{2,1,0:T(8,128)S(1)}, u32[]{:S(2)}, u32[]{:S(2)}) collective-permute-start(f32[7,32,128]{2,1,0:T(8,128)S(1)} %get-tuple-element.36.own_ref.after_ref), channel_id=1, source_target_pairs={{0,32},{4,36},{8,40},{12,44},{16,48},{20,52},{24,56},{28,60},{32,0... | collective-permute-start | bytes 344072 | tf_op jit(solution)/shard_map/ppermute | solution.py:400
  25.2 8.9 %collective-permute-start.7 = (f32[7,32,128]{2,1,0:T(8,128)S(1)}, f32[7,32,128]{2,1,0:T(8,128)S(1)}, u32[]{:S(2)}, u32[]{:S(2)}) collective-permute-start(f32[7,32,128]{2,1,0:T(8,128)S(1)} %get-tuple-element.36.own_ref.after_ref), channel_id=1, source_target_pairs={{0,64},{4,68},{8,72},{12,76},{16,80},{20,84},{24,88},{28,92},{32,9... | collective-permute-start | bytes 344072 | tf_op jit(solution)/shard_map/ppermute | solution.py:400
  28.8 7.1 %collective-permute-start.8 = (f32[7,32,128]{2,1,0:T(8,128)S(1)}, f32[7,32,128]{2,1,0:T(8,128)S(1)}, u32[]{:S(2)}, u32[]{:S(2)}) collective-permute-start(f32[7,32,128]{2,1,0:T(8,128)S(1)} %get-tuple-element.36.own_ref.after_ref), channel_id=1, source_target_pairs={{0,96},{4,100},{8,104},{12,108},{16,112},{20,116},{24,120},{28,124... | collective-permute-start | bytes 344072 | tf_op jit(solution)/shard_map/ppermute | solution.py:400
  35.9 1.0 %copy-start.3 = (f32[8,64,128]{2,1,0:T(8,128)S(1)}, f32[8,64,128]{2,1,0:T(8,128)}, u32[]{:S(2)}) copy-start(f32[8,64,128]{2,1,0:T(8,128)} %u_ref.7) | copy-start | bytes 786436
  36.1 5.1 %collective-permute-start.9 = (f32[2,32,128]{2,1,0:T(8,128)S(1)}, f32[2,32,128]{2,1,0:T(8,128)S(1)}, u32[]{:S(2)}, u32[]{:S(2)}) collective-permute-start(f32[2,32,128]{2,1,0:T(8,128)S(1)} %get-tuple-element.40), channel_id=1, source_target_pairs={{0,4},{4,0},{8,12},{12,8},{16,20},{20,16},{24,28},{28,24},{32,36},... | collective-permute-start | bytes 98312 | tf_op jit(solution)/shard_map/ppermute | solution.py:400
  42.0 8.7 %collective-permute-start.10 = (f32[8,512]{1,0:T(8,128)S(1)}, f32[8,512]{1,0:T(8,128)S(1)}, u32[]{:S(2)}, u32[]{:S(2)}) collective-permute-start(f32[8,512]{1,0:T(8,128)S(1)} %get-tuple-element.51.own_ref), channel_id=1, source_target_pairs={{0,1},{1,0},{2,3},{3,2},{4,5},{5,4},{6,7},{7,6},{8,9},{9,8},{10,11... | collective-permute-start | bytes 49160 | tf_op jit(solution)/shard_map/ppermute | solution.py:400
  42.0 8.7 %collective-permute-start.11 = (f32[8,512]{1,0:T(8,128)S(1)}, f32[8,512]{1,0:T(8,128)S(1)}, u32[]{:S(2)}, u32[]{:S(2)}) collective-permute-start(f32[8,512]{1,0:T(8,128)S(1)} %get-tuple-element.51.own_ref), channel_id=1, source_target_pairs={{0,2},{1,3},{2,0},{3,1},{4,6},{5,7},{6,4},{7,5},{8,10},{9,11},{10,... | collective-permute-start | bytes 49160 | tf_op jit(solution)/shard_map/ppermute | solution.py:400
  45.6 5.0 %collective-permute-start.12 = (f32[8,512]{1,0:T(8,128)S(1)}, f32[8,512]{1,0:T(8,128)S(1)}, u32[]{:S(2)}, u32[]{:S(2)}) collective-permute-start(f32[8,512]{1,0:T(8,128)S(1)} %get-tuple-element.51.own_ref), channel_id=1, source_target_pairs={{0,3},{1,2},{2,1},{3,0},{4,7},{5,6},{6,5},{7,4},{8,11},{9,10},{10,... | collective-permute-start | bytes 49160 | tf_op jit(solution)/shard_map/ppermute | solution.py:400

commit v2 on v1

--- a/solution.py
+++ b/solution.py
@@ -18,15 +18,16 @@
 HIGHEST = lax.Precision.HIGHEST
 
 
-def call(kernel, outs, *args, scratch=(), flops=0, name=None):
+def call(kernel, outs, *args, scratch=(), sems=0, ins_in=pltpu.VMEM, outs_in=pltpu.VMEM, flops=0, name=None):
     shapes = [jax.ShapeDtypeStruct(s, F32) for s in outs]
     nbytes = sum(4 * a.size for a in args) + sum(4 * s.size for s in shapes)
     return pl.pallas_call(
         kernel,
         out_shape=shapes,
-        in_specs=[pl.BlockSpec(memory_space=pltpu.VMEM) for _ in args],
-        out_specs=[pl.BlockSpec(memory_space=pltpu.VMEM) for _ in outs],
-        scratch_shapes=[pltpu.VMEM(s, F32) for s in scratch],
+        in_specs=[pl.BlockSpec(memory_space=ins_in) for _ in args],
+        out_specs=[pl.BlockSpec(memory_space=outs_in) for _ in outs],
+        scratch_shapes=[pltpu.VMEM(s, F32) for s in scratch]
+        + [pltpu.SemaphoreType.DMA] * sems,
         compiler_params=pltpu.CompilerParams(vmem_limit_bytes=VMEM_LIMIT),
         cost_estimate=pl.CostEstimate(flops=flops, bytes_accessed=nbytes, transcendentals=0),
         name=name,
@@ -107,12 +108,18 @@
     return e, c, r
 
 
-def edges_kernel(u_ref, k_ref, out_ref):
-    u = u_ref[...].reshape(ROWS, NZ)
-    k = k_ref[...].reshape(ROWS, NZ)
-    out_ref[...] = lanes_to_rows(selector([(0, 0), (1, NZ - 1)]), u) + lanes_to_rows(
-        selector([(2, 0), (3, NZ - 1)]), k
-    )
+def edges_kernel(u_hbm, k_hbm, f_hbm, u_ref, k_ref, f_ref, out_ref, *sems):
+    pairs = ((u_hbm, u_ref), (k_hbm, k_ref), (f_hbm, f_ref))
+    copies = [pltpu.make_async_copy(a, b, sem) for (a, b), sem in zip(pairs, sems)]
+    for copy in copies:
+        copy.start()
+    copies[0].wait()
+    u = lanes_to_rows(selector([(0, 0), (1, NZ - 1)]), u_ref[...].reshape(ROWS, NZ))
+    copies[1].wait()
+    out_ref[...] = u + lanes_to_rows(
+        selector([(2, 0), (3, NZ - 1)]), k_ref[...].reshape(ROWS, NZ)
+    )
+    copies[2].wait()
 
 
 def local_kernel(u_ref, k_ref, f_ref, rp_ref, a_ref, m_ref, inv_ref, ew_ref):
@@ -186,7 +193,7 @@
     return held
 
 
-def chips_kernel(own_ref, one_ref, two_ref, three_ref, out_ref, parts_ref, held):
+def chips_kernel(own_ref, one_ref, two_ref, three_ref, after_ref, also_ref, out_ref, parts_ref, held):
     me = lax.rem(lax.axis_index("gx") // 2, 4)
     ordered(me, (own_ref, one_ref, two_ref, three_ref), held)
     blocks = [[held[b, i] for i in range(7)] for b in range(4)]
@@ -199,7 +206,7 @@
             parts_ref[3 * j + i] = p[i]
 
 
-def back_kernel(own_ref, one_ref, two_ref, three_ref, chips_ref, cores_ref, keep_ref, send_ref, held, nodes):
+def back_kernel(own_ref, one_ref, two_ref, three_ref, chips_ref, cores_ref, after_ref, keep_ref, send_ref, held, nodes):
     index = lax.axis_index("gx")
     core, x, z = lax.rem(index, 2), lax.rem(index // 2, 4), index // 8
     ordered(z, (own_ref, one_ref, two_ref, three_ref), held)
@@ -256,53 +263,56 @@
     my_ref[mid] = jnp.zeros((NX, NZ), F32)
 
 
-def z_levels(k, r):
+LEVELS = 7
+STEP = 16
+
+
+def z_factors(k, keep):
     lane = lax.broadcasted_iota(jnp.int32, k.shape, 1)
     up = CZ * (k + pltpu.roll(k, NZ - 1, 1))
     low = pltpu.roll(up, 1, 1)
     top = up
     e = jnp.ones(k.shape, F32)
-    s = 1
-    while s < NZ:
+    for n in range(LEVELS):
+        s = 1 << n
         inv = 1.0 / (e + low + up)
         has_low, has_up = lane >= s + 1, lane <= NZ - 2 - s
+        low_in, up_in = jnp.where(has_low, low, 0.0), jnp.where(has_up, up, 0.0)
+        keep(n, low_in, up_in, inv)
         share = e * inv
-        low_in, up_in = jnp.where(has_low, low, 0.0), jnp.where(has_up, up, 0.0)
         e = e + low_in * pltpu.roll(share, s, 1) + up_in * pltpu.roll(share, NZ - s, 1)
-        if r is not None:
-            q = r * inv
-            r = r + low_in * pltpu.roll(q, s, 1) + up_in * pltpu.roll(q, NZ - s, 1)
         new_low = jnp.where(has_low, low * pltpu.roll(low * inv, s, 1), low)
         up = jnp.where(has_up, up * pltpu.roll(up * inv, NZ - s, 1), up)
         low = new_low
-        s *= 2
     inv = 1.0 / (e + low + up)
     first, last = lane == 0, lane == NZ - 1
-    if r is not None:
-        return jnp.where(first | last, 0.0, r * inv)
     g = jnp.where(first, 1.0, jnp.where(last, 0.0, low * inv))
     h = jnp.where(first, 0.0, jnp.where(last, 1.0, up * inv))
-    return g, h, jnp.where(lane == NZ - 2, top * g, 0.0)
-
-
-STEP = 32
-
-
-def z_ports_kernel(k_ref, after_ref, g_ref, h_ref, port_ref, t_ref):
+    inv = jnp.where(first | last, 0.0, inv)
+    return g, h, jnp.where(lane == NZ - 2, top * g, 0.0), inv
+
+
+def z_ports_kernel(start, k_ref, after_ref, g_ref, h_ref, port_ref, f_ref, t_ref):
     del after_ref
     k2 = k_ref.reshape(ROWS, NZ)
-    g2, h2 = g_ref.reshape(ROWS, NZ), h_ref.reshape(ROWS, NZ)
+    g2, h2 = g_ref.reshape(ROWS // 2, NZ), h_ref.reshape(ROWS // 2, NZ)
 
     def body(i, carry):
-        y = i * STEP
+        y = start + i * STEP
         k = jnp.concatenate([k2[pl.ds(y + n, NX, stride=NY), :] for n in range(STEP)], axis=0)
-        g, h, w = z_levels(k, None)
-        at = pl.ds(pl.multiple_of(y * NX, NX * STEP), NX * STEP)
+        at = pl.ds(pl.multiple_of(i * (STEP * NX), NX * STEP), NX * STEP)
+
+        def keep(n, *values):
+            for j, v in enumerate(values):
+                f_ref[3 * n + j, at, :] = v
+
+        g, h, w, inv = z_factors(k, keep)
+        f_ref[3 * LEVELS, at, :] = inv
         g2[at, :], h2[at, :] = g, h
         t_ref[0, at, :], t_ref[1, at, :] = k, w
         return carry
 
-    lax.fori_loop(0, NY // STEP, body, 0)
+    lax.fori_loop(0, HALF // STEP, body, 0)
     port_ref[...] = (
         lanes_to_rows(selector([(0, None)]), g2[...])
         + lanes_to_rows(selector([(1, None)]), h2[...])
@@ -311,7 +321,7 @@
     )
 
 
-def y_kernel(keep_ref, got_ref, base_ref, gx_ref, hx_ref, my_ref, iy_ref, g_ref, h_ref, port_ref, v_ref, out_ref, b_ref, s_ref, d_ref):
+def y_kernel(keep_ref, got_ref, base_ref, gx_ref, hx_ref, my_ref, iy_ref, g0_ref, g1_ref, h0_ref, h1_ref, p0_ref, p1_ref, v_ref, out_ref, b_ref, s_ref, d_ref):
     core = lax.rem(lax.axis_index("gx"), 2)
     for i in range(2):
         b_ref[i, pl.ds(pl.multiple_of(core * HALF, HALF), HALF)] = keep_ref[i]
@@ -337,8 +347,9 @@
 
     def emit(y, v):
         v_ref[y] = v
-        d_ref[0, y * NX : (y + 1) * NX, :] = g_ref[y] * v
-        d_ref[1, y * NX : (y + 1) * NX, :] = h_ref[y] * v
+        g, h = (g0_ref, h0_ref) if y < HALF else (g1_ref, h1_ref)
+        d_ref[0, y * NX : (y + 1) * NX, :] = g[y % HALF] * v
+        d_ref[1, y * NX : (y + 1) * NX, :] = h[y % HALF] * v
 
     emit(mid, v)
     for n in range(1, mid + 1):
@@ -350,27 +361,40 @@
             high = v_ref[y] + my_ref[y] * high
             emit(y, high)
     out_ref[...] = (
-        port_ref[...]
+        jnp.concatenate([p0_ref[...], p1_ref[...]], axis=1)
         + lanes_to_rows(selector([(3, None)]), d_ref[0])
         + lanes_to_rows(selector([(4, None)]), d_ref[1])
     )
 
 
-def z_local_kernel(k_ref, v_ref, y_ref):
-    k2 = k_ref.reshape(ROWS, NZ)
+def z_local_kernel(f0_ref, f1_ref, v_ref, y_ref):
     v2, y2 = v_ref.reshape(ROWS, NZ), y_ref.reshape(ROWS, NZ)
-
-    def body(i, carry):
-        y = i * STEP
-        k = jnp.concatenate([k2[pl.ds(y + n, NX, stride=NY), :] for n in range(STEP)], axis=0)
-        at = pl.ds(pl.multiple_of(y * NX, NX * STEP), NX * STEP)
-        y2[at, :] = z_levels(k, v2[at, :])
-        return carry
-
-    lax.fori_loop(0, NY // STEP, body, 0)
-
-
-def final_kernel(own_ref, one_ref, two_ref, three_ref, y_ref, g_ref, h_ref, u_ref, out_ref, held, nodes, b_ref):
+    rows = STEP * NX
+
+    for half, f_ref in enumerate((f0_ref, f1_ref)):
+
+        def body(i, carry):
+            at = pl.ds(pl.multiple_of(i * rows, rows), rows)
+            full = pl.ds(pl.multiple_of(half * (ROWS // 2) + i * rows, rows), rows)
+            r = v2[full, :]
+            for n in range(LEVELS):
+                s = 1 << n
+                q = r * f_ref[3 * n + 2, at, :]
+                r = (
+                    r
+                    + f_ref[3 * n, at, :] * pltpu.roll(q, s, 1)
+                    + f_ref[3 * n + 1, at, :] * pltpu.roll(q, NZ - s, 1)
+                )
+            y2[full, :] = r * f_ref[3 * LEVELS, at, :]
+            return carry
+
+        lax.fori_loop(0, HALF // STEP, body, 0)
+
+
+CHUNK = 16
+
+
+def final_kernel(own_ref, one_ref, two_ref, three_ref, y_ref, g0_ref, g1_ref, h0_ref, h1_ref, u_ref, out_ref, held, b_ref, o_ref, *sems):
     me = lax.axis_index("gz")
     ordered(me, (own_ref, one_ref, two_ref, three_ref), held)
     blocks = [[held[b, i : i + 1, :] for i in range(7)] for b in range(4)]
@@ -386,13 +410,21 @@
     both = jnp.where(row == 0, first, jnp.where(row == 1, last, 0.0))
     b_ref[0] = rows_to_lanes(both, selector([(0, None)]))
     b_ref[1] = rows_to_lanes(both, selector([(1, None)]))
-    u2, out2 = u_ref.reshape(ROWS, NZ), out_ref.reshape(ROWS, NZ)
+    u2, o2 = u_ref.reshape(ROWS, NZ), o_ref.reshape(ROWS, NZ)
+    copies = []
     for y in range(NY):
         at = pl.ds(y, NX, stride=NY)
         ys = slice(y * NX, (y + 1) * NX)
-        out2[at, :] = u2[at, :] + 2.0 * (
-            y_ref[y] + g_ref[y] * b_ref[0, ys, :] + h_ref[y] * b_ref[1, ys, :]
+        g, h = (g0_ref, h0_ref) if y < HALF else (g1_ref, h1_ref)
+        o2[at, :] = u2[at, :] + 2.0 * (
+            y_ref[y] + g[y % HALF] * b_ref[0, ys, :] + h[y % HALF] * b_ref[1, ys, :]
         )
+        if y % CHUNK == CHUNK - 1:
+            part = pl.ds(y + 1 - CHUNK, CHUNK)
+            copies.append(pltpu.make_async_copy(o_ref.at[:, part], out_ref.at[:, part], sems[y // CHUNK]))
+            copies[-1].start()
+    for copy in copies:
+        copy.wait()
 
 
 def swap(block, axis, mask):
@@ -401,7 +433,10 @@
 
 
 def per_device(u, k, f):
-    edges, = call(edges_kernel, [(8, ROWS)], u, k, name="edges")
+    u, k, f = (pltpu.with_memory_space_constraint(t, pltpu.HBM) for t in (u, k, f))
+    u, k, f, edges = call(
+        edges_kernel, [(NX, NY, NZ)] * 3 + [(8, ROWS)], u, k, f, sems=3, ins_in=pltpu.HBM, name="edges"
+    )
     one, two = swap(edges, "gz", 1), swap(edges, "gz", 3)
     rp, a, m, inv, ew = call(
         local_kernel,
@@ -421,35 +456,40 @@
         [(NX, NY, NZ), (NX - 2, NY, NZ), (NX - 2, NY, NZ), (NY, NX, NZ), (NY, NX, NZ)],
         u, k, a, m, inv, rr, name="prepare",
     )
+    z_shapes = [(HALF, NX, NZ), (HALF, NX, NZ), (8, ROWS // 2), (3 * LEVELS + 1, ROWS // 2, NZ)]
+    g0, h0, p0, f0 = call(
+        functools.partial(z_ports_kernel, 0), z_shapes, k, chip, scratch=[(2, ROWS // 2, NZ)], name="z_ports"
+    )
     group, chip_parts = call(
-        chips_kernel, [(7, HALF, NZ), (18, HALF, NZ)], chip, *x_got, scratch=[(4, 7, HALF, NZ)], name="chips"
+        chips_kernel,
+        [(7, HALF, NZ), (18, HALF, NZ)],
+        chip, *x_got, my, p0, scratch=[(4, 7, HALF, NZ)], name="chips",
     )
     z_got = [swap(group, "gx", 8 * i) for i in (1, 2, 3)]
-    gz, hz, port = call(
-        z_ports_kernel,
-        [(NY, NX, NZ), (NY, NX, NZ), (8, ROWS)],
-        k, group, scratch=[(2, ROWS, NZ)], name="z_ports",
+    g1, h1, p1, f1 = call(
+        functools.partial(z_ports_kernel, HALF), z_shapes, k, group, scratch=[(2, ROWS // 2, NZ)], name="z_ports"
     )
     keep, send = call(
         back_kernel,
         [(2, HALF, NZ), (2, HALF, NZ)],
-        group, *z_got, chip_parts, core_parts,
+        group, *z_got, chip_parts, core_parts, p1,
         scratch=[(4, 7, HALF, NZ), (8, HALF, NZ)], name="back",
     )
     got = swap(send, "gx", 1)
     v, message = call(
         y_kernel,
         [(NY, NX, NZ), (8, ROWS)],
-        keep, got, base, gx, hx, my, iy, gz, hz, port,
+        keep, got, base, gx, hx, my, iy, g0, g1, h0, h1, p0, p1,
         scratch=[(2, NY, NZ), (ROWS, NZ), (2, ROWS, NZ)], name="y_solve",
     )
     l_got = [swap(message, "gz", i) for i in (1, 2, 3)]
-    yz, = call(z_local_kernel, [(NY, NX, NZ)], k, v, name="z_local")
+    yz, = call(z_local_kernel, [(NY, NX, NZ)], f0, f1, v, name="z_local")
     out, = call(
         final_kernel,
         [(NX, NY, NZ)],
-        message, *l_got, yz, gz, hz, u,
-        scratch=[(4, 8, ROWS), (8, ROWS), (2, ROWS, NZ)], name="final",
+        message, *l_got, yz, g0, g1, h0, h1, u,
+        scratch=[(4, 8, ROWS), (2, ROWS, NZ), (NX, NY, NZ)], sems=NY // CHUNK,
+        outs_in=pltpu.HBM, name="final",
     )
     return out
 

time: 52.5 us -> 47.7 us (0.909)
  waiting for transfers between devices: 17.9 us -> 14.7 us
  local copies, waits for them, and re-layouts: 2.58 us -> 0 us
  Pallas kernels: 12.6 us -> 13.6 us
    ppermute x13, waiting for transfers between devices: 17.9 us -> 14.7 us  [swap(): return lax.ppermute(block, axis, [(i, i ^ mask) for i in range(n)])]
    unnamed x10 -> x0, local copies, waits for them, and re-layouts: 2.58 us -> none
    pallas_call x11 -> x12, Pallas kernels: 12.6 us -> 13.6 us  [call(): pl.pallas_call(kernel, out_shape=shapes, in_specs=[pl.BlockSpec(memory_sp...]
  transfers between devices with their start and end apart: 13 -> 13, of which waited for: 7 -> 8; matrix products, arithmetic and copies ran while one was open for 0% -> 0% of each run, Pallas kernels for 17% -> 18%
where the time goes in v2:
time: 47.7 us; the launch traced here: 47.6 us
  starting transfers between devices  19.2 us (40%)
  waiting for transfers between devices  14.7 us (31%)
  Pallas kernels  13.6 us (29%)
    ppermute x13, starting transfers between devices, swap(): return lax.ppermute(block, axis, [(i, i ^ mask) for i in range(n)])  19.2 us
    ppermute x13, waiting for transfers between devices, swap(): return lax.ppermute(block, axis, [(i, i ^ mask) for i in range(n)])  14.7 us
    pallas_call x12, Pallas kernels, call(): pl.pallas_call(kernel, out_shape=shapes, in_specs=[pl.BlockSpec(memory_sp...  13.6 us
  transfers between devices with their start and end apart: 13, of which 8 were waited for; matrix products, arithmetic and copies ran while one was open for 0% of the time, Pallas kernels for 18%

profile of v2, /device:TPU:0, one launch (start us, length us, event | category | flops | bytes accessed | tf_op | source)
XLA Modules:
  0.0 47.6 jit_solution(12601443029320806802)
XLA Ops:
  0.0 1.6 %edges.1 = (f32[8,64,128]{2,1,0:T(8,128)S(1)}, f32[8,64,128]{2,1,0:T(8,128)S(1)}, f32[8,64,128]{2,1,0:T(8,128)S(1)}, f32[8,512]{1,0:T(8,128)S(1)}) custom-call(f32[8,64,128]{2,1,0:T(8,128)} %u_hbm.1, f32[8,64,128]{2,1,0:T(8,128)} %k_hbm.1, f32[8,64,128]{2,1,0:T(8,128)} %f_hbm.1), custom_call_target="tpu_custom_call" | custom-call | bytes 1589248 | tf_op jit(solution)/shard_map/edges/pallas_call | solution.py:24
  1.6 1.7 %collective-permute-start = (f32[8,512]{1,0:T(8,128)S(1)}, f32[8,512]{1,0:T(8,128)S(1)}, u32[]{:S(2)}, u32[]{:S(2)}) collective-permute-start(f32[8,512]{1,0:T(8,128)S(1)} %get-tuple-element.38.own_ref), channel_id=1, source_target_pairs={{0,1},{1,0},{2,3},{3,2},{4,5},{5,4},{6,7},{7,6},{8,9},{9,8},{10,11... | collective-permute-start | bytes 49160 | tf_op jit(solution)/shard_map/ppermute | solution.py:432
  3.3 2.2 %collective-permute-start.1 = (f32[8,512]{1,0:T(8,128)S(1)}, f32[8,512]{1,0:T(8,128)S(1)}, u32[]{:S(2)}, u32[]{:S(2)}) collective-permute-start(f32[8,512]{1,0:T(8,128)S(1)} %get-tuple-element.38.own_ref), channel_id=1, source_target_pairs={{0,3},{1,2},{2,1},{3,0},{4,7},{5,6},{6,5},{7,4},{8,11},{9,10},{10,... | collective-permute-start | bytes 49160 | tf_op jit(solution)/shard_map/ppermute | solution.py:432
  5.5 0.5 %local.1 = (f32[8,64,128]{2,1,0:T(8,128)S(1)}, f32[6,64,128]{2,1,0:T(8,128)S(1)}, f32[6,64,128]{2,1,0:T(8,128)S(1)}, f32[6,64,128]{2,1,0:T(8,128)S(1)}, f32[3,64,128]{2,1,0:T(8,128)S(1)}) custom-call(f32[8,64,128]{2,1,0:T(8,128)S(1)} %get-tuple-element.39.u_ref, f32[8,64,128]{2,1,0:T(8,128)S(1)} %get-tuple-element.40.k_ref, ...), custom_call_target="tpu_custom_call" | custom-call | bytes 1736704 | tf_op jit(solution)/shard_map/local/pallas_call | solution.py:24
  6.1 2.2 %collective-permute-done.1.two_ref = f32[8,512]{1,0:T(8,128)S(1)} collective-permute-done((f32[8,512]{1,0:T(8,128)S(1)}, f32[8,512]{1,0:T(8,128)S(1)}, u32[]{:S(2)}, u32[]{:S(2)}) %collective-permute-start.1) | collective-permute-done | bytes 16416 | tf_op jit(solution)/shard_map/ppermute | solution.py:432
  8.3 0.5 %halo.1 = (f32[7,32,128]{2,1,0:T(8,128)S(1)}, f32[7,32,128]{2,1,0:T(8,128)S(1)}, f32[6,64,128]{2,1,0:T(8,128)S(1)}) custom-call(f32[8,512]{1,0:T(8,128)S(1)} %get-tuple-element.38.own_ref, f32[8,512]{1,0:T(8,128)S(1)} %collective-permute-done.one_ref, f32[8,512]{1,0:T(8,128)S(1)} %collective-permute-done.1.two_ref, ...), custom_call_target="tpu_custom_call" | custom-call | bytes 1490944 | tf_op jit(solution)/shard_map/halo/pallas_call | solution.py:24
  8.8 0.1 collective-permute-start.2
  8.9 1.3 %collective-permute-done.2.got_ref = f32[7,32,128]{2,1,0:T(8,128)S(1)} collective-permute-done((f32[7,32,128]{2,1,0:T(8,128)S(1)}, f32[7,32,128]{2,1,0:T(8,128)S(1)}, u32[]{:S(2)}, u32[]{:S(2)}) %collective-permute-start.2) | collective-permute-done | bytes 114720 | tf_op jit(solution)/shard_map/ppermute | solution.py:432
  10.2 1.6 %collective-permute-start.3 = (f32[7,32,128]{2,1,0:T(8,128)S(1)}, f32[7,32,128]{2,1,0:T(8,128)S(1)}, u32[]{:S(2)}, u32[]{:S(2)}) collective-permute-start(f32[7,32,128]{2,1,0:T(8,128)S(1)} %get-tuple-element.48.after_ref.own_ref), channel_id=1, source_target_pairs={{0,8},{4,12},{8,0},{12,4},{16,24},{20,28},{24,16},{28,20},{32,40},... | collective-permute-start | bytes 344072 | tf_op jit(solution)/shard_map/ppermute | solution.py:432
  11.8 2.7 %collective-permute-start.4 = (f32[7,32,128]{2,1,0:T(8,128)S(1)}, f32[7,32,128]{2,1,0:T(8,128)S(1)}, u32[]{:S(2)}, u32[]{:S(2)}) collective-permute-start(f32[7,32,128]{2,1,0:T(8,128)S(1)} %get-tuple-element.48.after_ref.own_ref), channel_id=1, source_target_pairs={{0,16},{4,20},{8,24},{12,28},{16,0},{20,4},{24,8},{28,12},{32,48},... | collective-permute-start | bytes 344072 | tf_op jit(solution)/shard_map/ppermute | solution.py:432
  14.5 0.5 %collective-permute-start.5 = (f32[7,32,128]{2,1,0:T(8,128)S(1)}, f32[7,32,128]{2,1,0:T(8,128)S(1)}, u32[]{:S(2)}, u32[]{:S(2)}) collective-permute-start(f32[7,32,128]{2,1,0:T(8,128)S(1)} %get-tuple-element.48.after_ref.own_ref), channel_id=1, source_target_pairs={{0,24},{4,28},{8,16},{12,20},{16,8},{20,12},{24,0},{28,4},{32,56},... | collective-permute-start | bytes 344072 | tf_op jit(solution)/shard_map/ppermute | solution.py:432
  15.0 0.4 prepare.1
  15.4 2.7 %z_ports.2 = (f32[32,8,128]{2,1,0:T(8,128)S(1)}, f32[32,8,128]{2,1,0:T(8,128)S(1)}, f32[8,256]{1,0:T(8,128)S(1)}, f32[22,256,128]{2,1,0:T(8,128)S(1)}) custom-call(f32[8,64,128]{2,1,0:T(8,128)S(1)} %get-tuple-element.40.k_ref, f32[7,32,128]{2,1,0:T(8,128)S(1)} %get-tuple-element.48.after_ref.own_ref), custom_call_target="tpu_custom_call" | custom-call | bytes 3530752 | tf_op jit(solution)/shard_map/z_ports/pallas_call | solution.py:24
  18.1 0.0 collective-permute-done.3.one_ref
  18.1 2.2 %collective-permute-done.4.two_ref = f32[7,32,128]{2,1,0:T(8,128)S(1)} collective-permute-done((f32[7,32,128]{2,1,0:T(8,128)S(1)}, f32[7,32,128]{2,1,0:T(8,128)S(1)}, u32[]{:S(2)}, u32[]{:S(2)}) %collective-permute-start.4) | collective-permute-done | bytes 114720 | tf_op jit(solution)/shard_map/ppermute | solution.py:432
  20.3 2.1 %collective-permute-done.5.three_ref = f32[7,32,128]{2,1,0:T(8,128)S(1)} collective-permute-done((f32[7,32,128]{2,1,0:T(8,128)S(1)}, f32[7,32,128]{2,1,0:T(8,128)S(1)}, u32[]{:S(2)}, u32[]{:S(2)}) %collective-permute-start.5) | collective-permute-done | bytes 114720 | tf_op jit(solution)/shard_map/ppermute | solution.py:432
  22.3 0.1 chips.1
  22.5 2.0 %collective-permute-start.6 = (f32[7,32,128]{2,1,0:T(8,128)S(1)}, f32[7,32,128]{2,1,0:T(8,128)S(1)}, u32[]{:S(2)}, u32[]{:S(2)}) collective-permute-start(f32[7,32,128]{2,1,0:T(8,128)S(1)} %get-tuple-element.53.after_ref.own_ref), channel_id=1, source_target_pairs={{0,32},{4,36},{8,40},{12,44},{16,48},{20,52},{24,56},{28,60},{32,0... | collective-permute-start | bytes 344072 | tf_op jit(solution)/shard_map/ppermute | solution.py:432
  24.5 3.6 %collective-permute-start.7 = (f32[7,32,128]{2,1,0:T(8,128)S(1)}, f32[7,32,128]{2,1,0:T(8,128)S(1)}, u32[]{:S(2)}, u32[]{:S(2)}) collective-permute-start(f32[7,32,128]{2,1,0:T(8,128)S(1)} %get-tuple-element.53.after_ref.own_ref), channel_id=1, source_target_pairs={{0,64},{4,68},{8,72},{12,76},{16,80},{20,84},{24,88},{28,92},{32,9... | collective-permute-start | bytes 344072 | tf_op jit(solution)/shard_map/ppermute | solution.py:432
  28.1 2.7 %z_ports.3 = (f32[32,8,128]{2,1,0:T(8,128)S(1)}, f32[32,8,128]{2,1,0:T(8,128)S(1)}, f32[8,256]{1,0:T(8,128)S(1)}, f32[22,256,128]{2,1,0:T(8,128)S(1)}) custom-call(f32[8,64,128]{2,1,0:T(8,128)S(1)} %get-tuple-element.40.k_ref, f32[7,32,128]{2,1,0:T(8,128)S(1)} %get-tuple-element.53.after_ref.own_ref), custom_call_target="tpu_custom_call" | custom-call | bytes 3530752 | tf_op jit(solution)/shard_map/z_ports/pallas_call | solution.py:24
  30.8 2.6 %collective-permute-done.7.two_ref = f32[7,32,128]{2,1,0:T(8,128)S(1)} collective-permute-done((f32[7,32,128]{2,1,0:T(8,128)S(1)}, f32[7,32,128]{2,1,0:T(8,128)S(1)}, u32[]{:S(2)}, u32[]{:S(2)}) %collective-permute-start.7) | collective-permute-done | bytes 114720 | tf_op jit(solution)/shard_map/ppermute | solution.py:432
  33.3 1.8 %collective-permute-done.8.three_ref = f32[7,32,128]{2,1,0:T(8,128)S(1)} collective-permute-done((f32[7,32,128]{2,1,0:T(8,128)S(1)}, f32[7,32,128]{2,1,0:T(8,128)S(1)}, u32[]{:S(2)}, u32[]{:S(2)}) %collective-permute-start.8) | collective-permute-done | bytes 114720 | tf_op jit(solution)/shard_map/ppermute | solution.py:432
  35.1 0.2 back.1
  35.3 0.1 collective-permute-start.9
  35.4 1.2 %collective-permute-done.9.got_ref = f32[2,32,128]{2,1,0:T(8,128)S(1)} collective-permute-done((f32[2,32,128]{2,1,0:T(8,128)S(1)}, f32[2,32,128]{2,1,0:T(8,128)S(1)}, u32[]{:S(2)}, u32[]{:S(2)}) %collective-permute-start.9) | collective-permute-done | bytes 32800 | tf_op jit(solution)/shard_map/ppermute | solution.py:432
  36.6 0.8 %y_solve.1 = (f32[64,8,128]{2,1,0:T(8,128)S(1)}, f32[8,512]{1,0:T(8,128)S(1)}) custom-call(f32[2,32,128]{2,1,0:T(8,128)S(1)} %get-tuple-element.57.keep_ref, f32[2,32,128]{2,1,0:T(8,128)S(1)} %collective-permute-done.9.got_ref, f32[8,64,128]{2,1,0:T(8,128)S(1)} %get-tuple-element.59.base_ref, f32[6,64,128]{2,1,0:T(8,128)S(1)} %get-tuple-element.60.gx_ref, ...), custom_call_target="tpu_custom_call" | custom-call | bytes 2064384 | tf_op jit(solution)/shard_map/y_solve/pallas_call | solution.py:24
  37.4 3.7 %collective-permute-start.11 = (f32[8,512]{1,0:T(8,128)S(1)}, f32[8,512]{1,0:T(8,128)S(1)}, u32[]{:S(2)}, u32[]{:S(2)}) collective-permute-start(f32[8,512]{1,0:T(8,128)S(1)} %get-tuple-element.67.own_ref), channel_id=1, source_target_pairs={{0,2},{1,3},{2,0},{3,1},{4,6},{5,7},{6,4},{7,5},{8,10},{9,11},{10,... | collective-permute-start | bytes 49160 | tf_op jit(solution)/shard_map/ppermute | solution.py:432
  41.1 1.1 %collective-permute-start.12 = (f32[8,512]{1,0:T(8,128)S(1)}, f32[8,512]{1,0:T(8,128)S(1)}, u32[]{:S(2)}, u32[]{:S(2)}) collective-permute-start(f32[8,512]{1,0:T(8,128)S(1)} %get-tuple-element.67.own_ref), channel_id=1, source_target_pairs={{0,3},{1,2},{2,1},{3,0},{4,7},{5,6},{6,5},{7,4},{8,11},{9,10},{10,... | collective-permute-start | bytes 49160 | tf_op jit(solution)/shard_map/ppermute | solution.py:432
  42.1 2.4 %z_local.1.y_ref = f32[64,8,128]{2,1,0:T(8,128)S(1)} custom-call(f32[22,256,128]{2,1,0:T(8,128)S(1)} %get-tuple-element.68.f0_ref, f32[22,256,128]{2,1,0:T(8,128)S(1)} %get-tuple-element.69.f1_ref, f32[64,8,128]{2,1,0:T(8,128)S(1)} %get-tuple-element.70.v_ref), custom_call_target="tpu_custom_call" | custom-call | bytes 6291456 | tf_op jit(solution)/shard_map/z_local/pallas_call | solution.py:24
  44.6 0.0 collective-permute-done.11.two_ref
  44.6 1.4 %collective-permute-done.12.three_ref = f32[8,512]{1,0:T(8,128)S(1)} collective-permute-done((f32[8,512]{1,0:T(8,128)S(1)}, f32[8,512]{1,0:T(8,128)S(1)}, u32[]{:S(2)}, u32[]{:S(2)}) %collective-permute-start.12) | collective-permute-done | bytes 16416 | tf_op jit(solution)/shard_map/ppermute | solution.py:432
  46.0 1.6 %final.1 = f32[8,64,128]{2,1,0:T(8,128)} custom-call(f32[8,512]{1,0:T(8,128)S(1)} %get-tuple-element.67.own_ref, f32[8,512]{1,0:T(8,128)S(1)} %collective-permute-done.10.one_ref, f32[8,512]{1,0:T(8,128)S(1)} %collective-permute-done.11.two_ref, f32[8,512]{1,0:T(8,128)S(1)} %collective-permute-done.12.three_ref, f32[64,8,128]{2,1,0:T(8,128)S(1)} %z_local.1.y_ref, ...), custom_call_target="tpu_custom_call" | custom-call | bytes 1376256 | tf_op jit(solution)/shard_map/final/pallas_call | solution.py:24
  (6 shorter events, 0.1 us)
Async XLA Ops:
  1.6 4.5 %collective-permute-start = (f32[8,512]{1,0:T(8,128)S(1)}, f32[8,512]{1,0:T(8,128)S(1)}, u32[]{:S(2)}, u32[]{:S(2)}) collective-permute-start(f32[8,512]{1,0:T(8,128)S(1)} %get-tuple-element.38.own_ref), channel_id=1, source_target_pairs={{0,1},{1,0},{2,3},{3,2},{4,5},{5,4},{6,7},{7,6},{8,9},{9,8},{10,11... | collective-permute-start | bytes 49160 | tf_op jit(solution)/shard_map/ppermute | solution.py:432
  3.3 4.9 %collective-permute-start.1 = (f32[8,512]{1,0:T(8,128)S(1)}, f32[8,512]{1,0:T(8,128)S(1)}, u32[]{:S(2)}, u32[]{:S(2)}) collective-permute-start(f32[8,512]{1,0:T(8,128)S(1)} %get-tuple-element.38.own_ref), channel_id=1, source_target_pairs={{0,3},{1,2},{2,1},{3,0},{4,7},{5,6},{6,5},{7,4},{8,11},{9,10},{10,... | collective-permute-start | bytes 49160 | tf_op jit(solution)/shard_map/ppermute | solution.py:432
  8.8 1.4 %collective-permute-start.2 = (f32[7,32,128]{2,1,0:T(8,128)S(1)}, f32[7,32,128]{2,1,0:T(8,128)S(1)}, u32[]{:S(2)}, u32[]{:S(2)}) collective-permute-start(f32[7,32,128]{2,1,0:T(8,128)S(1)} %get-tuple-element.47), channel_id=1, source_target_pairs={{0,4},{4,0},{8,12},{12,8},{16,20},{20,16},{24,28},{28,24},{32,36},... | collective-permute-start | bytes 344072 | tf_op jit(solution)/shard_map/ppermute | solution.py:432
  10.2 7.9 %collective-permute-start.3 = (f32[7,32,128]{2,1,0:T(8,128)S(1)}, f32[7,32,128]{2,1,0:T(8,128)S(1)}, u32[]{:S(2)}, u32[]{:S(2)}) collective-permute-start(f32[7,32,128]{2,1,0:T(8,128)S(1)} %get-tuple-element.48.after_ref.own_ref), channel_id=1, source_target_pairs={{0,8},{4,12},{8,0},{12,4},{16,24},{20,28},{24,16},{28,20},{32,40},... | collective-permute-start | bytes 344072 | tf_op jit(solution)/shard_map/ppermute | solution.py:432
  11.8 8.5 %collective-permute-start.4 = (f32[7,32,128]{2,1,0:T(8,128)S(1)}, f32[7,32,128]{2,1,0:T(8,128)S(1)}, u32[]{:S(2)}, u32[]{:S(2)}) collective-permute-start(f32[7,32,128]{2,1,0:T(8,128)S(1)} %get-tuple-element.48.after_ref.own_ref), channel_id=1, source_target_pairs={{0,16},{4,20},{8,24},{12,28},{16,0},{20,4},{24,8},{28,12},{32,48},... | collective-permute-start | bytes 344072 | tf_op jit(solution)/shard_map/ppermute | solution.py:432
  14.5 7.8 %collective-permute-start.5 = (f32[7,32,128]{2,1,0:T(8,128)S(1)}, f32[7,32,128]{2,1,0:T(8,128)S(1)}, u32[]{:S(2)}, u32[]{:S(2)}) collective-permute-start(f32[7,32,128]{2,1,0:T(8,128)S(1)} %get-tuple-element.48.after_ref.own_ref), channel_id=1, source_target_pairs={{0,24},{4,28},{8,16},{12,20},{16,8},{20,12},{24,0},{28,4},{32,56},... | collective-permute-start | bytes 344072 | tf_op jit(solution)/shard_map/ppermute | solution.py:432
  22.5 8.3 %collective-permute-start.6 = (f32[7,32,128]{2,1,0:T(8,128)S(1)}, f32[7,32,128]{2,1,0:T(8,128)S(1)}, u32[]{:S(2)}, u32[]{:S(2)}) collective-permute-start(f32[7,32,128]{2,1,0:T(8,128)S(1)} %get-tuple-element.53.after_ref.own_ref), channel_id=1, source_target_pairs={{0,32},{4,36},{8,40},{12,44},{16,48},{20,52},{24,56},{28,60},{32,0... | collective-permute-start | bytes 344072 | tf_op jit(solution)/shard_map/ppermute | solution.py:432
  24.5 8.9 %collective-permute-start.7 = (f32[7,32,128]{2,1,0:T(8,128)S(1)}, f32[7,32,128]{2,1,0:T(8,128)S(1)}, u32[]{:S(2)}, u32[]{:S(2)}) collective-permute-start(f32[7,32,128]{2,1,0:T(8,128)S(1)} %get-tuple-element.53.after_ref.own_ref), channel_id=1, source_target_pairs={{0,64},{4,68},{8,72},{12,76},{16,80},{20,84},{24,88},{28,92},{32,9... | collective-permute-start | bytes 344072 | tf_op jit(solution)/shard_map/ppermute | solution.py:432
  28.1 7.1 %collective-permute-start.8 = (f32[7,32,128]{2,1,0:T(8,128)S(1)}, f32[7,32,128]{2,1,0:T(8,128)S(1)}, u32[]{:S(2)}, u32[]{:S(2)}) collective-permute-start(f32[7,32,128]{2,1,0:T(8,128)S(1)} %get-tuple-element.53.after_ref.own_ref), channel_id=1, source_target_pairs={{0,96},{4,100},{8,104},{12,108},{16,112},{20,116},{24,120},{28,124... | collective-permute-start | bytes 344072 | tf_op jit(solution)/shard_map/ppermute | solution.py:432
  35.3 1.3 %collective-permute-start.9 = (f32[2,32,128]{2,1,0:T(8,128)S(1)}, f32[2,32,128]{2,1,0:T(8,128)S(1)}, u32[]{:S(2)}, u32[]{:S(2)}) collective-permute-start(f32[2,32,128]{2,1,0:T(8,128)S(1)} %get-tuple-element.58), channel_id=1, source_target_pairs={{0,4},{4,0},{8,12},{12,8},{16,20},{20,16},{24,28},{28,24},{32,36},... | collective-permute-start | bytes 98312 | tf_op jit(solution)/shard_map/ppermute | solution.py:432
  37.4 7.2 %collective-permute-start.10 = (f32[8,512]{1,0:T(8,128)S(1)}, f32[8,512]{1,0:T(8,128)S(1)}, u32[]{:S(2)}, u32[]{:S(2)}) collective-permute-start(f32[8,512]{1,0:T(8,128)S(1)} %get-tuple-element.67.own_ref), channel_id=1, source_target_pairs={{0,1},{1,0},{2,3},{3,2},{4,5},{5,4},{6,7},{7,6},{8,9},{9,8},{10,11... | collective-permute-start | bytes 49160 | tf_op jit(solution)/shard_map/ppermute | solution.py:432
  37.4 7.2 %collective-permute-start.11 = (f32[8,512]{1,0:T(8,128)S(1)}, f32[8,512]{1,0:T(8,128)S(1)}, u32[]{:S(2)}, u32[]{:S(2)}) collective-permute-start(f32[8,512]{1,0:T(8,128)S(1)} %get-tuple-element.67.own_ref), channel_id=1, source_target_pairs={{0,2},{1,3},{2,0},{3,1},{4,6},{5,7},{6,4},{7,5},{8,10},{9,11},{10,... | collective-permute-start | bytes 49160 | tf_op jit(solution)/shard_map/ppermute | solution.py:432
  41.1 4.9 %collective-permute-start.12 = (f32[8,512]{1,0:T(8,128)S(1)}, f32[8,512]{1,0:T(8,128)S(1)}, u32[]{:S(2)}, u32[]{:S(2)}) collective-permute-start(f32[8,512]{1,0:T(8,128)S(1)} %get-tuple-element.67.own_ref), channel_id=1, source_target_pairs={{0,3},{1,2},{2,1},{3,0},{4,7},{5,6},{6,5},{7,4},{8,11},{9,10},{10,... | collective-permute-start | bytes 49160 | tf_op jit(solution)/shard_map/ppermute | solution.py:432

commit v3 on v2

v3 whole, which is shorter than its diff:
```python
import functools

import jax
import jax.numpy as jnp
from jax import lax
from jax.experimental import pallas as pl
from jax.experimental.pallas import tpu as pltpu
from jax.sharding import PartitionSpec as P

NX, NY, NZ = 8, 64, 128
ROWS = NX * NY
HALF = NY // 2
CX = 0.25 * 16.0 * NX * NX
CY = 0.25 * 2.0
CZ = 0.25 * 0.5 * NZ * NZ
F32 = jnp.float32
VMEM_LIMIT = 24 * 1024 * 1024
BF16 = jnp.bfloat16


def call(kernel, outs, *args, scratch=(), sems=0, ins_in=pltpu.VMEM, outs_in=pltpu.VMEM, flops=0, name=None):
    shapes = [jax.ShapeDtypeStruct(s, F32) for s in outs]
    nbytes = sum(4 * a.size for a in args) + sum(4 * s.size for s in shapes)
    return pl.pallas_call(
        kernel,
        out_shape=shapes,
        in_specs=[pl.BlockSpec(memory_space=ins_in) for _ in args],
        out_specs=[pl.BlockSpec(memory_space=outs_in) for _ in outs],
        scratch_shapes=[pltpu.VMEM(s, F32) for s in scratch]
        + [pltpu.SemaphoreType.DMA] * sems,
        compiler_params=pltpu.CompilerParams(vmem_limit_bytes=VMEM_LIMIT),
        cost_estimate=pl.CostEstimate(flops=flops, bytes_accessed=nbytes, transcendentals=0),
        name=name,
    )(*args)


def pieces(x):
    high = x.astype(BF16).astype(F32)
    rest = x - high
    middle = rest.astype(BF16).astype(F32)
    return high, middle, rest - middle


def lanes_to_rows(entries, block):
    high, middle, low = (p.astype(BF16) for p in pieces(block))
    select = selector(entries, 16, NZ).astype(BF16)
    dims = (((1,), (1,)), ((), ()))
    return lax.dot_general(
        jnp.concatenate([select, select], axis=1),
        jnp.concatenate([high, middle], axis=1),
        dims,
        preferred_element_type=F32,
    ) + lax.dot_general(select, low, dims, preferred_element_type=F32)


def rows_to_lanes(entries, rows, lanes):
    both = jnp.concatenate(pieces(rows) + (jnp.zeros_like(rows),), axis=0).astype(BF16)
    select = selector([(r + 8 * i, l) for i in range(3) for r, l in entries], 32, lanes)
    return lax.dot_general(
        both, select.astype(BF16), (((0,), (0,)), ((), ())), preferred_element_type=F32
    )


def selector(entries, rows, lanes):
    row = lax.broadcasted_iota(jnp.int32, (rows, lanes), 0)
    lane = lax.broadcasted_iota(jnp.int32, (rows, lanes), 1)
    hit = None
    for r, l in entries:
        one = row == r
        if isinstance(l, range):
            one = one & (lane >= l.start) & (lane < l.stop)
        elif l is not None:
            one = one & (lane == l)
        hit = one if hit is None else (hit | one)
    return jnp.where(hit, 1.0, 0.0).astype(F32)


def reduce_chain(e, c, r):
    n = len(e)
    e_h, r_h = e[0], r[0]
    s, w, rr = e[1], c[0], r[1]
    parts = []
    for j in range(1, n - 1):
        inv = 1.0 / (s + w + c[j])
        a, m = w * inv, c[j] * inv
        parts.append((a, m, rr * inv))
        e_h = e_h + a * s
        r_h = r_h + a * rr
        s = e[j + 1] + m * s
        rr = r[j + 1] + m * rr
        w = m * w
    return (e_h, s, w, r_h, rr), parts


def expand_chain(first, last, parts):
    values = [last]
    for a, m, q in reversed(parts):
        values.append(q + a * first + m * values[-1])
    values.append(first)
    return values[::-1]


def solve_chain(e, c, r):
    n = len(e)
    mid = n // 2
    low, high = [], []
    s, rr = e[0], r[0]
    t, tt = e[n - 1], r[n - 1]
    for j in range(mid):
        inv = 1.0 / (s + c[j])
        m = c[j] * inv
        low.append((m, rr * inv))
        s, rr = e[j + 1] + m * s, r[j + 1] + m * rr
        i = n - 1 - j
        if i > mid:
            inv = 1.0 / (t + c[i - 1])
            m = c[i - 1] * inv
            high.append((m, tt * inv))
            t, tt = m * t, m * tt
            if i - 1 > mid:
                t, tt = e[i - 1] + t, r[i - 1] + tt
    values = [None] * n
    values[mid] = (rr + tt) / (s + t)
    for j in range(mid - 1, -1, -1):
        m, q = low[j]
        values[j] = q + m * values[j + 1]
    for i in range(mid + 1, n):
        m, q = high[n - 1 - i]
        values[i] = q + m * values[i - 1]
    return values


def join(blocks):
    e = [blocks[0][0]]
    r = [blocks[0][3]]
    for i, b in enumerate(blocks):
        e.append(b[1] + blocks[i + 1][0] if i + 1 < len(blocks) else b[1])
        r.append(b[4] + blocks[i + 1][3] if i + 1 < len(blocks) else b[4])
    return e, [b[2] for b in blocks], r


def edges_kernel(u_hbm, k_hbm, f_hbm, u_ref, k_ref, f_ref, out_ref, end_ref, *sems):
    pairs = ((k_hbm, k_ref), (u_hbm, u_ref), (f_hbm, f_ref))
    copies = [pltpu.make_async_copy(a, b, sem) for (a, b), sem in zip(pairs, sems)]
    for copy in copies:
        copy.start()
    lane = lax.broadcasted_iota(jnp.int32, (ROWS, NZ), 1)
    copies[0].wait()
    k = pltpu.roll(k_ref[...].reshape(ROWS, NZ), 2, 1)
    copies[1].wait()
    both = jnp.where((lane == 1) | (lane == 2), k, u_ref[...].reshape(ROWS, NZ))
    out_ref[...] = lanes_to_rows([(0, 0), (1, NZ - 1), (2, 2), (3, 1)], both)[:8]
    end_ref[...] = k_ref[NX - 1]
    copies[2].wait()


def local_kernel(u_ref, k_ref, f_ref, rp_ref, a_ref, m_ref, inv_ref, ew_ref):
    row = lax.broadcasted_iota(jnp.int32, (NY, NZ), 0)
    lane = lax.broadcasted_iota(jnp.int32, (NY, NZ), 1)
    for x in range(NX):
        u, k = u_ref[x], k_ref[x]
        flux_y = (CY * (k + pltpu.roll(k, NY - 1, 0))) * (pltpu.roll(u, NY - 1, 0) - u)
        flux_y = jnp.where(row == NY - 1, -(CY * k) * u, flux_y)
        low_y = jnp.where(row == 0, (CY * k) * u, pltpu.roll(flux_y, 1, 0))
        flux_z = (CZ * (k + pltpu.roll(k, NZ - 1, 1))) * (pltpu.roll(u, NZ - 1, 1) - u)
        flux_z = jnp.where(lane == NZ - 1, 0.0, flux_z)
        low_z = pltpu.roll(flux_z, 1, 1)
        rp_ref[x] = u + (flux_y - low_y) + (flux_z - low_z) + 0.5 * f_ref[x]
    s = jnp.ones((NY, NZ), F32)
    e_h = s
    w = CX * (k_ref[0] + k_ref[1])
    for j in range(1, NX - 1):
        c = CX * (k_ref[j] + k_ref[j + 1])
        inv = 1.0 / (s + w + c)
        a, m = w * inv, c * inv
        inv_ref[j - 1], a_ref[j - 1], m_ref[j - 1] = inv, a, m
        e_h = e_h + a * s
        s = 1.0 + m * s
        w = m * w
    ew_ref[0], ew_ref[1], ew_ref[2] = e_h, s, w


def halo_kernel(own_ref, one_ref, two_ref, below_ref, rp_ref, a_ref, m_ref, ew_ref, k_ref, keep_ref, send_ref, rr_ref, fix_ref):
    g = lax.axis_index("gz")
    index = lax.axis_index("gx")
    core = lax.rem(index, 2)
    odd = lax.rem(g, 2) == 1
    own, one, two = own_ref[...], one_ref[...], two_ref[...]
    low = jnp.where(odd, one, two) * jnp.where(g > 0, 1.0, 0.0)
    high = jnp.where(odd, two, one) * jnp.where(g < 3, 1.0, 0.0)
    at_low = CZ * (low[3:4] + own[2:3]) * (low[1:2] - own[0:1])
    at_high = CZ * (high[2:3] + own[3:4]) * (high[0:1] - own[1:2])
    row = lax.broadcasted_iota(jnp.int32, (8, ROWS), 0)
    both = jnp.where(row == 0, at_low, jnp.where(row == 1, at_high, 0.0))
    fix_ref[...] = rows_to_lanes([(0, 0), (1, NZ - 1)], both, NZ).reshape(NX, NY, NZ)
    top = jnp.where(index == lax.axis_size("gx") - 1, CX, 0.0)
    inner = jnp.where(core == 0, NX - 1, 0)
    for which, out in ((core, keep_ref), (1 - core, send_ref)):
        ys = pl.ds(pl.multiple_of(which * HALF, HALF), HALF)
        r_h = rp_ref[0, ys] + fix_ref[0, ys]
        rr = rp_ref[1, ys] + fix_ref[1, ys]
        for j in range(1, NX - 1):
            rr_ref[j - 1, ys] = rr
            r_h = r_h + a_ref[j - 1, ys] * rr
            rr = (rp_ref[j + 1, ys] + fix_ref[j + 1, ys]) + m_ref[j - 1, ys] * rr
        out[0], out[2] = ew_ref[0, ys], ew_ref[2, ys]
        out[1] = ew_ref[1, ys] + top * k_ref[NX - 1, ys]
        out[3], out[4] = r_h, rr
        out[5] = k_ref[inner, ys]
        out[6] = CX * (below_ref[ys] + k_ref[0, ys])


def core_kernel(own_ref, got_ref, out_ref, parts_ref):
    first = lax.rem(lax.axis_index("gx"), 2) == 0
    low = [jnp.where(first, own_ref[i], got_ref[i]) for i in range(7)]
    high = [jnp.where(first, got_ref[i], own_ref[i]) for i in range(6)]
    e = [0.0, low[0], low[1], high[0], high[1]]
    c = [low[6], low[2], CX * (low[5] + high[5]), high[2]]
    r = [0.0, low[3], low[4], high[3], high[4]]
    port, parts = reduce_chain(e, c, r)
    for i, v in enumerate(port):
        out_ref[i] = v
    for j, p in enumerate(parts):
        for i in range(3):
            parts_ref[3 * j + i] = p[i]


def ordered(me, refs, held):
    for i, ref in enumerate(refs):
        held[jnp.bitwise_xor(me, i)] = ref[...]
    return held


def chips_kernel(own_ref, one_ref, two_ref, three_ref, after_ref, also_ref, out_ref, parts_ref, held):
    del after_ref, also_ref
    me = lax.rem(lax.axis_index("gx") // 2, 4)
    ordered(me, (own_ref, one_ref, two_ref, three_ref), held)
    blocks = [[held[b, i] for i in range(5)] for b in range(4)]
    port, parts = reduce_chain(*join(blocks))
    for i, v in enumerate(port):
        out_ref[i] = v
    for j, p in enumerate(parts):
        for i in range(3):
            parts_ref[3 * j + i] = p[i]


def back_kernel(own_ref, one_ref, two_ref, three_ref, chips_ref, cores_ref, after_ref, keep_ref, send_ref, held, nodes):
    del after_ref
    index = lax.axis_index("gx")
    core, x, z = lax.rem(index, 2), lax.rem(index // 2, 4), index // 8
    ordered(z, (own_ref, one_ref, two_ref, three_ref), held)
    blocks = [[held[b, i] for i in range(5)] for b in range(4)]
    e, c, r = join(blocks)
    e[1] = e[1] + c[0]
    nodes[0] = jnp.zeros((HALF, NZ), F32)
    for i, v in enumerate(solve_chain(e[1:], c[1:], r[1:])):
        nodes[i + 1] = v
    first, last = nodes[z], nodes[z + 1]
    parts = [tuple(chips_ref[3 * j + i] for i in range(3)) for j in range(3)]
    for i, v in enumerate(expand_chain(first, last, parts)):
        nodes[i] = v
    first, last = nodes[x], nodes[x + 1]
    parts = [tuple(cores_ref[3 * j + i] for i in range(3)) for j in range(3)]
    v = expand_chain(first, last, parts)
    even = core == 0
    keep_ref[0], keep_ref[1] = jnp.where(even, v[1], v[3]), jnp.where(even, v[2], v[4])
    send_ref[0], send_ref[1] = jnp.where(even, v[3], v[1]), jnp.where(even, v[4], v[2])


def y_major(ref, x, block):
    rows = ref.reshape(ROWS, NZ)
    for t in range(NY // 8):
        rows[pl.ds(t * 8 * NX + x, 8, stride=NX), :] = block[8 * t : 8 * t + 8]


def prepare_kernel(u_ref, k_ref, a_ref, m_ref, inv_ref, rr_ref, base_ref, g_ref, h_ref, my_ref, iy_ref):
    zero = jnp.zeros((NY, NZ), F32)
    y, g, h = zero, zero, zero + 1.0
    y_major(base_ref, NX - 1, -u_ref[NX - 1])
    y_major(g_ref, NX - 1, g)
    y_major(h_ref, NX - 1, h)
    for j in range(NX - 2, 0, -1):
        m = m_ref[j - 1]
        y = rr_ref[j - 1] * inv_ref[j - 1] + m * y
        g = a_ref[j - 1] + m * g
        h = m * h
        y_major(base_ref, j, y - u_ref[j])
        y_major(g_ref, j, g)
        y_major(h_ref, j, h)
    y_major(base_ref, 0, -u_ref[0])
    y_major(g_ref, 0, zero + 1.0)
    y_major(h_ref, 0, zero)
    k2 = k_ref.reshape(ROWS, NZ)
    at = lambda y: k2[pl.ds(y, NX, stride=NY), :]
    mid = HALF
    ends = []
    for start, step in ((0, 1), (NY - 1, -1)):
        k = at(start)
        ends.append([1.0 + CY * k, k, start, step])
    while any(e[2] != mid for e in ends):
        for e in ends:
            s, k, y, step = e
            if y == mid:
                continue
            k_next = at(y + step)
            c = CY * (k + k_next)
            inv = 1.0 / (s + c)
            m = c * inv
            my_ref[y], iy_ref[y] = m, inv
            e[0] = (0.0 if y + step == mid else 1.0) + m * s
            e[1], e[2] = k_next, y + step
    iy_ref[mid] = 1.0 / (1.0 + ends[0][0] + ends[1][0])
    my_ref[mid] = jnp.zeros((NX, NZ), F32)


LEVELS = 7
STEP = 32


def z_factors(k, keep):
    lane = lax.broadcasted_iota(jnp.int32, k.shape, 1)
    up = CZ * (k + pltpu.roll(k, NZ - 1, 1))
    low = pltpu.roll(up, 1, 1)
    top = up
    e = jnp.ones(k.shape, F32)
    for n in range(LEVELS):
        s = 1 << n
        inv = 1.0 / (e + low + up)
        has_low, has_up = lane >= s + 1, lane <= NZ - 2 - s
        low_in, up_in = jnp.where(has_low, low, 0.0), jnp.where(has_up, up, 0.0)
        keep(n, low_in, up_in, inv)
        share = e * inv
        e = e + low_in * pltpu.roll(share, s, 1) + up_in * pltpu.roll(share, NZ - s, 1)
        new_low = jnp.where(has_low, low * pltpu.roll(low * inv, s, 1), low)
        up = jnp.where(has_up, up * pltpu.roll(up * inv, NZ - s, 1), up)
        low = new_low
    inv = 1.0 / (e + low + up)
    first, last = lane == 0, lane == NZ - 1
    g = jnp.where(first, 1.0, jnp.where(last, 0.0, low * inv))
    h = jnp.where(first, 0.0, jnp.where(last, 1.0, up * inv))
    inv = jnp.where(first | last, 0.0, inv)
    return g, h, jnp.where(lane == NZ - 2, top * g, 0.0), inv


def z_ports_kernel(start, k_ref, u_ref, after_ref, uy_ref, g_ref, h_ref, port_ref, f_ref, t_ref):
    del after_ref
    k2, u2 = k_ref.reshape(ROWS, NZ), u_ref.reshape(ROWS, NZ)
    for y in range(HALF):
        uy_ref[y] = u2[pl.ds(start + y, NX, stride=NY), :]
    g2, h2 = g_ref.reshape(ROWS // 2, NZ), h_ref.reshape(ROWS // 2, NZ)

    def body(i, carry):
        y = start + i * STEP
        k = jnp.concatenate([k2[pl.ds(y + n, NX, stride=NY), :] for n in range(STEP)], axis=0)
        at = pl.ds(pl.multiple_of(i * (STEP * NX), NX * STEP), NX * STEP)

        def keep(n, *values):
            for j, v in enumerate(values):
                f_ref[3 * n + j, at, :] = v

        g, h, w, inv = z_factors(k, keep)
        f_ref[3 * LEVELS, at, :] = inv
        g2[at, :], h2[at, :] = g, h
        t_ref[0, at, :], t_ref[1, at, :] = k, w
        return carry

    lax.fori_loop(0, HALF // STEP, body, 0)
    port_ref[...] = (
        lanes_to_rows([(0, None)], g2[...])
        + lanes_to_rows([(1, None)], h2[...])
        + lanes_to_rows([(2, NZ - 2)], t_ref[1])
        + lanes_to_rows([(5, 0), (6, NZ - 1)], t_ref[0])
    )[:8]


def y_kernel(keep_ref, got_ref, base_ref, gx_ref, hx_ref, my_ref, iy_ref, g0_ref, g1_ref, h0_ref, h1_ref, p0_ref, p1_ref, v_ref, out_ref, b_ref, d_ref):
    core = lax.rem(lax.axis_index("gx"), 2)
    for i in range(2):
        b_ref[i, pl.ds(pl.multiple_of(core * HALF, HALF), HALF)] = keep_ref[i]
        b_ref[i, pl.ds(pl.multiple_of((1 - core) * HALF, HALF), HALF)] = got_ref[i]

    def at(y):
        first = jnp.broadcast_to(b_ref[0, y : y + 1, :], (NX, NZ))
        last = jnp.broadcast_to(b_ref[1, y : y + 1, :], (NX, NZ))
        return base_ref[y] + gx_ref[y] * first + hx_ref[y] * last

    mid = HALF
    low, high = at(0), at(NY - 1)
    for n in range(mid):
        y = n
        v_ref[y] = low * iy_ref[y]
        low = (at(y + 1) if y + 1 < mid else 0.0) + my_ref[y] * low
        y = NY - 1 - n
        if y > mid:
            v_ref[y] = high * iy_ref[y]
            high = (at(y - 1) if y - 1 > mid else 0.0) + my_ref[y] * high
    v = (at(mid) + low + high) * iy_ref[mid]
    low = high = v

    def emit(y, v):
        v_ref[y] = v
        g, h = (g0_ref, h0_ref) if y < HALF else (g1_ref, h1_ref)
        d_ref[0, y * NX : (y + 1) * NX, :] = g[y % HALF] * v
        d_ref[1, y * NX : (y + 1) * NX, :] = h[y % HALF] * v

    emit(mid, v)
    for n in range(1, mid + 1):
        y = mid - n
        low = v_ref[y] + my_ref[y] * low
        emit(y, low)
        y = mid + n
        if y < NY:
            high = v_ref[y] + my_ref[y] * high
            emit(y, high)
    out_ref[...] = (
        jnp.concatenate([p0_ref[...], p1_ref[...]], axis=1)
        + (lanes_to_rows([(3, None)], d_ref[0]) + lanes_to_rows([(4, None)], d_ref[1]))[:8]
    )


def z_local_kernel(f0_ref, f1_ref, u0_ref, u1_ref, v_ref, y_ref):
    v2, y2 = v_ref.reshape(ROWS, NZ), y_ref.reshape(ROWS, NZ)
    rows = STEP * NX

    for half, (f_ref, u_ref) in enumerate(((f0_ref, u0_ref), (f1_ref, u1_ref))):
        u2 = u_ref.reshape(ROWS // 2, NZ)

        def body(i, carry):
            at = pl.ds(pl.multiple_of(i * rows, rows), rows)
            full = pl.ds(pl.multiple_of(half * (ROWS // 2) + i * rows, rows), rows)
            r = v2[full, :]
            for n in range(LEVELS):
                s = 1 << n
                q = r * f_ref[3 * n + 2, at, :]
                r = (
                    r
                    + f_ref[3 * n, at, :] * pltpu.roll(q, s, 1)
                    + f_ref[3 * n + 1, at, :] * pltpu.roll(q, NZ - s, 1)
                )
            y2[full, :] = u2[at, :] + 2.0 * (r * f_ref[3 * LEVELS, at, :])
            return carry

        lax.fori_loop(0, HALF // STEP, body, 0)


CHUNK = 16


def final_kernel(own_ref, one_ref, two_ref, three_ref, y_ref, g0_ref, g1_ref, h0_ref, h1_ref, out_ref, held, b_ref, o_ref, *sems):
    me = lax.axis_index("gz")
    ordered(me, (own_ref, one_ref, two_ref, three_ref), held)
    blocks = [[held[b, i : i + 1, :] for i in range(7)] for b in range(4)]
    e, c, r = [], [], []
    for i, b in enumerate(blocks):
        e += [b[0], b[1]]
        r += [b[3], b[4]]
        c.append(b[2])
        if i < 3:
            c.append(CZ * (b[6] + blocks[i + 1][5]))
    e[0] = e[0] + CZ * blocks[0][5]
    e[-1] = e[-1] + CZ * blocks[3][6]
    values = solve_chain(e, c, r)
    first, last = values[0], values[1]
    for b in range(1, 4):
        first = jnp.where(me == b, values[2 * b], first)
        last = jnp.where(me == b, values[2 * b + 1], last)
    row = lax.broadcasted_iota(jnp.int32, (8, ROWS), 0)
    both = jnp.where(row == 0, 2.0 * first, jnp.where(row == 1, 2.0 * last, 0.0))
    b_ref[...] = rows_to_lanes([(0, range(0, NZ)), (1, range(NZ, 2 * NZ))], both, 2 * NZ)
    o2 = o_ref.reshape(ROWS, NZ)
    copies = []
    for y in range(NY):
        ys = slice(y * NX, (y + 1) * NX)
        g, h = (g0_ref, h0_ref) if y < HALF else (g1_ref, h1_ref)
        o2[pl.ds(y, NX, stride=NY), :] = (
            y_ref[y] + g[y % HALF] * b_ref[ys, :NZ] + h[y % HALF] * b_ref[ys, NZ:]
        )
        if y % CHUNK == CHUNK - 1:
            part = pl.ds(y + 1 - CHUNK, CHUNK)
            copies.append(pltpu.make_async_copy(o_ref.at[:, part], out_ref.at[:, part], sems[y // CHUNK]))
            copies[-1].start()
    for copy in copies:
        copy.wait()


def swap(block, axis, mask):
    n = lax.axis_size(axis)
    return lax.ppermute(block, axis, [(i, i ^ mask) for i in range(n)])


def per_device(u, k, f):
    n = lax.axis_size("gx")
    u, k, f = (pltpu.with_memory_space_constraint(t, pltpu.HBM) for t in (u, k, f))
    u, k, f, edges, end = call(
        edges_kernel,
        [(NX, NY, NZ)] * 3 + [(8, ROWS), (NY, NZ)],
        u, k, f, sems=3, ins_in=pltpu.HBM, name="edges",
    )
    one, two = swap(edges, "gz", 1), swap(edges, "gz", 3)
    below = lax.ppermute(end, "gx", [(i, i + 1) for i in range(1, n - 1, 2)])
    rp, a, m, inv, ew = call(
        local_kernel,
        [(NX, NY, NZ), (NX - 2, NY, NZ), (NX - 2, NY, NZ), (NX - 2, NY, NZ), (3, NY, NZ)],
        u, k, f, name="local",
    )
    keep, send, rr = call(
        halo_kernel,
        [(7, HALF, NZ), (7, HALF, NZ), (NX - 2, NY, NZ)],
        edges, one, two, below, rp, a, m, ew, k, scratch=[(NX, NY, NZ)], name="halo",
    )
    got = swap(send, "gx", 1)
    chip, core_parts = call(core_kernel, [(5, HALF, NZ), (9, HALF, NZ)], keep, got, name="core")
    x_got = [swap(chip, "gx", 2 * i) for i in (1, 2, 3)]
    base, gx, hx, my, iy = call(
        prepare_kernel, [(NY, NX, NZ)] * 5, u, k, a, m, inv, rr, name="prepare"
    )
    z_shapes = [(HALF, NX, NZ)] * 3 + [(8, ROWS // 2), (3 * LEVELS + 1, ROWS // 2, NZ)]
    u0, g0, h0, p0, f0 = call(
        functools.partial(z_ports_kernel, 0),
        z_shapes, k, u, chip, scratch=[(2, ROWS // 2, NZ)], name="z_ports",
    )
    group, chip_parts = call(
        chips_kernel,
        [(5, HALF, NZ), (9, HALF, NZ)],
        chip, *x_got, my, p0, scratch=[(4, 5, HALF, NZ)], name="chips",
    )
    z_got = [swap(group, "gx", 8 * i) for i in (1, 2, 3)]
    u1, g1, h1, p1, f1 = call(
        functools.partial(z_ports_kernel, HALF),
        z_shapes, k, u, group, scratch=[(2, ROWS // 2, NZ)], name="z_ports",
    )
    keep, send = call(
        back_kernel,
        [(2, HALF, NZ), (2, HALF, NZ)],
        group, *z_got, chip_parts, core_parts, p1,
        scratch=[(4, 5, HALF, NZ), (5, HALF, NZ)], name="back",
    )
    got = swap(send, "gx", 1)
    v, message = call(
        y_kernel,
        [(NY, NX, NZ), (8, ROWS)],
        keep, got, base, gx, hx, my, iy, g0, g1, h0, h1, p0, p1,
        scratch=[(2, NY, NZ), (2, ROWS, NZ)], name="y_solve",
    )
    l_got = [swap(message, "gz", i) for i in (1, 2, 3)]
    yz, = call(z_local_kernel, [(NY, NX, NZ)], f0, f1, u0, u1, v, name="z_local")
    out, = call(
        final_kernel,
        [(NX, NY, NZ)],
        message, *l_got, yz, g0, g1, h0, h1,
        scratch=[(4, 8, ROWS), (ROWS, 2 * NZ), (NX, NY, NZ)], sems=NY // CHUNK,
        outs_in=pltpu.HBM, name="final",
    )
    return out


def solution(mesh):
    spec = P("gx", None, "gz")
    return jax.shard_map(
        per_device, mesh=mesh, in_specs=(spec, spec, spec), out_specs=spec, check_vma=False
    )
```

time: 47.7 us -> 44.5 us (0.933)
  Pallas kernels: 13.6 us -> 9.19 us
  starting transfers between devices: 19.2 us -> 20.5 us
    pallas_call x12, Pallas kernels: 13.6 us -> 9.19 us  [call(): pl.pallas_call(kernel, out_shape=shapes, in_specs=[pl.BlockSpec(memory_sp...]
    ppermute x13, starting transfers between devices: 19.2 us -> 19.8 us  [swap(): return lax.ppermute(block, axis, [(i, i ^ mask) for i in range(n)])]
    ppermute x0 -> x1, starting transfers between devices: none -> 0.66 us  [per_device(): below = lax.ppermute(end, 'gx', [(i, i + 1) for i in range(1, n - 1, 2)])]
  transfers between devices with their start and end apart: 13 -> 14, of which waited for: 8 -> 8; matrix products, arithmetic and copies ran while one was open for 0% -> 0% of each run, Pallas kernels for 18% -> 13%
where the time goes in v3:
time: 44.5 us; the launch traced here: 44.4 us
  starting transfers between devices  20.5 us (46%)
  waiting for transfers between devices  14.5 us (33%)
  Pallas kernels  9.19 us (21%)
    ppermute x13, starting transfers between devices, swap(): return lax.ppermute(block, axis, [(i, i ^ mask) for i in range(n)])  19.8 us
    ppermute x13, waiting for transfers between devices, swap(): return lax.ppermute(block, axis, [(i, i ^ mask) for i in range(n)])  14.5 us
    pallas_call x12, Pallas kernels, call(): pl.pallas_call(kernel, out_shape=shapes, in_specs=[pl.BlockSpec(memory_sp...  9.19 us
  transfers between devices with their start and end apart: 14, of which 8 were waited for; matrix products, arithmetic and copies ran while one was open for 0% of the time, Pallas kernels for 13%

profile of v3, /device:TPU:0, one launch (start us, length us, event | category | flops | bytes accessed | tf_op | source)
XLA Modules:
  0.0 44.4 jit_solution(10794461886517156312)
XLA Ops:
  0.0 1.4 %edges.1 = (f32[8,64,128]{2,1,0:T(8,128)S(1)}, f32[8,64,128]{2,1,0:T(8,128)S(1)}, f32[8,64,128]{2,1,0:T(8,128)S(1)}, f32[8,512]{1,0:T(8,128)S(1)}, f32[64,128]{1,0:T(8,128)S(1)}) custom-call(f32[8,64,128]{2,1,0:T(8,128)} %u_hbm.1, f32[8,64,128]{2,1,0:T(8,128)} %k_hbm.1, f32[8,64,128]{2,1,0:T(8,128)} %f_hbm.1), custom_call_target="tpu_custom_call" | custom-call | bytes 1622016 | tf_op jit(solution)/shard_map/edges/pallas_call | solution.py:24
  1.4 0.7 %collective-permute-start.2 = (f32[64,128]{1,0:T(8,128)S(1)}, f32[64,128]{1,0:T(8,128)S(1)}, u32[]{:S(2)}, u32[]{:S(2)}) collective-permute-start(f32[64,128]{1,0:T(8,128)S(1)} %get-tuple-element.42), channel_id=1, source_target_pairs={{4,8},{12,16},{20,24},{28,32},{36,40},{44,48},{52,56},{60,64},{68,... | collective-permute-start | bytes 98312 | tf_op jit(solution)/shard_map/ppermute | solution.py:500
  2.0 1.7 %collective-permute-start = (f32[8,512]{1,0:T(8,128)S(1)}, f32[8,512]{1,0:T(8,128)S(1)}, u32[]{:S(2)}, u32[]{:S(2)}) collective-permute-start(f32[8,512]{1,0:T(8,128)S(1)} %get-tuple-element.41.own_ref), channel_id=1, source_target_pairs={{0,1},{1,0},{2,3},{3,2},{4,5},{5,4},{6,7},{7,6},{8,9},{9,8},{10,11... | collective-permute-start | bytes 49160 | tf_op jit(solution)/shard_map/ppermute | solution.py:488
  3.8 2.2 %collective-permute-start.1 = (f32[8,512]{1,0:T(8,128)S(1)}, f32[8,512]{1,0:T(8,128)S(1)}, u32[]{:S(2)}, u32[]{:S(2)}) collective-permute-start(f32[8,512]{1,0:T(8,128)S(1)} %get-tuple-element.41.own_ref), channel_id=1, source_target_pairs={{0,3},{1,2},{2,1},{3,0},{4,7},{5,6},{6,5},{7,4},{8,11},{9,10},{10,... | collective-permute-start | bytes 49160 | tf_op jit(solution)/shard_map/ppermute | solution.py:488
  6.0 0.5 %local.1 = (f32[8,64,128]{2,1,0:T(8,128)S(1)}, f32[6,64,128]{2,1,0:T(8,128)S(1)}, f32[6,64,128]{2,1,0:T(8,128)S(1)}, f32[6,64,128]{2,1,0:T(8,128)S(1)}, f32[3,64,128]{2,1,0:T(8,128)S(1)}) custom-call(f32[8,64,128]{2,1,0:T(8,128)S(1)} %get-tuple-element.43.u_ref, f32[8,64,128]{2,1,0:T(8,128)S(1)} %get-tuple-element.44.k_ref, ...), custom_call_target="tpu_custom_call" | custom-call | bytes 1736704 | tf_op jit(solution)/shard_map/local/pallas_call | solution.py:24
  6.5 2.2 %collective-permute-done.1.two_ref = f32[8,512]{1,0:T(8,128)S(1)} collective-permute-done((f32[8,512]{1,0:T(8,128)S(1)}, f32[8,512]{1,0:T(8,128)S(1)}, u32[]{:S(2)}, u32[]{:S(2)}) %collective-permute-start.1) | collective-permute-done | bytes 16416 | tf_op jit(solution)/shard_map/ppermute | solution.py:488
  8.7 0.3 halo.1
  9.0 1.5 %collective-permute-start.3 = (f32[7,32,128]{2,1,0:T(8,128)S(1)}, f32[7,32,128]{2,1,0:T(8,128)S(1)}, u32[]{:S(2)}, u32[]{:S(2)}) collective-permute-start(f32[7,32,128]{2,1,0:T(8,128)S(1)} %get-tuple-element.51), channel_id=1, source_target_pairs={{0,4},{4,0},{8,12},{12,8},{16,20},{20,16},{24,28},{28,24},{32,36},... | collective-permute-start | bytes 344072 | tf_op jit(solution)/shard_map/ppermute | solution.py:488
  10.5 1.0 %collective-permute-done.3.got_ref = f32[7,32,128]{2,1,0:T(8,128)S(1)} collective-permute-done((f32[7,32,128]{2,1,0:T(8,128)S(1)}, f32[7,32,128]{2,1,0:T(8,128)S(1)}, u32[]{:S(2)}, u32[]{:S(2)}) %collective-permute-start.3) | collective-permute-done | bytes 114720 | tf_op jit(solution)/shard_map/ppermute | solution.py:488
  11.6 1.6 %collective-permute-start.4 = (f32[5,32,128]{2,1,0:T(8,128)S(1)}, f32[5,32,128]{2,1,0:T(8,128)S(1)}, u32[]{:S(2)}, u32[]{:S(2)}) collective-permute-start(f32[5,32,128]{2,1,0:T(8,128)S(1)} %get-tuple-element.52.after_ref.own_ref), channel_id=1, source_target_pairs={{0,8},{4,12},{8,0},{12,4},{16,24},{20,28},{24,16},{28,20},{32,40},... | collective-permute-start | bytes 245768 | tf_op jit(solution)/shard_map/ppermute | solution.py:488
  13.2 3.1 %collective-permute-start.5 = (f32[5,32,128]{2,1,0:T(8,128)S(1)}, f32[5,32,128]{2,1,0:T(8,128)S(1)}, u32[]{:S(2)}, u32[]{:S(2)}) collective-permute-start(f32[5,32,128]{2,1,0:T(8,128)S(1)} %get-tuple-element.52.after_ref.own_ref), channel_id=1, source_target_pairs={{0,16},{4,20},{8,24},{12,28},{16,0},{20,4},{24,8},{28,12},{32,48},... | collective-permute-start | bytes 245768 | tf_op jit(solution)/shard_map/ppermute | solution.py:488
  16.2 0.1 collective-permute-start.6
  16.4 0.5 %prepare.1 = (f32[64,8,128]{2,1,0:T(8,128)S(1)}, f32[64,8,128]{2,1,0:T(8,128)S(1)}, f32[64,8,128]{2,1,0:T(8,128)S(1)}, f32[64,8,128]{2,1,0:T(8,128)S(1)}, f32[64,8,128]{2,1,0:T(8,128)S(1)}) custom-call(f32[8,64,128]{2,1,0:T(8,128)S(1)} %get-tuple-element.43.u_ref, f32[8,64,128]{2,1,0:T(8,128)S(1)} %get-tuple-element.44.k_ref, ...), custom_call_target="tpu_custom_call" | custom-call | bytes 2621440 | tf_op jit(solution)/shard_map/prepare/pallas_call | solution.py:24
  16.9 1.7 %z_ports.2 = (f32[32,8,128]{2,1,0:T(8,128)S(1)}, f32[32,8,128]{2,1,0:T(8,128)S(1)}, f32[32,8,128]{2,1,0:T(8,128)S(1)}, f32[8,256]{1,0:T(8,128)S(1)}, f32[22,256,128]{2,1,0:T(8,128)S(1)}) custom-call(f32[8,64,128]{2,1,0:T(8,128)S(1)} %get-tuple-element.44.k_ref, f32[8,64,128]{2,1,0:T(8,128)S(1)} %get-tuple-element.43.u_ref, ...), custom_call_target="tpu_custom_call" | custom-call | bytes 3891200 | tf_op jit(solution)/shard_map/z_ports/pallas_call | solution.py:24
  18.6 2.2 %collective-permute-done.5.two_ref = f32[5,32,128]{2,1,0:T(8,128)S(1)} collective-permute-done((f32[5,32,128]{2,1,0:T(8,128)S(1)}, f32[5,32,128]{2,1,0:T(8,128)S(1)}, u32[]{:S(2)}, u32[]{:S(2)}) %collective-permute-start.5) | collective-permute-done | bytes 81952 | tf_op jit(solution)/shard_map/ppermute | solution.py:488
  20.7 1.7 %collective-permute-done.6.three_ref = f32[5,32,128]{2,1,0:T(8,128)S(1)} collective-permute-done((f32[5,32,128]{2,1,0:T(8,128)S(1)}, f32[5,32,128]{2,1,0:T(8,128)S(1)}, u32[]{:S(2)}, u32[]{:S(2)}) %collective-permute-start.6) | collective-permute-done | bytes 81952 | tf_op jit(solution)/shard_map/ppermute | solution.py:488
  22.5 2.0 %collective-permute-start.7 = (f32[5,32,128]{2,1,0:T(8,128)S(1)}, f32[5,32,128]{2,1,0:T(8,128)S(1)}, u32[]{:S(2)}, u32[]{:S(2)}) collective-permute-start(f32[5,32,128]{2,1,0:T(8,128)S(1)} %get-tuple-element.57.after_ref.own_ref), channel_id=1, source_target_pairs={{0,32},{4,36},{8,40},{12,44},{16,48},{20,52},{24,56},{28,60},{32,0... | collective-permute-start | bytes 245768 | tf_op jit(solution)/shard_map/ppermute | solution.py:488
  24.5 2.6 %collective-permute-start.8 = (f32[5,32,128]{2,1,0:T(8,128)S(1)}, f32[5,32,128]{2,1,0:T(8,128)S(1)}, u32[]{:S(2)}, u32[]{:S(2)}) collective-permute-start(f32[5,32,128]{2,1,0:T(8,128)S(1)} %get-tuple-element.57.after_ref.own_ref), channel_id=1, source_target_pairs={{0,64},{4,68},{8,72},{12,76},{16,80},{20,84},{24,88},{28,92},{32,9... | collective-permute-start | bytes 245768 | tf_op jit(solution)/shard_map/ppermute | solution.py:488
  27.1 0.2 collective-permute-start.9
  27.3 1.6 %z_ports.3 = (f32[32,8,128]{2,1,0:T(8,128)S(1)}, f32[32,8,128]{2,1,0:T(8,128)S(1)}, f32[32,8,128]{2,1,0:T(8,128)S(1)}, f32[8,256]{1,0:T(8,128)S(1)}, f32[22,256,128]{2,1,0:T(8,128)S(1)}) custom-call(f32[8,64,128]{2,1,0:T(8,128)S(1)} %get-tuple-element.44.k_ref, f32[8,64,128]{2,1,0:T(8,128)S(1)} %get-tuple-element.43.u_ref, ...), custom_call_target="tpu_custom_call" | custom-call | bytes 3891200 | tf_op jit(solution)/shard_map/z_ports/pallas_call | solution.py:24
  28.9 1.9 %collective-permute-done.8.two_ref = f32[5,32,128]{2,1,0:T(8,128)S(1)} collective-permute-done((f32[5,32,128]{2,1,0:T(8,128)S(1)}, f32[5,32,128]{2,1,0:T(8,128)S(1)}, u32[]{:S(2)}, u32[]{:S(2)}) %collective-permute-start.8) | collective-permute-done | bytes 81952 | tf_op jit(solution)/shard_map/ppermute | solution.py:488
  30.8 2.0 %collective-permute-done.9.three_ref = f32[5,32,128]{2,1,0:T(8,128)S(1)} collective-permute-done((f32[5,32,128]{2,1,0:T(8,128)S(1)}, f32[5,32,128]{2,1,0:T(8,128)S(1)}, u32[]{:S(2)}, u32[]{:S(2)}) %collective-permute-start.9) | collective-permute-done | bytes 81952 | tf_op jit(solution)/shard_map/ppermute | solution.py:488
  32.7 0.1 back.1
  32.9 0.1 collective-permute-start.10
  32.9 1.2 %collective-permute-done.10.got_ref = f32[2,32,128]{2,1,0:T(8,128)S(1)} collective-permute-done((f32[2,32,128]{2,1,0:T(8,128)S(1)}, f32[2,32,128]{2,1,0:T(8,128)S(1)}, u32[]{:S(2)}, u32[]{:S(2)}) %collective-permute-start.10) | collective-permute-done | bytes 32800 | tf_op jit(solution)/shard_map/ppermute | solution.py:488
  34.1 0.4 y_solve.1
  34.6 0.1 collective-permute-start.11
  34.7 3.6 %collective-permute-start.12 = (f32[8,512]{1,0:T(8,128)S(1)}, f32[8,512]{1,0:T(8,128)S(1)}, u32[]{:S(2)}, u32[]{:S(2)}) collective-permute-start(f32[8,512]{1,0:T(8,128)S(1)} %get-tuple-element.71.own_ref), channel_id=1, source_target_pairs={{0,2},{1,3},{2,0},{3,1},{4,6},{5,7},{6,4},{7,5},{8,10},{9,11},{10,... | collective-permute-start | bytes 49160 | tf_op jit(solution)/shard_map/ppermute | solution.py:488
  38.3 1.1 %collective-permute-start.13 = (f32[8,512]{1,0:T(8,128)S(1)}, f32[8,512]{1,0:T(8,128)S(1)}, u32[]{:S(2)}, u32[]{:S(2)}) collective-permute-start(f32[8,512]{1,0:T(8,128)S(1)} %get-tuple-element.71.own_ref), channel_id=1, source_target_pairs={{0,3},{1,2},{2,1},{3,0},{4,7},{5,6},{6,5},{7,4},{8,11},{9,10},{10,... | collective-permute-start | bytes 49160 | tf_op jit(solution)/shard_map/ppermute | solution.py:488
  39.4 1.4 %z_local.1.y_ref = f32[64,8,128]{2,1,0:T(8,128)S(1)} custom-call(f32[22,256,128]{2,1,0:T(8,128)S(1)} %get-tuple-element.72.f0_ref, f32[22,256,128]{2,1,0:T(8,128)S(1)} %get-tuple-element.73.f1_ref, f32[32,8,128]{2,1,0:T(8,128)S(1)} %get-tuple-element.74.u0_ref, f32[32,8,128]{2,1,0:T(8,128)S(1)} %get-tuple-element.75.u1_ref, ...), custom_call_target="tpu_custom_call" | custom-call | bytes 6553600 | tf_op jit(solution)/shard_map/z_local/pallas_call | solution.py:24
  40.8 2.5 %collective-permute-done.13.three_ref = f32[8,512]{1,0:T(8,128)S(1)} collective-permute-done((f32[8,512]{1,0:T(8,128)S(1)}, f32[8,512]{1,0:T(8,128)S(1)}, u32[]{:S(2)}, u32[]{:S(2)}) %collective-permute-start.13) | collective-permute-done | bytes 16416 | tf_op jit(solution)/shard_map/ppermute | solution.py:488
  43.3 1.1 %final.1 = f32[8,64,128]{2,1,0:T(8,128)} custom-call(f32[8,512]{1,0:T(8,128)S(1)} %get-tuple-element.71.own_ref, f32[8,512]{1,0:T(8,128)S(1)} %collective-permute-done.11.one_ref, f32[8,512]{1,0:T(8,128)S(1)} %collective-permute-done.12.two_ref, f32[8,512]{1,0:T(8,128)S(1)} %collective-permute-done.13.three_ref, f32[64,8,128]{2,1,0:T(8,128)S(1)} %z_local.1.y_ref, ...), custom_call_target="tpu_custom_call" | custom-call | bytes 1114112 | tf_op jit(solution)/shard_map/final/pallas_call | solution.py:24
  (8 shorter events, 0.1 us)
Async XLA Ops:
  1.4 7.4 %collective-permute-start.2 = (f32[64,128]{1,0:T(8,128)S(1)}, f32[64,128]{1,0:T(8,128)S(1)}, u32[]{:S(2)}, u32[]{:S(2)}) collective-permute-start(f32[64,128]{1,0:T(8,128)S(1)} %get-tuple-element.42), channel_id=1, source_target_pairs={{4,8},{12,16},{20,24},{28,32},{36,40},{44,48},{52,56},{60,64},{68,... | collective-permute-start | bytes 98312 | tf_op jit(solution)/shard_map/ppermute | solution.py:500
  2.0 4.5 %collective-permute-start = (f32[8,512]{1,0:T(8,128)S(1)}, f32[8,512]{1,0:T(8,128)S(1)}, u32[]{:S(2)}, u32[]{:S(2)}) collective-permute-start(f32[8,512]{1,0:T(8,128)S(1)} %get-tuple-element.41.own_ref), channel_id=1, source_target_pairs={{0,1},{1,0},{2,3},{3,2},{4,5},{5,4},{6,7},{7,6},{8,9},{9,8},{10,11... | collective-permute-start | bytes 49160 | tf_op jit(solution)/shard_map/ppermute | solution.py:488
  3.8 4.9 %collective-permute-start.1 = (f32[8,512]{1,0:T(8,128)S(1)}, f32[8,512]{1,0:T(8,128)S(1)}, u32[]{:S(2)}, u32[]{:S(2)}) collective-permute-start(f32[8,512]{1,0:T(8,128)S(1)} %get-tuple-element.41.own_ref), channel_id=1, source_target_pairs={{0,3},{1,2},{2,1},{3,0},{4,7},{5,6},{6,5},{7,4},{8,11},{9,10},{10,... | collective-permute-start | bytes 49160 | tf_op jit(solution)/shard_map/ppermute | solution.py:488
  9.0 2.5 %collective-permute-start.3 = (f32[7,32,128]{2,1,0:T(8,128)S(1)}, f32[7,32,128]{2,1,0:T(8,128)S(1)}, u32[]{:S(2)}, u32[]{:S(2)}) collective-permute-start(f32[7,32,128]{2,1,0:T(8,128)S(1)} %get-tuple-element.51), channel_id=1, source_target_pairs={{0,4},{4,0},{8,12},{12,8},{16,20},{20,16},{24,28},{28,24},{32,36},... | collective-permute-start | bytes 344072 | tf_op jit(solution)/shard_map/ppermute | solution.py:488
  11.6 7.0 %collective-permute-start.4 = (f32[5,32,128]{2,1,0:T(8,128)S(1)}, f32[5,32,128]{2,1,0:T(8,128)S(1)}, u32[]{:S(2)}, u32[]{:S(2)}) collective-permute-start(f32[5,32,128]{2,1,0:T(8,128)S(1)} %get-tuple-element.52.after_ref.own_ref), channel_id=1, source_target_pairs={{0,8},{4,12},{8,0},{12,4},{16,24},{20,28},{24,16},{28,20},{32,40},... | collective-permute-start | bytes 245768 | tf_op jit(solution)/shard_map/ppermute | solution.py:488
  13.2 7.6 %collective-permute-start.5 = (f32[5,32,128]{2,1,0:T(8,128)S(1)}, f32[5,32,128]{2,1,0:T(8,128)S(1)}, u32[]{:S(2)}, u32[]{:S(2)}) collective-permute-start(f32[5,32,128]{2,1,0:T(8,128)S(1)} %get-tuple-element.52.after_ref.own_ref), channel_id=1, source_target_pairs={{0,16},{4,20},{8,24},{12,28},{16,0},{20,4},{24,8},{28,12},{32,48},... | collective-permute-start | bytes 245768 | tf_op jit(solution)/shard_map/ppermute | solution.py:488
  16.2 6.2 %collective-permute-start.6 = (f32[5,32,128]{2,1,0:T(8,128)S(1)}, f32[5,32,128]{2,1,0:T(8,128)S(1)}, u32[]{:S(2)}, u32[]{:S(2)}) collective-permute-start(f32[5,32,128]{2,1,0:T(8,128)S(1)} %get-tuple-element.52.after_ref.own_ref), channel_id=1, source_target_pairs={{0,24},{4,28},{8,16},{12,20},{16,8},{20,12},{24,0},{28,4},{32,56},... | collective-permute-start | bytes 245768 | tf_op jit(solution)/shard_map/ppermute | solution.py:488
  22.5 6.4 %collective-permute-start.7 = (f32[5,32,128]{2,1,0:T(8,128)S(1)}, f32[5,32,128]{2,1,0:T(8,128)S(1)}, u32[]{:S(2)}, u32[]{:S(2)}) collective-permute-start(f32[5,32,128]{2,1,0:T(8,128)S(1)} %get-tuple-element.57.after_ref.own_ref), channel_id=1, source_target_pairs={{0,32},{4,36},{8,40},{12,44},{16,48},{20,52},{24,56},{28,60},{32,0... | collective-permute-start | bytes 245768 | tf_op jit(solution)/shard_map/ppermute | solution.py:488
  24.5 6.3 %collective-permute-start.8 = (f32[5,32,128]{2,1,0:T(8,128)S(1)}, f32[5,32,128]{2,1,0:T(8,128)S(1)}, u32[]{:S(2)}, u32[]{:S(2)}) collective-permute-start(f32[5,32,128]{2,1,0:T(8,128)S(1)} %get-tuple-element.57.after_ref.own_ref), channel_id=1, source_target_pairs={{0,64},{4,68},{8,72},{12,76},{16,80},{20,84},{24,88},{28,92},{32,9... | collective-permute-start | bytes 245768 | tf_op jit(solution)/shard_map/ppermute | solution.py:488
  27.1 5.7 %collective-permute-start.9 = (f32[5,32,128]{2,1,0:T(8,128)S(1)}, f32[5,32,128]{2,1,0:T(8,128)S(1)}, u32[]{:S(2)}, u32[]{:S(2)}) collective-permute-start(f32[5,32,128]{2,1,0:T(8,128)S(1)} %get-tuple-element.57.after_ref.own_ref), channel_id=1, source_target_pairs={{0,96},{4,100},{8,104},{12,108},{16,112},{20,116},{24,120},{28,124... | collective-permute-start | bytes 245768 | tf_op jit(solution)/shard_map/ppermute | solution.py:488
  32.9 1.3 %collective-permute-start.10 = (f32[2,32,128]{2,1,0:T(8,128)S(1)}, f32[2,32,128]{2,1,0:T(8,128)S(1)}, u32[]{:S(2)}, u32[]{:S(2)}) collective-permute-start(f32[2,32,128]{2,1,0:T(8,128)S(1)} %get-tuple-element.62), channel_id=1, source_target_pairs={{0,4},{4,0},{8,12},{12,8},{16,20},{20,16},{24,28},{28,24},{32,36},... | collective-permute-start | bytes 98312 | tf_op jit(solution)/shard_map/ppermute | solution.py:488
  34.6 6.2 %collective-permute-start.11 = (f32[8,512]{1,0:T(8,128)S(1)}, f32[8,512]{1,0:T(8,128)S(1)}, u32[]{:S(2)}, u32[]{:S(2)}) collective-permute-start(f32[8,512]{1,0:T(8,128)S(1)} %get-tuple-element.71.own_ref), channel_id=1, source_target_pairs={{0,1},{1,0},{2,3},{3,2},{4,5},{5,4},{6,7},{7,6},{8,9},{9,8},{10,11... | collective-permute-start | bytes 49160 | tf_op jit(solution)/shard_map/ppermute | solution.py:488
  34.7 6.1 %collective-permute-start.12 = (f32[8,512]{1,0:T(8,128)S(1)}, f32[8,512]{1,0:T(8,128)S(1)}, u32[]{:S(2)}, u32[]{:S(2)}) collective-permute-start(f32[8,512]{1,0:T(8,128)S(1)} %get-tuple-element.71.own_ref), channel_id=1, source_target_pairs={{0,2},{1,3},{2,0},{3,1},{4,6},{5,7},{6,4},{7,5},{8,10},{9,11},{10,... | collective-permute-start | bytes 49160 | tf_op jit(solution)/shard_map/ppermute | solution.py:488
  38.3 4.9 %collective-permute-start.13 = (f32[8,512]{1,0:T(8,128)S(1)}, f32[8,512]{1,0:T(8,128)S(1)}, u32[]{:S(2)}, u32[]{:S(2)}) collective-permute-start(f32[8,512]{1,0:T(8,128)S(1)} %get-tuple-element.71.own_ref), channel_id=1, source_target_pairs={{0,3},{1,2},{2,1},{3,0},{4,7},{5,6},{6,5},{7,4},{8,11},{9,10},{10,... | collective-permute-start | bytes 49160 | tf_op jit(solution)/shard_map/ppermute | solution.py:488

commit v4 on v3

--- a/solution.py
+++ b/solution.py
@@ -10,6 +10,8 @@
 NX, NY, NZ = 8, 64, 128
 ROWS = NX * NY
 HALF = NY // 2
+X_ORDER, Z_ORDER, L_ORDER = (2, 3, 1), (2, 3, 1), (2, 3, 1)
+RING = 8
 CX = 0.25 * 16.0 * NX * NX
 CY = 0.25 * 2.0
 CZ = 0.25 * 0.5 * NZ * NZ
@@ -150,7 +152,8 @@
     copies[1].wait()
     both = jnp.where((lane == 1) | (lane == 2), k, u_ref[...].reshape(ROWS, NZ))
     out_ref[...] = lanes_to_rows([(0, 0), (1, NZ - 1), (2, 2), (3, 1)], both)[:8]
-    end_ref[...] = k_ref[NX - 1]
+    index = lax.axis_index("gx")
+    end_ref[...] = k_ref[jnp.where(lax.rem(index, 2) == 1, NX - 1, 0)]
     copies[2].wait()
 
 
@@ -195,6 +198,8 @@
     fix_ref[...] = rows_to_lanes([(0, 0), (1, NZ - 1)], both, NZ).reshape(NX, NY, NZ)
     top = jnp.where(index == lax.axis_size("gx") - 1, CX, 0.0)
     inner = jnp.where(core == 0, NX - 1, 0)
+    place = lax.rem(index, RING)
+    inside = jnp.where(index >= RING, 1.0, 0.0)
     for which, out in ((core, keep_ref), (1 - core, send_ref)):
         ys = pl.ds(pl.multiple_of(which * HALF, HALF), HALF)
         r_h = rp_ref[0, ys] + fix_ref[0, ys]
@@ -207,17 +212,43 @@
         out[1] = ew_ref[1, ys] + top * k_ref[NX - 1, ys]
         out[3], out[4] = r_h, rr
         out[5] = k_ref[inner, ys]
-        out[6] = CX * (below_ref[ys] + k_ref[0, ys])
+        below, k = below_ref[ys], k_ref[0, ys]
+        out[6] = jnp.where(place == 0, k, jnp.where(place == RING - 1, below * inside, CX * (below + k)))
 
 
 def core_kernel(own_ref, got_ref, out_ref, parts_ref):
-    first = lax.rem(lax.axis_index("gx"), 2) == 0
+    index = lax.axis_index("gx")
+    first = lax.rem(index, 2) == 0
+    head = lax.rem(index, RING) < 2
     low = [jnp.where(first, own_ref[i], got_ref[i]) for i in range(7)]
-    high = [jnp.where(first, got_ref[i], own_ref[i]) for i in range(6)]
-    e = [0.0, low[0], low[1], high[0], high[1]]
-    c = [low[6], low[2], CX * (low[5] + high[5]), high[2]]
-    r = [0.0, low[3], low[4], high[3], high[4]]
+    high = [jnp.where(first, got_ref[i], own_ref[i]) for i in range(7)]
+    cut = jnp.where(head, 1.0, 0.0)
+    near = jnp.where(head, 2.0 * low[2], low[2])
+    e = [cut * low[0], (1.0 - cut) * low[0], low[1], high[0], high[1]]
+    c = [jnp.where(head, near, low[6]), near, CX * (low[5] + high[5]), high[2]]
+    r = [cut * low[3], (1.0 - cut) * low[3], low[4], high[3], high[4]]
     port, parts = reduce_chain(e, c, r)
+    for i, v in enumerate(port):
+        out_ref[i] = v
+    out_ref[5] = jnp.where(head, low[6], high[6])
+    for j, p in enumerate(parts):
+        for i in range(3):
+            parts_ref[3 * j + i] = p[i]
+
+
+def ordered(me, refs, order, held):
+    for i, ref in zip((0,) + order, refs):
+        held[jnp.bitwise_xor(me, i)] = ref[...]
+
+
+def chips_kernel(own_ref, one_ref, two_ref, three_ref, after_ref, also_ref, out_ref, parts_ref, held):
+    del after_ref, also_ref
+    me = lax.rem(lax.axis_index("gx") // 2, 4)
+    ordered(me, (own_ref, one_ref, two_ref, three_ref), X_ORDER, held)
+    blocks = [[held[b, i] for i in range(5)] for b in range(4)]
+    e, c, r = join(blocks)
+    below = CX * (held[0, 5] + held[3, 5])
+    port, parts = reduce_chain([0.0] + e, [below] + c, [0.0] + r)
     for i, v in enumerate(port):
         out_ref[i] = v
     for j, p in enumerate(parts):
@@ -225,30 +256,11 @@
             parts_ref[3 * j + i] = p[i]
 
 
-def ordered(me, refs, held):
-    for i, ref in enumerate(refs):
-        held[jnp.bitwise_xor(me, i)] = ref[...]
-    return held
-
-
-def chips_kernel(own_ref, one_ref, two_ref, three_ref, after_ref, also_ref, out_ref, parts_ref, held):
-    del after_ref, also_ref
-    me = lax.rem(lax.axis_index("gx") // 2, 4)
-    ordered(me, (own_ref, one_ref, two_ref, three_ref), held)
-    blocks = [[held[b, i] for i in range(5)] for b in range(4)]
-    port, parts = reduce_chain(*join(blocks))
-    for i, v in enumerate(port):
-        out_ref[i] = v
-    for j, p in enumerate(parts):
-        for i in range(3):
-            parts_ref[3 * j + i] = p[i]
-
-
 def back_kernel(own_ref, one_ref, two_ref, three_ref, chips_ref, cores_ref, after_ref, keep_ref, send_ref, held, nodes):
     del after_ref
     index = lax.axis_index("gx")
     core, x, z = lax.rem(index, 2), lax.rem(index // 2, 4), index // 8
-    ordered(z, (own_ref, one_ref, two_ref, three_ref), held)
+    ordered(z, (own_ref, one_ref, two_ref, three_ref), Z_ORDER, held)
     blocks = [[held[b, i] for i in range(5)] for b in range(4)]
     e, c, r = join(blocks)
     e[1] = e[1] + c[0]
@@ -256,12 +268,13 @@
     for i, v in enumerate(solve_chain(e[1:], c[1:], r[1:])):
         nodes[i + 1] = v
     first, last = nodes[z], nodes[z + 1]
-    parts = [tuple(chips_ref[3 * j + i] for i in range(3)) for j in range(3)]
+    parts = [tuple(chips_ref[3 * j + i] for i in range(3)) for j in range(4)]
     for i, v in enumerate(expand_chain(first, last, parts)):
         nodes[i] = v
-    first, last = nodes[x], nodes[x + 1]
+    first, last = nodes[x + 1], nodes[x + 2]
     parts = [tuple(cores_ref[3 * j + i] for i in range(3)) for j in range(3)]
     v = expand_chain(first, last, parts)
+    v[1] = jnp.where(x == 0, v[0], v[1])
     even = core == 0
     keep_ref[0], keep_ref[1] = jnp.where(even, v[1], v[3]), jnp.where(even, v[2], v[4])
     send_ref[0], send_ref[1] = jnp.where(even, v[3], v[1]), jnp.where(even, v[4], v[2])
@@ -448,7 +461,7 @@
 
 def final_kernel(own_ref, one_ref, two_ref, three_ref, y_ref, g0_ref, g1_ref, h0_ref, h1_ref, out_ref, held, b_ref, o_ref, *sems):
     me = lax.axis_index("gz")
-    ordered(me, (own_ref, one_ref, two_ref, three_ref), held)
+    ordered(me, (own_ref, one_ref, two_ref, three_ref), L_ORDER, held)
     blocks = [[held[b, i : i + 1, :] for i in range(7)] for b in range(4)]
     e, c, r = [], [], []
     for i, b in enumerate(blocks):
@@ -488,6 +501,13 @@
     return lax.ppermute(block, axis, [(i, i ^ mask) for i in range(n)])
 
 
+def below_target(i, n):
+    place = i % RING
+    if place in (0, RING - 1):
+        return (i + RING) % n
+    return i + 1 if place % 2 else i - 1
+
+
 def per_device(u, k, f):
     n = lax.axis_size("gx")
     u, k, f = (pltpu.with_memory_space_constraint(t, pltpu.HBM) for t in (u, k, f))
@@ -497,7 +517,7 @@
         u, k, f, sems=3, ins_in=pltpu.HBM, name="edges",
     )
     one, two = swap(edges, "gz", 1), swap(edges, "gz", 3)
-    below = lax.ppermute(end, "gx", [(i, i + 1) for i in range(1, n - 1, 2)])
+    below = lax.ppermute(end, "gx", [(i, below_target(i, n)) for i in range(n)])
     rp, a, m, inv, ew = call(
         local_kernel,
         [(NX, NY, NZ), (NX - 2, NY, NZ), (NX - 2, NY, NZ), (NX - 2, NY, NZ), (3, NY, NZ)],
@@ -509,8 +529,8 @@
         edges, one, two, below, rp, a, m, ew, k, scratch=[(NX, NY, NZ)], name="halo",
     )
     got = swap(send, "gx", 1)
-    chip, core_parts = call(core_kernel, [(5, HALF, NZ), (9, HALF, NZ)], keep, got, name="core")
-    x_got = [swap(chip, "gx", 2 * i) for i in (1, 2, 3)]
+    chip, core_parts = call(core_kernel, [(6, HALF, NZ), (9, HALF, NZ)], keep, got, name="core")
+    x_got = [swap(chip, "gx", 2 * i) for i in X_ORDER]
     base, gx, hx, my, iy = call(
         prepare_kernel, [(NY, NX, NZ)] * 5, u, k, a, m, inv, rr, name="prepare"
     )
@@ -521,10 +541,10 @@
     )
     group, chip_parts = call(
         chips_kernel,
-        [(5, HALF, NZ), (9, HALF, NZ)],
-        chip, *x_got, my, p0, scratch=[(4, 5, HALF, NZ)], name="chips",
-    )
-    z_got = [swap(group, "gx", 8 * i) for i in (1, 2, 3)]
+        [(5, HALF, NZ), (12, HALF, NZ)],
+        chip, *x_got, my, p0, scratch=[(4, 6, HALF, NZ)], name="chips",
+    )
+    z_got = [swap(group, "gx", 8 * i) for i in Z_ORDER]
     u1, g1, h1, p1, f1 = call(
         functools.partial(z_ports_kernel, HALF),
         z_shapes, k, u, group, scratch=[(2, ROWS // 2, NZ)], name="z_ports",
@@ -533,7 +553,7 @@
         back_kernel,
         [(2, HALF, NZ), (2, HALF, NZ)],
         group, *z_got, chip_parts, core_parts, p1,
-        scratch=[(4, 5, HALF, NZ), (5, HALF, NZ)], name="back",
+        scratch=[(4, 5, HALF, NZ), (6, HALF, NZ)], name="back",
     )
     got = swap(send, "gx", 1)
     v, message = call(
@@ -542,7 +562,7 @@
         keep, got, base, gx, hx, my, iy, g0, g1, h0, h1, p0, p1,
         scratch=[(2, NY, NZ), (2, ROWS, NZ)], name="y_solve",
     )
-    l_got = [swap(message, "gz", i) for i in (1, 2, 3)]
+    l_got = [swap(message, "gz", i) for i in L_ORDER]
     yz, = call(z_local_kernel, [(NY, NX, NZ)], f0, f1, u0, u1, v, name="z_local")
     out, = call(
         final_kernel,

time: 44.5 us -> 39.5 us (0.89)
  starting transfers between devices: 20.5 us -> 17.8 us
  waiting for transfers between devices: 14.5 us -> 12.2 us
    ppermute x13, starting transfers between devices: 19.8 us -> 15.7 us  [swap(): return lax.ppermute(block, axis, [(i, i ^ mask) for i in range(n)])]
    ppermute x13, waiting for transfers between devices: 14.5 us -> 12.2 us  [swap(): return lax.ppermute(block, axis, [(i, i ^ mask) for i in range(n)])]
    ppermute x1, starting transfers between devices: 0.66 us -> 2.07 us  [per_device(): below = lax.ppermute(end, 'gx', [(i, below_target(i, n)) for i in range(n)])]
  transfers between devices with their start and end apart: 14 -> 14, of which waited for: 8 -> 9; matrix products, arithmetic and copies ran while one was open for 0% -> 0% of each run, Pallas kernels for 13% -> 15%
where the time goes in v4:
time: 39.5 us; the launch traced here: 39.4 us
  starting transfers between devices  17.8 us (45%)
  waiting for transfers between devices  12.2 us (31%)
  Pallas kernels  9.23 us (23%)
    ppermute x13, starting transfers between devices, swap(): return lax.ppermute(block, axis, [(i, i ^ mask) for i in range(n)])  15.7 us
    ppermute x13, waiting for transfers between devices, swap(): return lax.ppermute(block, axis, [(i, i ^ mask) for i in range(n)])  12.2 us
    pallas_call x12, Pallas kernels, call(): pl.pallas_call(kernel, out_shape=shapes, in_specs=[pl.BlockSpec(memory_sp...  9.23 us
    ppermute x1, starting transfers between devices, per_device(): below = lax.ppermute(end, 'gx', [(i, below_target(i, n)) for i in range(n)])  2.07 us
  transfers between devices with their start and end apart: 14, of which 9 were waited for; matrix products, arithmetic and copies ran while one was open for 0% of the time, Pallas kernels for 15%

profile of v4, /device:TPU:0, one launch (start us, length us, event | category | flops | bytes accessed | tf_op | source)
XLA Modules:
  0.0 39.4 jit_solution(4620982669429960472)
XLA Ops:
  0.0 1.4 %edges.1 = (f32[8,64,128]{2,1,0:T(8,128)S(1)}, f32[8,64,128]{2,1,0:T(8,128)S(1)}, f32[8,64,128]{2,1,0:T(8,128)S(1)}, f32[8,512]{1,0:T(8,128)S(1)}, f32[64,128]{1,0:T(8,128)S(1)}) custom-call(f32[8,64,128]{2,1,0:T(8,128)} %u_hbm.1, f32[8,64,128]{2,1,0:T(8,128)} %k_hbm.1, f32[8,64,128]{2,1,0:T(8,128)} %f_hbm.1), custom_call_target="tpu_custom_call" | custom-call | bytes 1622016 | tf_op jit(solution)/shard_map/edges/pallas_call | solution.py:26
  1.4 2.1 %collective-permute-start.2 = (f32[64,128]{1,0:T(8,128)S(1)}, f32[64,128]{1,0:T(8,128)S(1)}, u32[]{:S(2)}, u32[]{:S(2)}) collective-permute-start(f32[64,128]{1,0:T(8,128)S(1)} %get-tuple-element.42), channel_id=1, source_target_pairs={{0,32},{4,8},{8,4},{12,16},{16,12},{20,24},{24,20},{28,60},{32,64}... | collective-permute-start | bytes 98312 | tf_op jit(solution)/shard_map/ppermute | solution.py:520
  3.4 1.6 %collective-permute-start = (f32[8,512]{1,0:T(8,128)S(1)}, f32[8,512]{1,0:T(8,128)S(1)}, u32[]{:S(2)}, u32[]{:S(2)}) collective-permute-start(f32[8,512]{1,0:T(8,128)S(1)} %get-tuple-element.41.own_ref), channel_id=1, source_target_pairs={{0,1},{1,0},{2,3},{3,2},{4,5},{5,4},{6,7},{7,6},{8,9},{9,8},{10,11... | collective-permute-start | bytes 49160 | tf_op jit(solution)/shard_map/ppermute | solution.py:501
  5.0 2.2 %collective-permute-start.1 = (f32[8,512]{1,0:T(8,128)S(1)}, f32[8,512]{1,0:T(8,128)S(1)}, u32[]{:S(2)}, u32[]{:S(2)}) collective-permute-start(f32[8,512]{1,0:T(8,128)S(1)} %get-tuple-element.41.own_ref), channel_id=1, source_target_pairs={{0,3},{1,2},{2,1},{3,0},{4,7},{5,6},{6,5},{7,4},{8,11},{9,10},{10,... | collective-permute-start | bytes 49160 | tf_op jit(solution)/shard_map/ppermute | solution.py:501
  7.2 0.5 %local.1 = (f32[8,64,128]{2,1,0:T(8,128)S(1)}, f32[6,64,128]{2,1,0:T(8,128)S(1)}, f32[6,64,128]{2,1,0:T(8,128)S(1)}, f32[6,64,128]{2,1,0:T(8,128)S(1)}, f32[3,64,128]{2,1,0:T(8,128)S(1)}) custom-call(f32[8,64,128]{2,1,0:T(8,128)S(1)} %get-tuple-element.43.u_ref, f32[8,64,128]{2,1,0:T(8,128)S(1)} %get-tuple-element.44.k_ref, ...), custom_call_target="tpu_custom_call" | custom-call | bytes 1736704 | tf_op jit(solution)/shard_map/local/pallas_call | solution.py:26
  7.8 2.2 %collective-permute-done.1.two_ref = f32[8,512]{1,0:T(8,128)S(1)} collective-permute-done((f32[8,512]{1,0:T(8,128)S(1)}, f32[8,512]{1,0:T(8,128)S(1)}, u32[]{:S(2)}, u32[]{:S(2)}) %collective-permute-start.1) | collective-permute-done | bytes 16416 | tf_op jit(solution)/shard_map/ppermute | solution.py:501
  10.0 0.3 halo.1
  10.3 0.1 collective-permute-start.3
  10.4 1.3 %collective-permute-done.3.got_ref = f32[7,32,128]{2,1,0:T(8,128)S(1)} collective-permute-done((f32[7,32,128]{2,1,0:T(8,128)S(1)}, f32[7,32,128]{2,1,0:T(8,128)S(1)}, u32[]{:S(2)}, u32[]{:S(2)}) %collective-permute-start.3) | collective-permute-done | bytes 114720 | tf_op jit(solution)/shard_map/ppermute | solution.py:501
  11.7 1.4 %collective-permute-start.4 = (f32[6,32,128]{2,1,0:T(8,128)S(1)}, f32[6,32,128]{2,1,0:T(8,128)S(1)}, u32[]{:S(2)}, u32[]{:S(2)}) collective-permute-start(f32[6,32,128]{2,1,0:T(8,128)S(1)} %get-tuple-element.52.after_ref.own_ref), channel_id=1, source_target_pairs={{0,16},{4,20},{8,24},{12,28},{16,0},{20,4},{24,8},{28,12},{32,48},... | collective-permute-start | bytes 294920 | tf_op jit(solution)/shard_map/ppermute | solution.py:501
  13.2 1.0 %collective-permute-start.5 = (f32[6,32,128]{2,1,0:T(8,128)S(1)}, f32[6,32,128]{2,1,0:T(8,128)S(1)}, u32[]{:S(2)}, u32[]{:S(2)}) collective-permute-start(f32[6,32,128]{2,1,0:T(8,128)S(1)} %get-tuple-element.52.after_ref.own_ref), channel_id=1, source_target_pairs={{0,24},{4,28},{8,16},{12,20},{16,8},{20,12},{24,0},{28,4},{32,56},... | collective-permute-start | bytes 294920 | tf_op jit(solution)/shard_map/ppermute | solution.py:501
  14.2 1.1 %collective-permute-start.6 = (f32[6,32,128]{2,1,0:T(8,128)S(1)}, f32[6,32,128]{2,1,0:T(8,128)S(1)}, u32[]{:S(2)}, u32[]{:S(2)}) collective-permute-start(f32[6,32,128]{2,1,0:T(8,128)S(1)} %get-tuple-element.52.after_ref.own_ref), channel_id=1, source_target_pairs={{0,8},{4,12},{8,0},{12,4},{16,24},{20,28},{24,16},{28,20},{32,40},... | collective-permute-start | bytes 294920 | tf_op jit(solution)/shard_map/ppermute | solution.py:501
  15.3 0.5 %prepare.1 = (f32[64,8,128]{2,1,0:T(8,128)S(1)}, f32[64,8,128]{2,1,0:T(8,128)S(1)}, f32[64,8,128]{2,1,0:T(8,128)S(1)}, f32[64,8,128]{2,1,0:T(8,128)S(1)}, f32[64,8,128]{2,1,0:T(8,128)S(1)}) custom-call(f32[8,64,128]{2,1,0:T(8,128)S(1)} %get-tuple-element.43.u_ref, f32[8,64,128]{2,1,0:T(8,128)S(1)} %get-tuple-element.44.k_ref, ...), custom_call_target="tpu_custom_call" | custom-call | bytes 2621440 | tf_op jit(solution)/shard_map/prepare/pallas_call | solution.py:26
  15.9 1.7 %z_ports.2 = (f32[32,8,128]{2,1,0:T(8,128)S(1)}, f32[32,8,128]{2,1,0:T(8,128)S(1)}, f32[32,8,128]{2,1,0:T(8,128)S(1)}, f32[8,256]{1,0:T(8,128)S(1)}, f32[22,256,128]{2,1,0:T(8,128)S(1)}) custom-call(f32[8,64,128]{2,1,0:T(8,128)S(1)} %get-tuple-element.44.k_ref, f32[8,64,128]{2,1,0:T(8,128)S(1)} %get-tuple-element.43.u_ref, ...), custom_call_target="tpu_custom_call" | custom-call | bytes 3907584 | tf_op jit(solution)/shard_map/z_ports/pallas_call | solution.py:26
  17.5 0.8 %collective-permute-done.4.one_ref = f32[6,32,128]{2,1,0:T(8,128)S(1)} collective-permute-done((f32[6,32,128]{2,1,0:T(8,128)S(1)}, f32[6,32,128]{2,1,0:T(8,128)S(1)}, u32[]{:S(2)}, u32[]{:S(2)}) %collective-permute-start.4) | collective-permute-done | bytes 98336 | tf_op jit(solution)/shard_map/ppermute | solution.py:501
  18.3 2.0 %collective-permute-done.5.two_ref = f32[6,32,128]{2,1,0:T(8,128)S(1)} collective-permute-done((f32[6,32,128]{2,1,0:T(8,128)S(1)}, f32[6,32,128]{2,1,0:T(8,128)S(1)}, u32[]{:S(2)}, u32[]{:S(2)}) %collective-permute-start.5) | collective-permute-done | bytes 98336 | tf_op jit(solution)/shard_map/ppermute | solution.py:501
  20.3 0.1 chips.1
  20.4 3.7 %collective-permute-start.7 = (f32[5,32,128]{2,1,0:T(8,128)S(1)}, f32[5,32,128]{2,1,0:T(8,128)S(1)}, u32[]{:S(2)}, u32[]{:S(2)}) collective-permute-start(f32[5,32,128]{2,1,0:T(8,128)S(1)} %get-tuple-element.57.after_ref.own_ref), channel_id=1, source_target_pairs={{0,64},{4,68},{8,72},{12,76},{16,80},{20,84},{24,88},{28,92},{32,9... | collective-permute-start | bytes 245768 | tf_op jit(solution)/shard_map/ppermute | solution.py:501
  24.1 1.0 %collective-permute-start.8 = (f32[5,32,128]{2,1,0:T(8,128)S(1)}, f32[5,32,128]{2,1,0:T(8,128)S(1)}, u32[]{:S(2)}, u32[]{:S(2)}) collective-permute-start(f32[5,32,128]{2,1,0:T(8,128)S(1)} %get-tuple-element.57.after_ref.own_ref), channel_id=1, source_target_pairs={{0,96},{4,100},{8,104},{12,108},{16,112},{20,116},{24,120},{28,124... | collective-permute-start | bytes 245768 | tf_op jit(solution)/shard_map/ppermute | solution.py:501
  25.1 1.6 %z_ports.3 = (f32[32,8,128]{2,1,0:T(8,128)S(1)}, f32[32,8,128]{2,1,0:T(8,128)S(1)}, f32[32,8,128]{2,1,0:T(8,128)S(1)}, f32[8,256]{1,0:T(8,128)S(1)}, f32[22,256,128]{2,1,0:T(8,128)S(1)}) custom-call(f32[8,64,128]{2,1,0:T(8,128)S(1)} %get-tuple-element.44.k_ref, f32[8,64,128]{2,1,0:T(8,128)S(1)} %get-tuple-element.43.u_ref, ...), custom_call_target="tpu_custom_call" | custom-call | bytes 3891200 | tf_op jit(solution)/shard_map/z_ports/pallas_call | solution.py:26
  26.7 0.1 collective-permute-done.7.one_ref
  26.8 2.9 %collective-permute-done.8.two_ref = f32[5,32,128]{2,1,0:T(8,128)S(1)} collective-permute-done((f32[5,32,128]{2,1,0:T(8,128)S(1)}, f32[5,32,128]{2,1,0:T(8,128)S(1)}, u32[]{:S(2)}, u32[]{:S(2)}) %collective-permute-start.8) | collective-permute-done | bytes 81952 | tf_op jit(solution)/shard_map/ppermute | solution.py:501
  29.7 0.1 back.1
  29.9 1.2 %collective-permute-done.10.got_ref = f32[2,32,128]{2,1,0:T(8,128)S(1)} collective-permute-done((f32[2,32,128]{2,1,0:T(8,128)S(1)}, f32[2,32,128]{2,1,0:T(8,128)S(1)}, u32[]{:S(2)}, u32[]{:S(2)}) %collective-permute-start.10) | collective-permute-done | bytes 32800 | tf_op jit(solution)/shard_map/ppermute | solution.py:501
  31.1 0.4 %y_solve.1 = (f32[64,8,128]{2,1,0:T(8,128)S(1)}, f32[8,512]{1,0:T(8,128)S(1)}) custom-call(f32[2,32,128]{2,1,0:T(8,128)S(1)} %get-tuple-element.61.keep_ref, f32[2,32,128]{2,1,0:T(8,128)S(1)} %collective-permute-done.10.got_ref, f32[64,8,128]{2,1,0:T(8,128)S(1)} %get-tuple-element.63.base_ref, f32[64,8,128]{2,1,0:T(8,128)S(1)} %get-tuple-element.64.gx_ref, ...), custom_call_target="tpu_custom_call" | custom-call | bytes 2195456 | tf_op jit(solution)/shard_map/y_solve/pallas_call | solution.py:26
  31.6 1.8 %collective-permute-start.11 = (f32[8,512]{1,0:T(8,128)S(1)}, f32[8,512]{1,0:T(8,128)S(1)}, u32[]{:S(2)}, u32[]{:S(2)}) collective-permute-start(f32[8,512]{1,0:T(8,128)S(1)} %get-tuple-element.71.own_ref), channel_id=1, source_target_pairs={{0,2},{1,3},{2,0},{3,1},{4,6},{5,7},{6,4},{7,5},{8,10},{9,11},{10,... | collective-permute-start | bytes 49160 | tf_op jit(solution)/shard_map/ppermute | solution.py:501
  33.4 0.6 %collective-permute-start.12 = (f32[8,512]{1,0:T(8,128)S(1)}, f32[8,512]{1,0:T(8,128)S(1)}, u32[]{:S(2)}, u32[]{:S(2)}) collective-permute-start(f32[8,512]{1,0:T(8,128)S(1)} %get-tuple-element.71.own_ref), channel_id=1, source_target_pairs={{0,3},{1,2},{2,1},{3,0},{4,7},{5,6},{6,5},{7,4},{8,11},{9,10},{10,... | collective-permute-start | bytes 49160 | tf_op jit(solution)/shard_map/ppermute | solution.py:501
  34.0 1.2 %collective-permute-start.13 = (f32[8,512]{1,0:T(8,128)S(1)}, f32[8,512]{1,0:T(8,128)S(1)}, u32[]{:S(2)}, u32[]{:S(2)}) collective-permute-start(f32[8,512]{1,0:T(8,128)S(1)} %get-tuple-element.71.own_ref), channel_id=1, source_target_pairs={{0,1},{1,0},{2,3},{3,2},{4,5},{5,4},{6,7},{7,6},{8,9},{9,8},{10,11... | collective-permute-start | bytes 49160 | tf_op jit(solution)/shard_map/ppermute | solution.py:501
  35.2 1.4 %z_local.1.y_ref = f32[64,8,128]{2,1,0:T(8,128)S(1)} custom-call(f32[22,256,128]{2,1,0:T(8,128)S(1)} %get-tuple-element.72.f0_ref, f32[22,256,128]{2,1,0:T(8,128)S(1)} %get-tuple-element.73.f1_ref, f32[32,8,128]{2,1,0:T(8,128)S(1)} %get-tuple-element.74.u0_ref, f32[32,8,128]{2,1,0:T(8,128)S(1)} %get-tuple-element.75.u1_ref, ...), custom_call_target="tpu_custom_call" | custom-call | bytes 6553600 | tf_op jit(solution)/shard_map/z_local/pallas_call | solution.py:26
  36.5 0.4 collective-permute-done.11.one_ref
  36.9 1.4 %collective-permute-done.12.two_ref = f32[8,512]{1,0:T(8,128)S(1)} collective-permute-done((f32[8,512]{1,0:T(8,128)S(1)}, f32[8,512]{1,0:T(8,128)S(1)}, u32[]{:S(2)}, u32[]{:S(2)}) %collective-permute-start.12) | collective-permute-done | bytes 16416 | tf_op jit(solution)/shard_map/ppermute | solution.py:501
  38.3 1.1 %final.1 = f32[8,64,128]{2,1,0:T(8,128)} custom-call(f32[8,512]{1,0:T(8,128)S(1)} %get-tuple-element.71.own_ref, f32[8,512]{1,0:T(8,128)S(1)} %collective-permute-done.11.one_ref, f32[8,512]{1,0:T(8,128)S(1)} %collective-permute-done.12.two_ref, f32[8,512]{1,0:T(8,128)S(1)} %collective-permute-done.13.three_ref, f32[64,8,128]{2,1,0:T(8,128)S(1)} %z_local.1.y_ref, ...), custom_call_target="tpu_custom_call" | custom-call | bytes 1114112 | tf_op jit(solution)/shard_map/final/pallas_call | solution.py:26
  (8 shorter events, 0.2 us)
Async XLA Ops:
  1.4 8.6 %collective-permute-start.2 = (f32[64,128]{1,0:T(8,128)S(1)}, f32[64,128]{1,0:T(8,128)S(1)}, u32[]{:S(2)}, u32[]{:S(2)}) collective-permute-start(f32[64,128]{1,0:T(8,128)S(1)} %get-tuple-element.42), channel_id=1, source_target_pairs={{0,32},{4,8},{8,4},{12,16},{16,12},{20,24},{24,20},{28,60},{32,64}... | collective-permute-start | bytes 98312 | tf_op jit(solution)/shard_map/ppermute | solution.py:520
  3.4 4.3 %collective-permute-start = (f32[8,512]{1,0:T(8,128)S(1)}, f32[8,512]{1,0:T(8,128)S(1)}, u32[]{:S(2)}, u32[]{:S(2)}) collective-permute-start(f32[8,512]{1,0:T(8,128)S(1)} %get-tuple-element.41.own_ref), channel_id=1, source_target_pairs={{0,1},{1,0},{2,3},{3,2},{4,5},{5,4},{6,7},{7,6},{8,9},{9,8},{10,11... | collective-permute-start | bytes 49160 | tf_op jit(solution)/shard_map/ppermute | solution.py:501
  5.0 4.9 %collective-permute-start.1 = (f32[8,512]{1,0:T(8,128)S(1)}, f32[8,512]{1,0:T(8,128)S(1)}, u32[]{:S(2)}, u32[]{:S(2)}) collective-permute-start(f32[8,512]{1,0:T(8,128)S(1)} %get-tuple-element.41.own_ref), channel_id=1, source_target_pairs={{0,3},{1,2},{2,1},{3,0},{4,7},{5,6},{6,5},{7,4},{8,11},{9,10},{10,... | collective-permute-start | bytes 49160 | tf_op jit(solution)/shard_map/ppermute | solution.py:501
  10.3 1.4 %collective-permute-start.3 = (f32[7,32,128]{2,1,0:T(8,128)S(1)}, f32[7,32,128]{2,1,0:T(8,128)S(1)}, u32[]{:S(2)}, u32[]{:S(2)}) collective-permute-start(f32[7,32,128]{2,1,0:T(8,128)S(1)} %get-tuple-element.51), channel_id=1, source_target_pairs={{0,4},{4,0},{8,12},{12,8},{16,20},{20,16},{24,28},{28,24},{32,36},... | collective-permute-start | bytes 344072 | tf_op jit(solution)/shard_map/ppermute | solution.py:501
  11.7 6.6 %collective-permute-start.4 = (f32[6,32,128]{2,1,0:T(8,128)S(1)}, f32[6,32,128]{2,1,0:T(8,128)S(1)}, u32[]{:S(2)}, u32[]{:S(2)}) collective-permute-start(f32[6,32,128]{2,1,0:T(8,128)S(1)} %get-tuple-element.52.after_ref.own_ref), channel_id=1, source_target_pairs={{0,16},{4,20},{8,24},{12,28},{16,0},{20,4},{24,8},{28,12},{32,48},... | collective-permute-start | bytes 294920 | tf_op jit(solution)/shard_map/ppermute | solution.py:501
  13.2 7.1 %collective-permute-start.5 = (f32[6,32,128]{2,1,0:T(8,128)S(1)}, f32[6,32,128]{2,1,0:T(8,128)S(1)}, u32[]{:S(2)}, u32[]{:S(2)}) collective-permute-start(f32[6,32,128]{2,1,0:T(8,128)S(1)} %get-tuple-element.52.after_ref.own_ref), channel_id=1, source_target_pairs={{0,24},{4,28},{8,16},{12,20},{16,8},{20,12},{24,0},{28,4},{32,56},... | collective-permute-start | bytes 294920 | tf_op jit(solution)/shard_map/ppermute | solution.py:501
  14.2 6.1 %collective-permute-start.6 = (f32[6,32,128]{2,1,0:T(8,128)S(1)}, f32[6,32,128]{2,1,0:T(8,128)S(1)}, u32[]{:S(2)}, u32[]{:S(2)}) collective-permute-start(f32[6,32,128]{2,1,0:T(8,128)S(1)} %get-tuple-element.52.after_ref.own_ref), channel_id=1, source_target_pairs={{0,8},{4,12},{8,0},{12,4},{16,24},{20,28},{24,16},{28,20},{32,40},... | collective-permute-start | bytes 294920 | tf_op jit(solution)/shard_map/ppermute | solution.py:501
  20.4 6.4 %collective-permute-start.7 = (f32[5,32,128]{2,1,0:T(8,128)S(1)}, f32[5,32,128]{2,1,0:T(8,128)S(1)}, u32[]{:S(2)}, u32[]{:S(2)}) collective-permute-start(f32[5,32,128]{2,1,0:T(8,128)S(1)} %get-tuple-element.57.after_ref.own_ref), channel_id=1, source_target_pairs={{0,64},{4,68},{8,72},{12,76},{16,80},{20,84},{24,88},{28,92},{32,9... | collective-permute-start | bytes 245768 | tf_op jit(solution)/shard_map/ppermute | solution.py:501
  24.1 5.7 %collective-permute-start.8 = (f32[5,32,128]{2,1,0:T(8,128)S(1)}, f32[5,32,128]{2,1,0:T(8,128)S(1)}, u32[]{:S(2)}, u32[]{:S(2)}) collective-permute-start(f32[5,32,128]{2,1,0:T(8,128)S(1)} %get-tuple-element.57.after_ref.own_ref), channel_id=1, source_target_pairs={{0,96},{4,100},{8,104},{12,108},{16,112},{20,116},{24,120},{28,124... | collective-permute-start | bytes 245768 | tf_op jit(solution)/shard_map/ppermute | solution.py:501
  25.1 4.6 %collective-permute-start.9 = (f32[5,32,128]{2,1,0:T(8,128)S(1)}, f32[5,32,128]{2,1,0:T(8,128)S(1)}, u32[]{:S(2)}, u32[]{:S(2)}) collective-permute-start(f32[5,32,128]{2,1,0:T(8,128)S(1)} %get-tuple-element.57.after_ref.own_ref), channel_id=1, source_target_pairs={{0,32},{4,36},{8,40},{12,44},{16,48},{20,52},{24,56},{28,60},{32,0... | collective-permute-start | bytes 245768 | tf_op jit(solution)/shard_map/ppermute | solution.py:501
  29.8 1.3 %collective-permute-start.10 = (f32[2,32,128]{2,1,0:T(8,128)S(1)}, f32[2,32,128]{2,1,0:T(8,128)S(1)}, u32[]{:S(2)}, u32[]{:S(2)}) collective-permute-start(f32[2,32,128]{2,1,0:T(8,128)S(1)} %get-tuple-element.62), channel_id=1, source_target_pairs={{0,4},{4,0},{8,12},{12,8},{16,20},{20,16},{24,28},{28,24},{32,36},... | collective-permute-start | bytes 98312 | tf_op jit(solution)/shard_map/ppermute | solution.py:501
  31.6 5.3 %collective-permute-start.11 = (f32[8,512]{1,0:T(8,128)S(1)}, f32[8,512]{1,0:T(8,128)S(1)}, u32[]{:S(2)}, u32[]{:S(2)}) collective-permute-start(f32[8,512]{1,0:T(8,128)S(1)} %get-tuple-element.71.own_ref), channel_id=1, source_target_pairs={{0,2},{1,3},{2,0},{3,1},{4,6},{5,7},{6,4},{7,5},{8,10},{9,11},{10,... | collective-permute-start | bytes 49160 | tf_op jit(solution)/shard_map/ppermute | solution.py:501
  33.4 4.9 %collective-permute-start.12 = (f32[8,512]{1,0:T(8,128)S(1)}, f32[8,512]{1,0:T(8,128)S(1)}, u32[]{:S(2)}, u32[]{:S(2)}) collective-permute-start(f32[8,512]{1,0:T(8,128)S(1)} %get-tuple-element.71.own_ref), channel_id=1, source_target_pairs={{0,3},{1,2},{2,1},{3,0},{4,7},{5,6},{6,5},{7,4},{8,11},{9,10},{10,... | collective-permute-start | bytes 49160 | tf_op jit(solution)/shard_map/ppermute | solution.py:501
  34.0 4.3 %collective-permute-start.13 = (f32[8,512]{1,0:T(8,128)S(1)}, f32[8,512]{1,0:T(8,128)S(1)}, u32[]{:S(2)}, u32[]{:S(2)}) collective-permute-start(f32[8,512]{1,0:T(8,128)S(1)} %get-tuple-element.71.own_ref), channel_id=1, source_target_pairs={{0,1},{1,0},{2,3},{3,2},{4,5},{5,4},{6,7},{7,6},{8,9},{9,8},{10,11... | collective-permute-start | bytes 49160 | tf_op jit(solution)/shard_map/ppermute | solution.py:501

commit v5 on v4

--- a/solution.py
+++ b/solution.py
@@ -10,7 +10,6 @@
 NX, NY, NZ = 8, 64, 128
 ROWS = NX * NY
 HALF = NY // 2
-X_ORDER, Z_ORDER, L_ORDER = (2, 3, 1), (2, 3, 1), (2, 3, 1)
 RING = 8
 CX = 0.25 * 16.0 * NX * NX
 CY = 0.25 * 2.0
@@ -18,6 +17,17 @@
 F32 = jnp.float32
 VMEM_LIMIT = 24 * 1024 * 1024
 BF16 = jnp.bfloat16
+X_ORDER, Z_ORDER, L_ORDER = ((2, 3), (3, 2), (1, 1)), ((2, 3), (3, 2), (1, 1)), ((3, 3), (2, 2), (1, 1))
+X_FLIP, Z_FLIP = 2, 2
+
+
+def flips(distance, bits):
+    both = distance & bits
+    return (both ^ (both >> 1)) & 1
+
+
+def half_of(index):
+    return (index & 1) ^ flips((index >> 1) & 3, X_FLIP) ^ flips(index >> 3, Z_FLIP)
 
 
 def call(kernel, outs, *args, scratch=(), sems=0, ins_in=pltpu.VMEM, outs_in=pltpu.VMEM, flops=0, name=None):
@@ -200,7 +210,8 @@
     inner = jnp.where(core == 0, NX - 1, 0)
     place = lax.rem(index, RING)
     inside = jnp.where(index >= RING, 1.0, 0.0)
-    for which, out in ((core, keep_ref), (1 - core, send_ref)):
+    half = half_of(index)
+    for which, out in ((half, keep_ref), (1 - half, send_ref)):
         ys = pl.ds(pl.multiple_of(which * HALF, HALF), HALF)
         r_h = rp_ref[0, ys] + fix_ref[0, ys]
         rr = rp_ref[1, ys] + fix_ref[1, ys]
@@ -237,8 +248,9 @@
 
 
 def ordered(me, refs, order, held):
-    for i, ref in zip((0,) + order, refs):
-        held[jnp.bitwise_xor(me, i)] = ref[...]
+    half = half_of(lax.axis_index("gx"))
+    for pair, ref in zip(((0, 0),) + order, refs):
+        held[jnp.bitwise_xor(me, jnp.where(half == 0, pair[0], pair[1]))] = ref[...]
 
 
 def chips_kernel(own_ref, one_ref, two_ref, three_ref, after_ref, also_ref, out_ref, parts_ref, held):
@@ -387,10 +399,10 @@
 
 
 def y_kernel(keep_ref, got_ref, base_ref, gx_ref, hx_ref, my_ref, iy_ref, g0_ref, g1_ref, h0_ref, h1_ref, p0_ref, p1_ref, v_ref, out_ref, b_ref, d_ref):
-    core = lax.rem(lax.axis_index("gx"), 2)
+    half = half_of(lax.axis_index("gx"))
     for i in range(2):
-        b_ref[i, pl.ds(pl.multiple_of(core * HALF, HALF), HALF)] = keep_ref[i]
-        b_ref[i, pl.ds(pl.multiple_of((1 - core) * HALF, HALF), HALF)] = got_ref[i]
+        b_ref[i, pl.ds(pl.multiple_of(half * HALF, HALF), HALF)] = keep_ref[i]
+        b_ref[i, pl.ds(pl.multiple_of((1 - half) * HALF, HALF), HALF)] = got_ref[i]
 
     def at(y):
         first = jnp.broadcast_to(b_ref[0, y : y + 1, :], (NX, NZ))
@@ -501,9 +513,22 @@
     return lax.ppermute(block, axis, [(i, i ^ mask) for i in range(n)])
 
 
+def gather(block, unit, order, bits):
+    got = []
+    for pair in order:
+        route = []
+        for i in range(lax.axis_size("gx")):
+            distance = pair[half_of(i)]
+            route.append((i, i ^ (unit * distance) ^ flips(distance, bits)))
+        got.append(lax.ppermute(block, "gx", route))
+    return got
+
+
 def below_target(i, n):
     place = i % RING
-    if place in (0, RING - 1):
+    if place == 0:
+        return i ^ RING
+    if place == RING - 1:
         return (i + RING) % n
     return i + 1 if place % 2 else i - 1
 
@@ -516,7 +541,13 @@
         [(NX, NY, NZ)] * 3 + [(8, ROWS), (NY, NZ)],
         u, k, f, sems=3, ins_in=pltpu.HBM, name="edges",
     )
-    one, two = swap(edges, "gz", 1), swap(edges, "gz", 3)
+    nz = lax.axis_size("gz")
+    inner = [
+        (i * nz + j, (i ^ 1) * nz + j if j in (0, nz - 1) else i * nz + (j ^ 3))
+        for i in range(n)
+        for j in range(nz)
+    ]
+    one, two = swap(edges, "gz", 1), lax.ppermute(edges, ("gx", "gz"), inner)
     below = lax.ppermute(end, "gx", [(i, below_target(i, n)) for i in range(n)])
     rp, a, m, inv, ew = call(
         local_kernel,
@@ -530,7 +561,7 @@
     )
     got = swap(send, "gx", 1)
     chip, core_parts = call(core_kernel, [(6, HALF, NZ), (9, HALF, NZ)], keep, got, name="core")
-    x_got = [swap(chip, "gx", 2 * i) for i in X_ORDER]
+    x_got = gather(chip, 2, X_ORDER, X_FLIP)
     base, gx, hx, my, iy = call(
         prepare_kernel, [(NY, NX, NZ)] * 5, u, k, a, m, inv, rr, name="prepare"
     )
@@ -544,7 +575,7 @@
         [(5, HALF, NZ), (12, HALF, NZ)],
         chip, *x_got, my, p0, scratch=[(4, 6, HALF, NZ)], name="chips",
     )
-    z_got = [swap(group, "gx", 8 * i) for i in Z_ORDER]
+    z_got = gather(group, 8, Z_ORDER, Z_FLIP)
     u1, g1, h1, p1, f1 = call(
         functools.partial(z_ports_kernel, HALF),
         z_shapes, k, u, group, scratch=[(2, ROWS // 2, NZ)], name="z_ports",
@@ -562,7 +593,7 @@
         keep, got, base, gx, hx, my, iy, g0, g1, h0, h1, p0, p1,
         scratch=[(2, NY, NZ), (2, ROWS, NZ)], name="y_solve",
     )
-    l_got = [swap(message, "gz", i) for i in L_ORDER]
+    l_got = [swap(message, "gz", i) for i, _ in L_ORDER]
     yz, = call(z_local_kernel, [(NY, NX, NZ)], f0, f1, u0, u1, v, name="z_local")
     out, = call(
         final_kernel,

time: 39.5 us -> 38.1 us (0.965)
  starting transfers between devices: 17.8 us -> 15 us
  waiting for transfers between devices: 12.2 us -> 13.6 us
    ppermute x13 -> x6, starting transfers between devices: 15.7 us -> 6.4 us  [swap(): return lax.ppermute(block, axis, [(i, i ^ mask) for i in range(n)])]
    ppermute x0 -> x7, waiting for transfers between devices: none -> 7.13 us  [the longest x6 7.12 us: gather(): got.append(lax.ppermute(block, 'gx', route))]
    ppermute x0 -> x7, starting transfers between devices: none -> 6.58 us  [the longest x6 6.58 us: gather(): got.append(lax.ppermute(block, 'gx', route))]
    ppermute x13 -> x6, waiting for transfers between devices: 12.2 us -> 6.44 us  [swap(): return lax.ppermute(block, axis, [(i, i ^ mask) for i in range(n)])]
  transfers between devices with their start and end apart: 14 -> 14, of which waited for: 9 -> 8; matrix products, arithmetic and copies ran while one was open for 0% -> 0% of each run, Pallas kernels for 15% -> 15%
where the time goes in v5:
time: 38.1 us; the launch traced here: 37.9 us
  starting transfers between devices  15 us (39%)
  waiting for transfers between devices  13.6 us (36%)
  Pallas kernels  9.2 us (24%)
    pallas_call x12, Pallas kernels, call(): pl.pallas_call(kernel, out_shape=shapes, in_specs=[pl.BlockSpec(memory_sp...  9.2 us
    ppermute x6, waiting for transfers between devices, gather(): got.append(lax.ppermute(block, 'gx', route))  7.12 us
    ppermute x6, starting transfers between devices, gather(): got.append(lax.ppermute(block, 'gx', route))  6.58 us
    ppermute x6, waiting for transfers between devices, swap(): return lax.ppermute(block, axis, [(i, i ^ mask) for i in range(n)])  6.44 us
    ppermute x6, starting transfers between devices, swap(): return lax.ppermute(block, axis, [(i, i ^ mask) for i in range(n)])  6.4 us
    ppermute x1, starting transfers between devices, per_device(): below = lax.ppermute(end, 'gx', [(i, below_target(i, n)) for i in range(n)])  2.06 us
  transfers between devices with their start and end apart: 14, of which 8 were waited for; matrix products, arithmetic and copies ran while one was open for 0% of the time, Pallas kernels for 15%

profile of v5, /device:TPU:0, one launch (start us, length us, event | category | flops | bytes accessed | tf_op | source)
XLA Modules:
  0.0 37.9 jit_solution(14636597414622321029)
XLA Ops:
  0.0 1.4 %edges.1 = (f32[8,64,128]{2,1,0:T(8,128)S(1)}, f32[8,64,128]{2,1,0:T(8,128)S(1)}, f32[8,64,128]{2,1,0:T(8,128)S(1)}, f32[8,512]{1,0:T(8,128)S(1)}, f32[64,128]{1,0:T(8,128)S(1)}) custom-call(f32[8,64,128]{2,1,0:T(8,128)} %u_hbm.1, f32[8,64,128]{2,1,0:T(8,128)} %k_hbm.1, f32[8,64,128]{2,1,0:T(8,128)} %f_hbm.1), custom_call_target="tpu_custom_call" | custom-call | bytes 1622016 | tf_op jit(solution)/shard_map/edges/pallas_call | solution.py:36
  1.4 2.1 %collective-permute-start.2 = (f32[64,128]{1,0:T(8,128)S(1)}, f32[64,128]{1,0:T(8,128)S(1)}, u32[]{:S(2)}, u32[]{:S(2)}) collective-permute-start(f32[64,128]{1,0:T(8,128)S(1)} %get-tuple-element.42), channel_id=1, source_target_pairs={{0,32},{4,8},{8,4},{12,16},{16,12},{20,24},{24,20},{28,60},{32,0},... | collective-permute-start | bytes 98312 | tf_op jit(solution)/shard_map/ppermute | solution.py:551
  3.4 1.6 %collective-permute-start = (f32[8,512]{1,0:T(8,128)S(1)}, f32[8,512]{1,0:T(8,128)S(1)}, u32[]{:S(2)}, u32[]{:S(2)}) collective-permute-start(f32[8,512]{1,0:T(8,128)S(1)} %get-tuple-element.41.own_ref), channel_id=1, source_target_pairs={{0,1},{1,0},{2,3},{3,2},{4,5},{5,4},{6,7},{7,6},{8,9},{9,8},{10,11... | collective-permute-start | bytes 49160 | tf_op jit(solution)/shard_map/ppermute | solution.py:513
  5.0 0.5 %local.1 = (f32[8,64,128]{2,1,0:T(8,128)S(1)}, f32[6,64,128]{2,1,0:T(8,128)S(1)}, f32[6,64,128]{2,1,0:T(8,128)S(1)}, f32[6,64,128]{2,1,0:T(8,128)S(1)}, f32[3,64,128]{2,1,0:T(8,128)S(1)}) custom-call(f32[8,64,128]{2,1,0:T(8,128)S(1)} %get-tuple-element.43.u_ref, f32[8,64,128]{2,1,0:T(8,128)S(1)} %get-tuple-element.44.k_ref, ...), custom_call_target="tpu_custom_call" | custom-call | bytes 1736704 | tf_op jit(solution)/shard_map/local/pallas_call | solution.py:36
  5.6 1.6 %collective-permute-done.one_ref = f32[8,512]{1,0:T(8,128)S(1)} collective-permute-done((f32[8,512]{1,0:T(8,128)S(1)}, f32[8,512]{1,0:T(8,128)S(1)}, u32[]{:S(2)}, u32[]{:S(2)}) %collective-permute-start) | collective-permute-done | bytes 16416 | tf_op jit(solution)/shard_map/ppermute | solution.py:513
  7.2 0.3 halo.1
  7.5 0.1 collective-permute-start.3
  7.6 1.3 %collective-permute-done.3.got_ref = f32[7,32,128]{2,1,0:T(8,128)S(1)} collective-permute-done((f32[7,32,128]{2,1,0:T(8,128)S(1)}, f32[7,32,128]{2,1,0:T(8,128)S(1)}, u32[]{:S(2)}, u32[]{:S(2)}) %collective-permute-start.3) | collective-permute-done | bytes 114720 | tf_op jit(solution)/shard_map/ppermute | solution.py:513
  8.9 0.1 core.1
  8.9 1.0 %collective-permute-start.4 = (f32[6,32,128]{2,1,0:T(8,128)S(1)}, f32[6,32,128]{2,1,0:T(8,128)S(1)}, u32[]{:S(2)}, u32[]{:S(2)}) collective-permute-start(f32[6,32,128]{2,1,0:T(8,128)S(1)} %get-tuple-element.52.after_ref.own_ref), channel_id=1, source_target_pairs={{0,20},{4,24},{8,28},{12,16},{16,12},{20,0},{24,4},{28,8},{32,52},... | collective-permute-start | bytes 294920 | tf_op jit(solution)/shard_map/ppermute | solution.py:523
  10.0 1.1 %collective-permute-start.5 = (f32[6,32,128]{2,1,0:T(8,128)S(1)}, f32[6,32,128]{2,1,0:T(8,128)S(1)}, u32[]{:S(2)}, u32[]{:S(2)}) collective-permute-start(f32[6,32,128]{2,1,0:T(8,128)S(1)} %get-tuple-element.52.after_ref.own_ref), channel_id=1, source_target_pairs={{0,28},{4,16},{8,20},{12,24},{16,4},{20,8},{24,12},{28,0},{32,60},... | collective-permute-start | bytes 294920 | tf_op jit(solution)/shard_map/ppermute | solution.py:523
  11.1 1.1 %collective-permute-start.6 = (f32[6,32,128]{2,1,0:T(8,128)S(1)}, f32[6,32,128]{2,1,0:T(8,128)S(1)}, u32[]{:S(2)}, u32[]{:S(2)}) collective-permute-start(f32[6,32,128]{2,1,0:T(8,128)S(1)} %get-tuple-element.52.after_ref.own_ref), channel_id=1, source_target_pairs={{0,8},{4,12},{8,0},{12,4},{16,24},{20,28},{24,16},{28,20},{32,40},... | collective-permute-start | bytes 294920 | tf_op jit(solution)/shard_map/ppermute | solution.py:523
  12.2 0.5 %prepare.1 = (f32[64,8,128]{2,1,0:T(8,128)S(1)}, f32[64,8,128]{2,1,0:T(8,128)S(1)}, f32[64,8,128]{2,1,0:T(8,128)S(1)}, f32[64,8,128]{2,1,0:T(8,128)S(1)}, f32[64,8,128]{2,1,0:T(8,128)S(1)}) custom-call(f32[8,64,128]{2,1,0:T(8,128)S(1)} %get-tuple-element.43.u_ref, f32[8,64,128]{2,1,0:T(8,128)S(1)} %get-tuple-element.44.k_ref, ...), custom_call_target="tpu_custom_call" | custom-call | bytes 2621440 | tf_op jit(solution)/shard_map/prepare/pallas_call | solution.py:36
  12.8 1.7 %z_ports.2 = (f32[32,8,128]{2,1,0:T(8,128)S(1)}, f32[32,8,128]{2,1,0:T(8,128)S(1)}, f32[32,8,128]{2,1,0:T(8,128)S(1)}, f32[8,256]{1,0:T(8,128)S(1)}, f32[22,256,128]{2,1,0:T(8,128)S(1)}) custom-call(f32[8,64,128]{2,1,0:T(8,128)S(1)} %get-tuple-element.44.k_ref, f32[8,64,128]{2,1,0:T(8,128)S(1)} %get-tuple-element.43.u_ref, ...), custom_call_target="tpu_custom_call" | custom-call | bytes 3907584 | tf_op jit(solution)/shard_map/z_ports/pallas_call | solution.py:36
  14.4 0.2 collective-permute-done.4.one_ref
  14.7 3.1 %collective-permute-done.5.two_ref = f32[6,32,128]{2,1,0:T(8,128)S(1)} collective-permute-done((f32[6,32,128]{2,1,0:T(8,128)S(1)}, f32[6,32,128]{2,1,0:T(8,128)S(1)}, u32[]{:S(2)}, u32[]{:S(2)}) %collective-permute-start.5) | collective-permute-done | bytes 98336 | tf_op jit(solution)/shard_map/ppermute | solution.py:523
  17.7 0.1 chips.1
  17.8 2.8 %collective-permute-start.7 = (f32[5,32,128]{2,1,0:T(8,128)S(1)}, f32[5,32,128]{2,1,0:T(8,128)S(1)}, u32[]{:S(2)}, u32[]{:S(2)}) collective-permute-start(f32[5,32,128]{2,1,0:T(8,128)S(1)} %get-tuple-element.57.after_ref.own_ref), channel_id=1, source_target_pairs={{0,68},{4,96},{8,76},{12,104},{16,116},{20,80},{24,124},{28,88},{3... | collective-permute-start | bytes 245768 | tf_op jit(solution)/shard_map/ppermute | solution.py:523
  20.6 0.3 collective-permute-start.8
  21.0 0.1 collective-permute-start.9
  21.1 1.6 %z_ports.3 = (f32[32,8,128]{2,1,0:T(8,128)S(1)}, f32[32,8,128]{2,1,0:T(8,128)S(1)}, f32[32,8,128]{2,1,0:T(8,128)S(1)}, f32[8,256]{1,0:T(8,128)S(1)}, f32[22,256,128]{2,1,0:T(8,128)S(1)}) custom-call(f32[8,64,128]{2,1,0:T(8,128)S(1)} %get-tuple-element.44.k_ref, f32[8,64,128]{2,1,0:T(8,128)S(1)} %get-tuple-element.43.u_ref, ...), custom_call_target="tpu_custom_call" | custom-call | bytes 3891200 | tf_op jit(solution)/shard_map/z_ports/pallas_call | solution.py:36
  22.8 0.6 %collective-permute-done.7.one_ref = f32[5,32,128]{2,1,0:T(8,128)S(1)} collective-permute-done((f32[5,32,128]{2,1,0:T(8,128)S(1)}, f32[5,32,128]{2,1,0:T(8,128)S(1)}, u32[]{:S(2)}, u32[]{:S(2)}) %collective-permute-start.7) | collective-permute-done | bytes 81952 | tf_op jit(solution)/shard_map/ppermute | solution.py:523
  23.4 3.2 %collective-permute-done.8.two_ref = f32[5,32,128]{2,1,0:T(8,128)S(1)} collective-permute-done((f32[5,32,128]{2,1,0:T(8,128)S(1)}, f32[5,32,128]{2,1,0:T(8,128)S(1)}, u32[]{:S(2)}, u32[]{:S(2)}) %collective-permute-start.8) | collective-permute-done | bytes 81952 | tf_op jit(solution)/shard_map/ppermute | solution.py:523
  26.6 0.1 back.1
  26.7 0.1 collective-permute-start.10
  26.8 1.2 %collective-permute-done.10.got_ref = f32[2,32,128]{2,1,0:T(8,128)S(1)} collective-permute-done((f32[2,32,128]{2,1,0:T(8,128)S(1)}, f32[2,32,128]{2,1,0:T(8,128)S(1)}, u32[]{:S(2)}, u32[]{:S(2)}) %collective-permute-start.10) | collective-permute-done | bytes 32800 | tf_op jit(solution)/shard_map/ppermute | solution.py:513
  28.0 0.4 %y_solve.1 = (f32[64,8,128]{2,1,0:T(8,128)S(1)}, f32[8,512]{1,0:T(8,128)S(1)}) custom-call(f32[2,32,128]{2,1,0:T(8,128)S(1)} %get-tuple-element.61.keep_ref, f32[2,32,128]{2,1,0:T(8,128)S(1)} %collective-permute-done.10.got_ref, f32[64,8,128]{2,1,0:T(8,128)S(1)} %get-tuple-element.63.base_ref, f32[64,8,128]{2,1,0:T(8,128)S(1)} %get-tuple-element.64.gx_ref, ...), custom_call_target="tpu_custom_call" | custom-call | bytes 2195456 | tf_op jit(solution)/shard_map/y_solve/pallas_call | solution.py:36
  28.5 3.1 %collective-permute-start.11 = (f32[8,512]{1,0:T(8,128)S(1)}, f32[8,512]{1,0:T(8,128)S(1)}, u32[]{:S(2)}, u32[]{:S(2)}) collective-permute-start(f32[8,512]{1,0:T(8,128)S(1)} %get-tuple-element.71.own_ref), channel_id=1, source_target_pairs={{0,3},{1,2},{2,1},{3,0},{4,7},{5,6},{6,5},{7,4},{8,11},{9,10},{10,... | collective-permute-start | bytes 49160 | tf_op jit(solution)/shard_map/ppermute | solution.py:513
  31.5 1.6 %collective-permute-start.12 = (f32[8,512]{1,0:T(8,128)S(1)}, f32[8,512]{1,0:T(8,128)S(1)}, u32[]{:S(2)}, u32[]{:S(2)}) collective-permute-start(f32[8,512]{1,0:T(8,128)S(1)} %get-tuple-element.71.own_ref), channel_id=1, source_target_pairs={{0,2},{1,3},{2,0},{3,1},{4,6},{5,7},{6,4},{7,5},{8,10},{9,11},{10,... | collective-permute-start | bytes 49160 | tf_op jit(solution)/shard_map/ppermute | solution.py:513
  33.1 1.4 %z_local.1.y_ref = f32[64,8,128]{2,1,0:T(8,128)S(1)} custom-call(f32[22,256,128]{2,1,0:T(8,128)S(1)} %get-tuple-element.72.f0_ref, f32[22,256,128]{2,1,0:T(8,128)S(1)} %get-tuple-element.73.f1_ref, f32[32,8,128]{2,1,0:T(8,128)S(1)} %get-tuple-element.74.u0_ref, f32[32,8,128]{2,1,0:T(8,128)S(1)} %get-tuple-element.75.u1_ref, ...), custom_call_target="tpu_custom_call" | custom-call | bytes 6553600 | tf_op jit(solution)/shard_map/z_local/pallas_call | solution.py:36
  34.5 2.3 %collective-permute-done.12.two_ref = f32[8,512]{1,0:T(8,128)S(1)} collective-permute-done((f32[8,512]{1,0:T(8,128)S(1)}, f32[8,512]{1,0:T(8,128)S(1)}, u32[]{:S(2)}, u32[]{:S(2)}) %collective-permute-start.12) | collective-permute-done | bytes 16416 | tf_op jit(solution)/shard_map/ppermute | solution.py:513
  36.8 1.1 %final.1 = f32[8,64,128]{2,1,0:T(8,128)} custom-call(f32[8,512]{1,0:T(8,128)S(1)} %get-tuple-element.71.own_ref, f32[8,512]{1,0:T(8,128)S(1)} %collective-permute-done.11.one_ref, f32[8,512]{1,0:T(8,128)S(1)} %collective-permute-done.12.two_ref, f32[8,512]{1,0:T(8,128)S(1)} %collective-permute-done.13.three_ref, f32[64,8,128]{2,1,0:T(8,128)S(1)} %z_local.1.y_ref, ...), custom_call_target="tpu_custom_call" | custom-call | bytes 1114112 | tf_op jit(solution)/shard_map/final/pallas_call | solution.py:36
  (8 shorter events, 0.1 us)
Async XLA Ops:
  1.4 5.8 %collective-permute-start.2 = (f32[64,128]{1,0:T(8,128)S(1)}, f32[64,128]{1,0:T(8,128)S(1)}, u32[]{:S(2)}, u32[]{:S(2)}) collective-permute-start(f32[64,128]{1,0:T(8,128)S(1)} %get-tuple-element.42), channel_id=1, source_target_pairs={{0,32},{4,8},{8,4},{12,16},{16,12},{20,24},{24,20},{28,60},{32,0},... | collective-permute-start | bytes 98312 | tf_op jit(solution)/shard_map/ppermute | solution.py:551
  3.4 3.7 %collective-permute-start = (f32[8,512]{1,0:T(8,128)S(1)}, f32[8,512]{1,0:T(8,128)S(1)}, u32[]{:S(2)}, u32[]{:S(2)}) collective-permute-start(f32[8,512]{1,0:T(8,128)S(1)} %get-tuple-element.41.own_ref), channel_id=1, source_target_pairs={{0,1},{1,0},{2,3},{3,2},{4,5},{5,4},{6,7},{7,6},{8,9},{9,8},{10,11... | collective-permute-start | bytes 49160 | tf_op jit(solution)/shard_map/ppermute | solution.py:513
  5.0 2.2 %collective-permute-start.1 = (f32[8,512]{1,0:T(8,128)S(1)}, f32[8,512]{1,0:T(8,128)S(1)}, u32[]{:S(2)}, u32[]{:S(2)}) collective-permute-start(f32[8,512]{1,0:T(8,128)S(1)} %get-tuple-element.41.own_ref), channel_id=1, source_target_pairs={{0,4},{1,2},{2,1},{3,7},{4,0},{5,6},{6,5},{7,3},{8,12},{9,10},{10,... | collective-permute-start | bytes 49160 | tf_op jit(solution)/shard_map/ppermute | solution.py:550
  7.5 1.4 %collective-permute-start.3 = (f32[7,32,128]{2,1,0:T(8,128)S(1)}, f32[7,32,128]{2,1,0:T(8,128)S(1)}, u32[]{:S(2)}, u32[]{:S(2)}) collective-permute-start(f32[7,32,128]{2,1,0:T(8,128)S(1)} %get-tuple-element.51), channel_id=1, source_target_pairs={{0,4},{4,0},{8,12},{12,8},{16,20},{20,16},{24,28},{28,24},{32,36},... | collective-permute-start | bytes 344072 | tf_op jit(solution)/shard_map/ppermute | solution.py:513
  8.9 5.7 %collective-permute-start.4 = (f32[6,32,128]{2,1,0:T(8,128)S(1)}, f32[6,32,128]{2,1,0:T(8,128)S(1)}, u32[]{:S(2)}, u32[]{:S(2)}) collective-permute-start(f32[6,32,128]{2,1,0:T(8,128)S(1)} %get-tuple-element.52.after_ref.own_ref), channel_id=1, source_target_pairs={{0,20},{4,24},{8,28},{12,16},{16,12},{20,0},{24,4},{28,8},{32,52},... | collective-permute-start | bytes 294920 | tf_op jit(solution)/shard_map/ppermute | solution.py:523
  10.0 7.7 %collective-permute-start.5 = (f32[6,32,128]{2,1,0:T(8,128)S(1)}, f32[6,32,128]{2,1,0:T(8,128)S(1)}, u32[]{:S(2)}, u32[]{:S(2)}) collective-permute-start(f32[6,32,128]{2,1,0:T(8,128)S(1)} %get-tuple-element.52.after_ref.own_ref), channel_id=1, source_target_pairs={{0,28},{4,16},{8,20},{12,24},{16,4},{20,8},{24,12},{28,0},{32,60},... | collective-permute-start | bytes 294920 | tf_op jit(solution)/shard_map/ppermute | solution.py:523
  11.1 6.6 %collective-permute-start.6 = (f32[6,32,128]{2,1,0:T(8,128)S(1)}, f32[6,32,128]{2,1,0:T(8,128)S(1)}, u32[]{:S(2)}, u32[]{:S(2)}) collective-permute-start(f32[6,32,128]{2,1,0:T(8,128)S(1)} %get-tuple-element.52.after_ref.own_ref), channel_id=1, source_target_pairs={{0,8},{4,12},{8,0},{12,4},{16,24},{20,28},{24,16},{28,20},{32,40},... | collective-permute-start | bytes 294920 | tf_op jit(solution)/shard_map/ppermute | solution.py:523
  17.8 5.6 %collective-permute-start.7 = (f32[5,32,128]{2,1,0:T(8,128)S(1)}, f32[5,32,128]{2,1,0:T(8,128)S(1)}, u32[]{:S(2)}, u32[]{:S(2)}) collective-permute-start(f32[5,32,128]{2,1,0:T(8,128)S(1)} %get-tuple-element.57.after_ref.own_ref), channel_id=1, source_target_pairs={{0,68},{4,96},{8,76},{12,104},{16,116},{20,80},{24,124},{28,88},{3... | collective-permute-start | bytes 245768 | tf_op jit(solution)/shard_map/ppermute | solution.py:523
  20.6 6.0 %collective-permute-start.8 = (f32[5,32,128]{2,1,0:T(8,128)S(1)}, f32[5,32,128]{2,1,0:T(8,128)S(1)}, u32[]{:S(2)}, u32[]{:S(2)}) collective-permute-start(f32[5,32,128]{2,1,0:T(8,128)S(1)} %get-tuple-element.57.after_ref.own_ref), channel_id=1, source_target_pairs={{0,100},{4,64},{8,108},{12,72},{16,84},{20,112},{24,92},{28,120},{... | collective-permute-start | bytes 245768 | tf_op jit(solution)/shard_map/ppermute | solution.py:523
  21.0 5.6 %collective-permute-start.9 = (f32[5,32,128]{2,1,0:T(8,128)S(1)}, f32[5,32,128]{2,1,0:T(8,128)S(1)}, u32[]{:S(2)}, u32[]{:S(2)}) collective-permute-start(f32[5,32,128]{2,1,0:T(8,128)S(1)} %get-tuple-element.57.after_ref.own_ref), channel_id=1, source_target_pairs={{0,32},{4,36},{8,40},{12,44},{16,48},{20,52},{24,56},{28,60},{32,0... | collective-permute-start | bytes 245768 | tf_op jit(solution)/shard_map/ppermute | solution.py:523
  26.7 1.3 %collective-permute-start.10 = (f32[2,32,128]{2,1,0:T(8,128)S(1)}, f32[2,32,128]{2,1,0:T(8,128)S(1)}, u32[]{:S(2)}, u32[]{:S(2)}) collective-permute-start(f32[2,32,128]{2,1,0:T(8,128)S(1)} %get-tuple-element.62), channel_id=1, source_target_pairs={{0,4},{4,0},{8,12},{12,8},{16,20},{20,16},{24,28},{28,24},{32,36},... | collective-permute-start | bytes 98312 | tf_op jit(solution)/shard_map/ppermute | solution.py:513
  28.5 6.0 %collective-permute-start.11 = (f32[8,512]{1,0:T(8,128)S(1)}, f32[8,512]{1,0:T(8,128)S(1)}, u32[]{:S(2)}, u32[]{:S(2)}) collective-permute-start(f32[8,512]{1,0:T(8,128)S(1)} %get-tuple-element.71.own_ref), channel_id=1, source_target_pairs={{0,3},{1,2},{2,1},{3,0},{4,7},{5,6},{6,5},{7,4},{8,11},{9,10},{10,... | collective-permute-start | bytes 49160 | tf_op jit(solution)/shard_map/ppermute | solution.py:513
  31.5 5.2 %collective-permute-start.12 = (f32[8,512]{1,0:T(8,128)S(1)}, f32[8,512]{1,0:T(8,128)S(1)}, u32[]{:S(2)}, u32[]{:S(2)}) collective-permute-start(f32[8,512]{1,0:T(8,128)S(1)} %get-tuple-element.71.own_ref), channel_id=1, source_target_pairs={{0,2},{1,3},{2,0},{3,1},{4,6},{5,7},{6,4},{7,5},{8,10},{9,11},{10,... | collective-permute-start | bytes 49160 | tf_op jit(solution)/shard_map/ppermute | solution.py:513
  33.1 3.7 %collective-permute-start.13 = (f32[8,512]{1,0:T(8,128)S(1)}, f32[8,512]{1,0:T(8,128)S(1)}, u32[]{:S(2)}, u32[]{:S(2)}) collective-permute-start(f32[8,512]{1,0:T(8,128)S(1)} %get-tuple-element.71.own_ref), channel_id=1, source_target_pairs={{0,1},{1,0},{2,3},{3,2},{4,5},{5,4},{6,7},{7,6},{8,9},{9,8},{10,11... | collective-permute-start | bytes 49160 | tf_op jit(solution)/shard_map/ppermute | solution.py:513

commit v6 on v5

--- a/solution.py
+++ b/solution.py
@@ -17,7 +17,7 @@
 F32 = jnp.float32
 VMEM_LIMIT = 24 * 1024 * 1024
 BF16 = jnp.bfloat16
-X_ORDER, Z_ORDER, L_ORDER = ((2, 3), (3, 2), (1, 1)), ((2, 3), (3, 2), (1, 1)), ((3, 3), (2, 2), (1, 1))
+X_ORDER, Z_ORDER, L_ORDER = ((2, 3), (3, 2), (1, 1)), ((3, 3), (2, 2), (1, 1)), ((3, 3), (2, 2), (1, 1))
 X_FLIP, Z_FLIP = 2, 2
 
 
@@ -158,10 +158,12 @@
         copy.start()
     lane = lax.broadcasted_iota(jnp.int32, (ROWS, NZ), 1)
     copies[0].wait()
-    k = pltpu.roll(k_ref[...].reshape(ROWS, NZ), 2, 1)
+    k = pltpu.roll(k_ref[...].reshape(ROWS, NZ), 3, 1)
     copies[1].wait()
-    both = jnp.where((lane == 1) | (lane == 2), k, u_ref[...].reshape(ROWS, NZ))
-    out_ref[...] = lanes_to_rows([(0, 0), (1, NZ - 1), (2, 2), (3, 1)], both)[:8]
+    both = jnp.where(lane < 2, pltpu.roll(u_ref[...].reshape(ROWS, NZ), 1, 1), k)
+    for i in range(ROWS // NZ):
+        block = slice(i * NZ, (i + 1) * NZ)
+        out_ref[:, block] = both[block].T[:8]
     index = lax.axis_index("gx")
     end_ref[...] = k_ref[jnp.where(lax.rem(index, 2) == 1, NX - 1, 0)]
     copies[2].wait()
@@ -201,8 +203,8 @@
     own, one, two = own_ref[...], one_ref[...], two_ref[...]
     low = jnp.where(odd, one, two) * jnp.where(g > 0, 1.0, 0.0)
     high = jnp.where(odd, two, one) * jnp.where(g < 3, 1.0, 0.0)
-    at_low = CZ * (low[3:4] + own[2:3]) * (low[1:2] - own[0:1])
-    at_high = CZ * (high[2:3] + own[3:4]) * (high[0:1] - own[1:2])
+    at_low = CZ * (low[2:3] + own[3:4]) * (low[0:1] - own[1:2])
+    at_high = CZ * (high[3:4] + own[2:3]) * (high[1:2] - own[0:1])
     row = lax.broadcasted_iota(jnp.int32, (8, ROWS), 0)
     both = jnp.where(row == 0, at_low, jnp.where(row == 1, at_high, 0.0))
     fix_ref[...] = rows_to_lanes([(0, 0), (1, NZ - 1)], both, NZ).reshape(NX, NY, NZ)

time: 38.1 us -> 37.9 us (level)
  waiting for transfers between devices: 13.6 us -> 12.2 us
  starting transfers between devices: 15 us -> 16.2 us
    ppermute x6, waiting for transfers between devices: 7.12 us -> 6.12 us  [gather(): got.append(lax.ppermute(block, 'gx', route))]
    ppermute x6, starting transfers between devices: 6.58 us -> 7.18 us  [gather(): got.append(lax.ppermute(block, 'gx', route))]
    ppermute x6, starting transfers between devices: 6.4 us -> 6.95 us  [swap(): return lax.ppermute(block, axis, [(i, i ^ mask) for i in range(n)])]
  transfers between devices with their start and end apart: 14 -> 14, of which waited for: 8 -> 9; matrix products, arithmetic and copies ran while one was open for 0% -> 0% of each run, Pallas kernels for 15% -> 15%
where the time goes in v6:
time: 37.9 us; the launch traced here: 37.7 us
  starting transfers between devices  16.2 us (43%)
  waiting for transfers between devices  12.2 us (32%)
  Pallas kernels  9.14 us (24%)
    pallas_call x12, Pallas kernels, call(): pl.pallas_call(kernel, out_shape=shapes, in_specs=[pl.BlockSpec(memory_sp...  9.14 us
    ppermute x6, starting transfers between devices, gather(): got.append(lax.ppermute(block, 'gx', route))  7.18 us
    ppermute x6, starting transfers between devices, swap(): return lax.ppermute(block, axis, [(i, i ^ mask) for i in range(n)])  6.95 us
    ppermute x6, waiting for transfers between devices, gather(): got.append(lax.ppermute(block, 'gx', route))  6.12 us
    ppermute x6, waiting for transfers between devices, swap(): return lax.ppermute(block, axis, [(i, i ^ mask) for i in range(n)])  6.11 us
    ppermute x1, starting transfers between devices, per_device(): below = lax.ppermute(end, 'gx', [(i, below_target(i, n)) for i in range(n)])  2.06 us
  transfers between devices with their start and end apart: 14, of which 9 were waited for; matrix products, arithmetic and copies ran while one was open for 0% of the time, Pallas kernels for 15%

profile of v6, /device:TPU:0, one launch (start us, length us, event | category | flops | bytes accessed | tf_op | source)
XLA Modules:
  0.0 37.7 jit_solution(675804879653844293)
XLA Ops:
  0.0 1.3 %edges.1 = (f32[8,64,128]{2,1,0:T(8,128)S(1)}, f32[8,64,128]{2,1,0:T(8,128)S(1)}, f32[8,64,128]{2,1,0:T(8,128)S(1)}, f32[8,512]{1,0:T(8,128)S(1)}, f32[64,128]{1,0:T(8,128)S(1)}) custom-call(f32[8,64,128]{2,1,0:T(8,128)} %u_hbm.1, f32[8,64,128]{2,1,0:T(8,128)} %k_hbm.1, f32[8,64,128]{2,1,0:T(8,128)} %f_hbm.1), custom_call_target="tpu_custom_call" | custom-call | bytes 1622016 | tf_op jit(solution)/shard_map/edges/pallas_call | solution.py:36
  1.3 2.1 %collective-permute-start.2 = (f32[64,128]{1,0:T(8,128)S(1)}, f32[64,128]{1,0:T(8,128)S(1)}, u32[]{:S(2)}, u32[]{:S(2)}) collective-permute-start(f32[64,128]{1,0:T(8,128)S(1)} %get-tuple-element.42), channel_id=1, source_target_pairs={{0,32},{4,8},{8,4},{12,16},{16,12},{20,24},{24,20},{28,60},{32,0},... | collective-permute-start | bytes 98312 | tf_op jit(solution)/shard_map/ppermute | solution.py:553
  3.4 1.6 %collective-permute-start = (f32[8,512]{1,0:T(8,128)S(1)}, f32[8,512]{1,0:T(8,128)S(1)}, u32[]{:S(2)}, u32[]{:S(2)}) collective-permute-start(f32[8,512]{1,0:T(8,128)S(1)} %get-tuple-element.41.own_ref), channel_id=1, source_target_pairs={{0,1},{1,0},{2,3},{3,2},{4,5},{5,4},{6,7},{7,6},{8,9},{9,8},{10,11... | collective-permute-start | bytes 49160 | tf_op jit(solution)/shard_map/ppermute | solution.py:515
  5.0 0.5 %local.1 = (f32[8,64,128]{2,1,0:T(8,128)S(1)}, f32[6,64,128]{2,1,0:T(8,128)S(1)}, f32[6,64,128]{2,1,0:T(8,128)S(1)}, f32[6,64,128]{2,1,0:T(8,128)S(1)}, f32[3,64,128]{2,1,0:T(8,128)S(1)}) custom-call(f32[8,64,128]{2,1,0:T(8,128)S(1)} %get-tuple-element.43.u_ref, f32[8,64,128]{2,1,0:T(8,128)S(1)} %get-tuple-element.44.k_ref, ...), custom_call_target="tpu_custom_call" | custom-call | bytes 1736704 | tf_op jit(solution)/shard_map/local/pallas_call | solution.py:36
  5.5 1.6 %collective-permute-done.one_ref = f32[8,512]{1,0:T(8,128)S(1)} collective-permute-done((f32[8,512]{1,0:T(8,128)S(1)}, f32[8,512]{1,0:T(8,128)S(1)}, u32[]{:S(2)}, u32[]{:S(2)}) %collective-permute-start) | collective-permute-done | bytes 16416 | tf_op jit(solution)/shard_map/ppermute | solution.py:515
  7.1 0.3 halo.1
  7.4 0.1 collective-permute-start.3
  7.5 1.3 %collective-permute-done.3.got_ref = f32[7,32,128]{2,1,0:T(8,128)S(1)} collective-permute-done((f32[7,32,128]{2,1,0:T(8,128)S(1)}, f32[7,32,128]{2,1,0:T(8,128)S(1)}, u32[]{:S(2)}, u32[]{:S(2)}) %collective-permute-start.3) | collective-permute-done | bytes 114720 | tf_op jit(solution)/shard_map/ppermute | solution.py:515
  8.9 1.0 %collective-permute-start.4 = (f32[6,32,128]{2,1,0:T(8,128)S(1)}, f32[6,32,128]{2,1,0:T(8,128)S(1)}, u32[]{:S(2)}, u32[]{:S(2)}) collective-permute-start(f32[6,32,128]{2,1,0:T(8,128)S(1)} %get-tuple-element.52.after_ref.own_ref), channel_id=1, source_target_pairs={{0,20},{4,24},{8,28},{12,16},{16,12},{20,0},{24,4},{28,8},{32,52},... | collective-permute-start | bytes 294920 | tf_op jit(solution)/shard_map/ppermute | solution.py:525
  9.9 1.1 %collective-permute-start.5 = (f32[6,32,128]{2,1,0:T(8,128)S(1)}, f32[6,32,128]{2,1,0:T(8,128)S(1)}, u32[]{:S(2)}, u32[]{:S(2)}) collective-permute-start(f32[6,32,128]{2,1,0:T(8,128)S(1)} %get-tuple-element.52.after_ref.own_ref), channel_id=1, source_target_pairs={{0,28},{4,16},{8,20},{12,24},{16,4},{20,8},{24,12},{28,0},{32,60},... | collective-permute-start | bytes 294920 | tf_op jit(solution)/shard_map/ppermute | solution.py:525
  11.0 1.1 %collective-permute-start.6 = (f32[6,32,128]{2,1,0:T(8,128)S(1)}, f32[6,32,128]{2,1,0:T(8,128)S(1)}, u32[]{:S(2)}, u32[]{:S(2)}) collective-permute-start(f32[6,32,128]{2,1,0:T(8,128)S(1)} %get-tuple-element.52.after_ref.own_ref), channel_id=1, source_target_pairs={{0,8},{4,12},{8,0},{12,4},{16,24},{20,28},{24,16},{28,20},{32,40},... | collective-permute-start | bytes 294920 | tf_op jit(solution)/shard_map/ppermute | solution.py:525
  12.2 0.5 %prepare.1 = (f32[64,8,128]{2,1,0:T(8,128)S(1)}, f32[64,8,128]{2,1,0:T(8,128)S(1)}, f32[64,8,128]{2,1,0:T(8,128)S(1)}, f32[64,8,128]{2,1,0:T(8,128)S(1)}, f32[64,8,128]{2,1,0:T(8,128)S(1)}) custom-call(f32[8,64,128]{2,1,0:T(8,128)S(1)} %get-tuple-element.43.u_ref, f32[8,64,128]{2,1,0:T(8,128)S(1)} %get-tuple-element.44.k_ref, ...), custom_call_target="tpu_custom_call" | custom-call | bytes 2621440 | tf_op jit(solution)/shard_map/prepare/pallas_call | solution.py:36
  12.7 1.7 %z_ports.2 = (f32[32,8,128]{2,1,0:T(8,128)S(1)}, f32[32,8,128]{2,1,0:T(8,128)S(1)}, f32[32,8,128]{2,1,0:T(8,128)S(1)}, f32[8,256]{1,0:T(8,128)S(1)}, f32[22,256,128]{2,1,0:T(8,128)S(1)}) custom-call(f32[8,64,128]{2,1,0:T(8,128)S(1)} %get-tuple-element.44.k_ref, f32[8,64,128]{2,1,0:T(8,128)S(1)} %get-tuple-element.43.u_ref, ...), custom_call_target="tpu_custom_call" | custom-call | bytes 3907584 | tf_op jit(solution)/shard_map/z_ports/pallas_call | solution.py:36
  14.4 0.2 collective-permute-done.4.one_ref
  14.6 3.1 %collective-permute-done.5.two_ref = f32[6,32,128]{2,1,0:T(8,128)S(1)} collective-permute-done((f32[6,32,128]{2,1,0:T(8,128)S(1)}, f32[6,32,128]{2,1,0:T(8,128)S(1)}, u32[]{:S(2)}, u32[]{:S(2)}) %collective-permute-start.5) | collective-permute-done | bytes 98336 | tf_op jit(solution)/shard_map/ppermute | solution.py:525
  17.7 0.1 chips.1
  17.8 2.3 %collective-permute-start.7 = (f32[5,32,128]{2,1,0:T(8,128)S(1)}, f32[5,32,128]{2,1,0:T(8,128)S(1)}, u32[]{:S(2)}, u32[]{:S(2)}) collective-permute-start(f32[5,32,128]{2,1,0:T(8,128)S(1)} %get-tuple-element.57.after_ref.own_ref), channel_id=1, source_target_pairs={{0,100},{4,96},{8,108},{12,104},{16,116},{20,112},{24,124},{28,120... | collective-permute-start | bytes 245768 | tf_op jit(solution)/shard_map/ppermute | solution.py:525
  20.1 0.6 %collective-permute-start.8 = (f32[5,32,128]{2,1,0:T(8,128)S(1)}, f32[5,32,128]{2,1,0:T(8,128)S(1)}, u32[]{:S(2)}, u32[]{:S(2)}) collective-permute-start(f32[5,32,128]{2,1,0:T(8,128)S(1)} %get-tuple-element.57.after_ref.own_ref), channel_id=1, source_target_pairs={{0,68},{4,64},{8,76},{12,72},{16,84},{20,80},{24,92},{28,88},{32,1... | collective-permute-start | bytes 245768 | tf_op jit(solution)/shard_map/ppermute | solution.py:525
  20.7 1.0 %collective-permute-start.9 = (f32[5,32,128]{2,1,0:T(8,128)S(1)}, f32[5,32,128]{2,1,0:T(8,128)S(1)}, u32[]{:S(2)}, u32[]{:S(2)}) collective-permute-start(f32[5,32,128]{2,1,0:T(8,128)S(1)} %get-tuple-element.57.after_ref.own_ref), channel_id=1, source_target_pairs={{0,32},{4,36},{8,40},{12,44},{16,48},{20,52},{24,56},{28,60},{32,0... | collective-permute-start | bytes 245768 | tf_op jit(solution)/shard_map/ppermute | solution.py:525
  21.7 1.6 %z_ports.3 = (f32[32,8,128]{2,1,0:T(8,128)S(1)}, f32[32,8,128]{2,1,0:T(8,128)S(1)}, f32[32,8,128]{2,1,0:T(8,128)S(1)}, f32[8,256]{1,0:T(8,128)S(1)}, f32[22,256,128]{2,1,0:T(8,128)S(1)}) custom-call(f32[8,64,128]{2,1,0:T(8,128)S(1)} %get-tuple-element.44.k_ref, f32[8,64,128]{2,1,0:T(8,128)S(1)} %get-tuple-element.43.u_ref, ...), custom_call_target="tpu_custom_call" | custom-call | bytes 3891200 | tf_op jit(solution)/shard_map/z_ports/pallas_call | solution.py:36
  23.3 1.1 %collective-permute-done.7.one_ref = f32[5,32,128]{2,1,0:T(8,128)S(1)} collective-permute-done((f32[5,32,128]{2,1,0:T(8,128)S(1)}, f32[5,32,128]{2,1,0:T(8,128)S(1)}, u32[]{:S(2)}, u32[]{:S(2)}) %collective-permute-start.7) | collective-permute-done | bytes 81952 | tf_op jit(solution)/shard_map/ppermute | solution.py:525
  24.4 1.4 %collective-permute-done.8.two_ref = f32[5,32,128]{2,1,0:T(8,128)S(1)} collective-permute-done((f32[5,32,128]{2,1,0:T(8,128)S(1)}, f32[5,32,128]{2,1,0:T(8,128)S(1)}, u32[]{:S(2)}, u32[]{:S(2)}) %collective-permute-start.8) | collective-permute-done | bytes 81952 | tf_op jit(solution)/shard_map/ppermute | solution.py:525
  25.8 0.4 collective-permute-done.9.three_ref
  26.1 0.1 back.1
  26.2 0.6 %collective-permute-start.10 = (f32[2,32,128]{2,1,0:T(8,128)S(1)}, f32[2,32,128]{2,1,0:T(8,128)S(1)}, u32[]{:S(2)}, u32[]{:S(2)}) collective-permute-start(f32[2,32,128]{2,1,0:T(8,128)S(1)} %get-tuple-element.62), channel_id=1, source_target_pairs={{0,4},{4,0},{8,12},{12,8},{16,20},{20,16},{24,28},{28,24},{32,36},... | collective-permute-start | bytes 98312 | tf_op jit(solution)/shard_map/ppermute | solution.py:515
  26.9 0.9 %collective-permute-done.10.got_ref = f32[2,32,128]{2,1,0:T(8,128)S(1)} collective-permute-done((f32[2,32,128]{2,1,0:T(8,128)S(1)}, f32[2,32,128]{2,1,0:T(8,128)S(1)}, u32[]{:S(2)}, u32[]{:S(2)}) %collective-permute-start.10) | collective-permute-done | bytes 32800 | tf_op jit(solution)/shard_map/ppermute | solution.py:515
  27.7 0.4 %y_solve.1 = (f32[64,8,128]{2,1,0:T(8,128)S(1)}, f32[8,512]{1,0:T(8,128)S(1)}) custom-call(f32[2,32,128]{2,1,0:T(8,128)S(1)} %get-tuple-element.61.keep_ref, f32[2,32,128]{2,1,0:T(8,128)S(1)} %collective-permute-done.10.got_ref, f32[64,8,128]{2,1,0:T(8,128)S(1)} %get-tuple-element.63.base_ref, f32[64,8,128]{2,1,0:T(8,128)S(1)} %get-tuple-element.64.gx_ref, ...), custom_call_target="tpu_custom_call" | custom-call | bytes 2195456 | tf_op jit(solution)/shard_map/y_solve/pallas_call | solution.py:36
  28.2 3.1 %collective-permute-start.11 = (f32[8,512]{1,0:T(8,128)S(1)}, f32[8,512]{1,0:T(8,128)S(1)}, u32[]{:S(2)}, u32[]{:S(2)}) collective-permute-start(f32[8,512]{1,0:T(8,128)S(1)} %get-tuple-element.71.own_ref), channel_id=1, source_target_pairs={{0,3},{1,2},{2,1},{3,0},{4,7},{5,6},{6,5},{7,4},{8,11},{9,10},{10,... | collective-permute-start | bytes 49160 | tf_op jit(solution)/shard_map/ppermute | solution.py:515
  31.3 1.6 %collective-permute-start.12 = (f32[8,512]{1,0:T(8,128)S(1)}, f32[8,512]{1,0:T(8,128)S(1)}, u32[]{:S(2)}, u32[]{:S(2)}) collective-permute-start(f32[8,512]{1,0:T(8,128)S(1)} %get-tuple-element.71.own_ref), channel_id=1, source_target_pairs={{0,2},{1,3},{2,0},{3,1},{4,6},{5,7},{6,4},{7,5},{8,10},{9,11},{10,... | collective-permute-start | bytes 49160 | tf_op jit(solution)/shard_map/ppermute | solution.py:515
  32.9 1.4 %z_local.1.y_ref = f32[64,8,128]{2,1,0:T(8,128)S(1)} custom-call(f32[22,256,128]{2,1,0:T(8,128)S(1)} %get-tuple-element.72.f0_ref, f32[22,256,128]{2,1,0:T(8,128)S(1)} %get-tuple-element.73.f1_ref, f32[32,8,128]{2,1,0:T(8,128)S(1)} %get-tuple-element.74.u0_ref, f32[32,8,128]{2,1,0:T(8,128)S(1)} %get-tuple-element.75.u1_ref, ...), custom_call_target="tpu_custom_call" | custom-call | bytes 6553600 | tf_op jit(solution)/shard_map/z_local/pallas_call | solution.py:36
  34.3 2.3 %collective-permute-done.12.two_ref = f32[8,512]{1,0:T(8,128)S(1)} collective-permute-done((f32[8,512]{1,0:T(8,128)S(1)}, f32[8,512]{1,0:T(8,128)S(1)}, u32[]{:S(2)}, u32[]{:S(2)}) %collective-permute-start.12) | collective-permute-done | bytes 16416 | tf_op jit(solution)/shard_map/ppermute | solution.py:515
  36.6 1.1 %final.1 = f32[8,64,128]{2,1,0:T(8,128)} custom-call(f32[8,512]{1,0:T(8,128)S(1)} %get-tuple-element.71.own_ref, f32[8,512]{1,0:T(8,128)S(1)} %collective-permute-done.11.one_ref, f32[8,512]{1,0:T(8,128)S(1)} %collective-permute-done.12.two_ref, f32[8,512]{1,0:T(8,128)S(1)} %collective-permute-done.13.three_ref, f32[64,8,128]{2,1,0:T(8,128)S(1)} %z_local.1.y_ref, ...), custom_call_target="tpu_custom_call" | custom-call | bytes 1114112 | tf_op jit(solution)/shard_map/final/pallas_call | solution.py:36
  (8 shorter events, 0.1 us)
Async XLA Ops:
  1.3 5.8 %collective-permute-start.2 = (f32[64,128]{1,0:T(8,128)S(1)}, f32[64,128]{1,0:T(8,128)S(1)}, u32[]{:S(2)}, u32[]{:S(2)}) collective-permute-start(f32[64,128]{1,0:T(8,128)S(1)} %get-tuple-element.42), channel_id=1, source_target_pairs={{0,32},{4,8},{8,4},{12,16},{16,12},{20,24},{24,20},{28,60},{32,0},... | collective-permute-start | bytes 98312 | tf_op jit(solution)/shard_map/ppermute | solution.py:553
  3.4 3.7 %collective-permute-start = (f32[8,512]{1,0:T(8,128)S(1)}, f32[8,512]{1,0:T(8,128)S(1)}, u32[]{:S(2)}, u32[]{:S(2)}) collective-permute-start(f32[8,512]{1,0:T(8,128)S(1)} %get-tuple-element.41.own_ref), channel_id=1, source_target_pairs={{0,1},{1,0},{2,3},{3,2},{4,5},{5,4},{6,7},{7,6},{8,9},{9,8},{10,11... | collective-permute-start | bytes 49160 | tf_op jit(solution)/shard_map/ppermute | solution.py:515
  4.9 2.2 %collective-permute-start.1 = (f32[8,512]{1,0:T(8,128)S(1)}, f32[8,512]{1,0:T(8,128)S(1)}, u32[]{:S(2)}, u32[]{:S(2)}) collective-permute-start(f32[8,512]{1,0:T(8,128)S(1)} %get-tuple-element.41.own_ref), channel_id=1, source_target_pairs={{0,4},{1,2},{2,1},{3,7},{4,0},{5,6},{6,5},{7,3},{8,12},{9,10},{10,... | collective-permute-start | bytes 49160 | tf_op jit(solution)/shard_map/ppermute | solution.py:552
  7.4 1.4 %collective-permute-start.3 = (f32[7,32,128]{2,1,0:T(8,128)S(1)}, f32[7,32,128]{2,1,0:T(8,128)S(1)}, u32[]{:S(2)}, u32[]{:S(2)}) collective-permute-start(f32[7,32,128]{2,1,0:T(8,128)S(1)} %get-tuple-element.51), channel_id=1, source_target_pairs={{0,4},{4,0},{8,12},{12,8},{16,20},{20,16},{24,28},{28,24},{32,36},... | collective-permute-start | bytes 344072 | tf_op jit(solution)/shard_map/ppermute | solution.py:515
  8.9 5.7 %collective-permute-start.4 = (f32[6,32,128]{2,1,0:T(8,128)S(1)}, f32[6,32,128]{2,1,0:T(8,128)S(1)}, u32[]{:S(2)}, u32[]{:S(2)}) collective-permute-start(f32[6,32,128]{2,1,0:T(8,128)S(1)} %get-tuple-element.52.after_ref.own_ref), channel_id=1, source_target_pairs={{0,20},{4,24},{8,28},{12,16},{16,12},{20,0},{24,4},{28,8},{32,52},... | collective-permute-start | bytes 294920 | tf_op jit(solution)/shard_map/ppermute | solution.py:525
  9.9 7.7 %collective-permute-start.5 = (f32[6,32,128]{2,1,0:T(8,128)S(1)}, f32[6,32,128]{2,1,0:T(8,128)S(1)}, u32[]{:S(2)}, u32[]{:S(2)}) collective-permute-start(f32[6,32,128]{2,1,0:T(8,128)S(1)} %get-tuple-element.52.after_ref.own_ref), channel_id=1, source_target_pairs={{0,28},{4,16},{8,20},{12,24},{16,4},{20,8},{24,12},{28,0},{32,60},... | collective-permute-start | bytes 294920 | tf_op jit(solution)/shard_map/ppermute | solution.py:525
  11.0 6.6 %collective-permute-start.6 = (f32[6,32,128]{2,1,0:T(8,128)S(1)}, f32[6,32,128]{2,1,0:T(8,128)S(1)}, u32[]{:S(2)}, u32[]{:S(2)}) collective-permute-start(f32[6,32,128]{2,1,0:T(8,128)S(1)} %get-tuple-element.52.after_ref.own_ref), channel_id=1, source_target_pairs={{0,8},{4,12},{8,0},{12,4},{16,24},{20,28},{24,16},{28,20},{32,40},... | collective-permute-start | bytes 294920 | tf_op jit(solution)/shard_map/ppermute | solution.py:525
  17.8 6.6 %collective-permute-start.7 = (f32[5,32,128]{2,1,0:T(8,128)S(1)}, f32[5,32,128]{2,1,0:T(8,128)S(1)}, u32[]{:S(2)}, u32[]{:S(2)}) collective-permute-start(f32[5,32,128]{2,1,0:T(8,128)S(1)} %get-tuple-element.57.after_ref.own_ref), channel_id=1, source_target_pairs={{0,100},{4,96},{8,108},{12,104},{16,116},{20,112},{24,124},{28,120... | collective-permute-start | bytes 245768 | tf_op jit(solution)/shard_map/ppermute | solution.py:525
  20.1 5.7 %collective-permute-start.8 = (f32[5,32,128]{2,1,0:T(8,128)S(1)}, f32[5,32,128]{2,1,0:T(8,128)S(1)}, u32[]{:S(2)}, u32[]{:S(2)}) collective-permute-start(f32[5,32,128]{2,1,0:T(8,128)S(1)} %get-tuple-element.57.after_ref.own_ref), channel_id=1, source_target_pairs={{0,68},{4,64},{8,76},{12,72},{16,84},{20,80},{24,92},{28,88},{32,1... | collective-permute-start | bytes 245768 | tf_op jit(solution)/shard_map/ppermute | solution.py:525
  20.7 5.5 %collective-permute-start.9 = (f32[5,32,128]{2,1,0:T(8,128)S(1)}, f32[5,32,128]{2,1,0:T(8,128)S(1)}, u32[]{:S(2)}, u32[]{:S(2)}) collective-permute-start(f32[5,32,128]{2,1,0:T(8,128)S(1)} %get-tuple-element.57.after_ref.own_ref), channel_id=1, source_target_pairs={{0,32},{4,36},{8,40},{12,44},{16,48},{20,52},{24,56},{28,60},{32,0... | collective-permute-start | bytes 245768 | tf_op jit(solution)/shard_map/ppermute | solution.py:525
  26.2 1.5 %collective-permute-start.10 = (f32[2,32,128]{2,1,0:T(8,128)S(1)}, f32[2,32,128]{2,1,0:T(8,128)S(1)}, u32[]{:S(2)}, u32[]{:S(2)}) collective-permute-start(f32[2,32,128]{2,1,0:T(8,128)S(1)} %get-tuple-element.62), channel_id=1, source_target_pairs={{0,4},{4,0},{8,12},{12,8},{16,20},{20,16},{24,28},{28,24},{32,36},... | collective-permute-start | bytes 98312 | tf_op jit(solution)/shard_map/ppermute | solution.py:515
  28.2 6.0 %collective-permute-start.11 = (f32[8,512]{1,0:T(8,128)S(1)}, f32[8,512]{1,0:T(8,128)S(1)}, u32[]{:S(2)}, u32[]{:S(2)}) collective-permute-start(f32[8,512]{1,0:T(8,128)S(1)} %get-tuple-element.71.own_ref), channel_id=1, source_target_pairs={{0,3},{1,2},{2,1},{3,0},{4,7},{5,6},{6,5},{7,4},{8,11},{9,10},{10,... | collective-permute-start | bytes 49160 | tf_op jit(solution)/shard_map/ppermute | solution.py:515
  31.3 5.2 %collective-permute-start.12 = (f32[8,512]{1,0:T(8,128)S(1)}, f32[8,512]{1,0:T(8,128)S(1)}, u32[]{:S(2)}, u32[]{:S(2)}) collective-permute-start(f32[8,512]{1,0:T(8,128)S(1)} %get-tuple-element.71.own_ref), channel_id=1, source_target_pairs={{0,2},{1,3},{2,0},{3,1},{4,6},{5,7},{6,4},{7,5},{8,10},{9,11},{10,... | collective-permute-start | bytes 49160 | tf_op jit(solution)/shard_map/ppermute | solution.py:515
  32.9 3.7 %collective-permute-start.13 = (f32[8,512]{1,0:T(8,128)S(1)}, f32[8,512]{1,0:T(8,128)S(1)}, u32[]{:S(2)}, u32[]{:S(2)}) collective-permute-start(f32[8,512]{1,0:T(8,128)S(1)} %get-tuple-element.71.own_ref), channel_id=1, source_target_pairs={{0,1},{1,0},{2,3},{3,2},{4,5},{5,4},{6,7},{7,6},{8,9},{9,8},{10,11... | collective-permute-start | bytes 49160 | tf_op jit(solution)/shard_map/ppermute | solution.py:515

commit v7 on v6

--- a/solution.py
+++ b/solution.py
@@ -17,7 +17,7 @@
 F32 = jnp.float32
 VMEM_LIMIT = 24 * 1024 * 1024
 BF16 = jnp.bfloat16
-X_ORDER, Z_ORDER, L_ORDER = ((2, 3), (3, 2), (1, 1)), ((3, 3), (2, 2), (1, 1)), ((3, 3), (2, 2), (1, 1))
+X_ORDER, Z_ORDER, L_ORDER = ((3, 2), (2, 3), (1, 1)), ((3, 2), (2, 3), (1, 1)), ((3, 3), (2, 2), (1, 1))
 X_FLIP, Z_FLIP = 2, 2
 
 

time: 37.9 us -> 37.9 us (level)
  starting transfers between devices: 16.2 us -> 16.9 us
  waiting for transfers between devices: 12.2 us -> 11.5 us
    ppermute x6, waiting for transfers between devices: 6.12 us -> 5.4 us  [gather(): got.append(lax.ppermute(block, 'gx', route))]
    ppermute x6, starting transfers between devices: 7.18 us -> 7.85 us  [gather(): got.append(lax.ppermute(block, 'gx', route))]
where the time goes in v7:
time: 37.9 us; the launch traced here: 37.6 us
  starting transfers between devices  16.9 us (45%)
  waiting for transfers between devices  11.5 us (30%)
  Pallas kernels  9.14 us (24%)
    pallas_call x12, Pallas kernels, call(): pl.pallas_call(kernel, out_shape=shapes, in_specs=[pl.BlockSpec(memory_sp...  9.14 us
    ppermute x6, starting transfers between devices, gather(): got.append(lax.ppermute(block, 'gx', route))  7.85 us
    ppermute x6, starting transfers between devices, swap(): return lax.ppermute(block, axis, [(i, i ^ mask) for i in range(n)])  6.95 us
    ppermute x6, waiting for transfers between devices, swap(): return lax.ppermute(block, axis, [(i, i ^ mask) for i in range(n)])  6.11 us
    ppermute x6, waiting for transfers between devices, gather(): got.append(lax.ppermute(block, 'gx', route))  5.4 us
    ppermute x1, starting transfers between devices, per_device(): below = lax.ppermute(end, 'gx', [(i, below_target(i, n)) for i in range(n)])  2.06 us
  transfers between devices with their start and end apart: 14, of which 9 were waited for; matrix products, arithmetic and copies ran while one was open for 0% of the time, Pallas kernels for 15%

profile of v7, /device:TPU:0, one launch (start us, length us, event | category | flops | bytes accessed | tf_op | source)
XLA Modules:
  0.0 37.6 jit_solution(2960706589548351327)
XLA Ops:
  0.0 1.3 %edges.1 = (f32[8,64,128]{2,1,0:T(8,128)S(1)}, f32[8,64,128]{2,1,0:T(8,128)S(1)}, f32[8,64,128]{2,1,0:T(8,128)S(1)}, f32[8,512]{1,0:T(8,128)S(1)}, f32[64,128]{1,0:T(8,128)S(1)}) custom-call(f32[8,64,128]{2,1,0:T(8,128)} %u_hbm.1, f32[8,64,128]{2,1,0:T(8,128)} %k_hbm.1, f32[8,64,128]{2,1,0:T(8,128)} %f_hbm.1), custom_call_target="tpu_custom_call" | custom-call | bytes 1622016 | tf_op jit(solution)/shard_map/edges/pallas_call | solution.py:36
  1.3 2.1 %collective-permute-start.2 = (f32[64,128]{1,0:T(8,128)S(1)}, f32[64,128]{1,0:T(8,128)S(1)}, u32[]{:S(2)}, u32[]{:S(2)}) collective-permute-start(f32[64,128]{1,0:T(8,128)S(1)} %get-tuple-element.42), channel_id=1, source_target_pairs={{0,32},{4,8},{8,4},{12,16},{16,12},{20,24},{24,20},{28,60},{32,0},... | collective-permute-start | bytes 98312 | tf_op jit(solution)/shard_map/ppermute | solution.py:553
  3.4 1.6 %collective-permute-start = (f32[8,512]{1,0:T(8,128)S(1)}, f32[8,512]{1,0:T(8,128)S(1)}, u32[]{:S(2)}, u32[]{:S(2)}) collective-permute-start(f32[8,512]{1,0:T(8,128)S(1)} %get-tuple-element.41.own_ref), channel_id=1, source_target_pairs={{0,1},{1,0},{2,3},{3,2},{4,5},{5,4},{6,7},{7,6},{8,9},{9,8},{10,11... | collective-permute-start | bytes 49160 | tf_op jit(solution)/shard_map/ppermute | solution.py:515
  5.0 0.5 %local.1 = (f32[8,64,128]{2,1,0:T(8,128)S(1)}, f32[6,64,128]{2,1,0:T(8,128)S(1)}, f32[6,64,128]{2,1,0:T(8,128)S(1)}, f32[6,64,128]{2,1,0:T(8,128)S(1)}, f32[3,64,128]{2,1,0:T(8,128)S(1)}) custom-call(f32[8,64,128]{2,1,0:T(8,128)S(1)} %get-tuple-element.43.u_ref, f32[8,64,128]{2,1,0:T(8,128)S(1)} %get-tuple-element.44.k_ref, ...), custom_call_target="tpu_custom_call" | custom-call | bytes 1736704 | tf_op jit(solution)/shard_map/local/pallas_call | solution.py:36
  5.5 1.6 %collective-permute-done.one_ref = f32[8,512]{1,0:T(8,128)S(1)} collective-permute-done((f32[8,512]{1,0:T(8,128)S(1)}, f32[8,512]{1,0:T(8,128)S(1)}, u32[]{:S(2)}, u32[]{:S(2)}) %collective-permute-start) | collective-permute-done | bytes 16416 | tf_op jit(solution)/shard_map/ppermute | solution.py:515
  7.1 0.3 halo.1
  7.4 0.1 collective-permute-start.3
  7.5 1.3 %collective-permute-done.3.got_ref = f32[7,32,128]{2,1,0:T(8,128)S(1)} collective-permute-done((f32[7,32,128]{2,1,0:T(8,128)S(1)}, f32[7,32,128]{2,1,0:T(8,128)S(1)}, u32[]{:S(2)}, u32[]{:S(2)}) %collective-permute-start.3) | collective-permute-done | bytes 114720 | tf_op jit(solution)/shard_map/ppermute | solution.py:515
  8.8 0.1 core.1
  8.9 1.7 %collective-permute-start.4 = (f32[6,32,128]{2,1,0:T(8,128)S(1)}, f32[6,32,128]{2,1,0:T(8,128)S(1)}, u32[]{:S(2)}, u32[]{:S(2)}) collective-permute-start(f32[6,32,128]{2,1,0:T(8,128)S(1)} %get-tuple-element.52.after_ref.own_ref), channel_id=1, source_target_pairs={{0,28},{4,16},{8,20},{12,24},{16,4},{20,8},{24,12},{28,0},{32,60},... | collective-permute-start | bytes 294920 | tf_op jit(solution)/shard_map/ppermute | solution.py:525
  10.5 2.2 %collective-permute-start.6 = (f32[6,32,128]{2,1,0:T(8,128)S(1)}, f32[6,32,128]{2,1,0:T(8,128)S(1)}, u32[]{:S(2)}, u32[]{:S(2)}) collective-permute-start(f32[6,32,128]{2,1,0:T(8,128)S(1)} %get-tuple-element.52.after_ref.own_ref), channel_id=1, source_target_pairs={{0,8},{4,12},{8,0},{12,4},{16,24},{20,28},{24,16},{28,20},{32,40},... | collective-permute-start | bytes 294920 | tf_op jit(solution)/shard_map/ppermute | solution.py:525
  12.8 0.5 %prepare.1 = (f32[64,8,128]{2,1,0:T(8,128)S(1)}, f32[64,8,128]{2,1,0:T(8,128)S(1)}, f32[64,8,128]{2,1,0:T(8,128)S(1)}, f32[64,8,128]{2,1,0:T(8,128)S(1)}, f32[64,8,128]{2,1,0:T(8,128)S(1)}) custom-call(f32[8,64,128]{2,1,0:T(8,128)S(1)} %get-tuple-element.43.u_ref, f32[8,64,128]{2,1,0:T(8,128)S(1)} %get-tuple-element.44.k_ref, ...), custom_call_target="tpu_custom_call" | custom-call | bytes 2621440 | tf_op jit(solution)/shard_map/prepare/pallas_call | solution.py:36
  13.3 1.7 %z_ports.2 = (f32[32,8,128]{2,1,0:T(8,128)S(1)}, f32[32,8,128]{2,1,0:T(8,128)S(1)}, f32[32,8,128]{2,1,0:T(8,128)S(1)}, f32[8,256]{1,0:T(8,128)S(1)}, f32[22,256,128]{2,1,0:T(8,128)S(1)}) custom-call(f32[8,64,128]{2,1,0:T(8,128)S(1)} %get-tuple-element.44.k_ref, f32[8,64,128]{2,1,0:T(8,128)S(1)} %get-tuple-element.43.u_ref, ...), custom_call_target="tpu_custom_call" | custom-call | bytes 3907584 | tf_op jit(solution)/shard_map/z_ports/pallas_call | solution.py:36
  15.0 1.6 %collective-permute-done.4.one_ref = f32[6,32,128]{2,1,0:T(8,128)S(1)} collective-permute-done((f32[6,32,128]{2,1,0:T(8,128)S(1)}, f32[6,32,128]{2,1,0:T(8,128)S(1)}, u32[]{:S(2)}, u32[]{:S(2)}) %collective-permute-start.4) | collective-permute-done | bytes 98336 | tf_op jit(solution)/shard_map/ppermute | solution.py:525
  16.6 0.6 %collective-permute-done.6.three_ref = f32[6,32,128]{2,1,0:T(8,128)S(1)} collective-permute-done((f32[6,32,128]{2,1,0:T(8,128)S(1)}, f32[6,32,128]{2,1,0:T(8,128)S(1)}, u32[]{:S(2)}, u32[]{:S(2)}) %collective-permute-start.6) | collective-permute-done | bytes 98336 | tf_op jit(solution)/shard_map/ppermute | solution.py:525
  17.1 0.1 chips.1
  17.2 3.0 %collective-permute-start.7 = (f32[5,32,128]{2,1,0:T(8,128)S(1)}, f32[5,32,128]{2,1,0:T(8,128)S(1)}, u32[]{:S(2)}, u32[]{:S(2)}) collective-permute-start(f32[5,32,128]{2,1,0:T(8,128)S(1)} %get-tuple-element.57.after_ref.own_ref), channel_id=1, source_target_pairs={{0,100},{4,64},{8,108},{12,72},{16,84},{20,112},{24,92},{28,120},{... | collective-permute-start | bytes 245768 | tf_op jit(solution)/shard_map/ppermute | solution.py:525
  20.2 0.9 %collective-permute-start.8 = (f32[5,32,128]{2,1,0:T(8,128)S(1)}, f32[5,32,128]{2,1,0:T(8,128)S(1)}, u32[]{:S(2)}, u32[]{:S(2)}) collective-permute-start(f32[5,32,128]{2,1,0:T(8,128)S(1)} %get-tuple-element.57.after_ref.own_ref), channel_id=1, source_target_pairs={{0,68},{4,96},{8,76},{12,104},{16,116},{20,80},{24,124},{28,88},{3... | collective-permute-start | bytes 245768 | tf_op jit(solution)/shard_map/ppermute | solution.py:525
  21.2 1.6 %z_ports.3 = (f32[32,8,128]{2,1,0:T(8,128)S(1)}, f32[32,8,128]{2,1,0:T(8,128)S(1)}, f32[32,8,128]{2,1,0:T(8,128)S(1)}, f32[8,256]{1,0:T(8,128)S(1)}, f32[22,256,128]{2,1,0:T(8,128)S(1)}) custom-call(f32[8,64,128]{2,1,0:T(8,128)S(1)} %get-tuple-element.44.k_ref, f32[8,64,128]{2,1,0:T(8,128)S(1)} %get-tuple-element.43.u_ref, ...), custom_call_target="tpu_custom_call" | custom-call | bytes 3891200 | tf_op jit(solution)/shard_map/z_ports/pallas_call | solution.py:36
  22.8 1.6 %collective-permute-done.7.one_ref = f32[5,32,128]{2,1,0:T(8,128)S(1)} collective-permute-done((f32[5,32,128]{2,1,0:T(8,128)S(1)}, f32[5,32,128]{2,1,0:T(8,128)S(1)}, u32[]{:S(2)}, u32[]{:S(2)}) %collective-permute-start.7) | collective-permute-done | bytes 81952 | tf_op jit(solution)/shard_map/ppermute | solution.py:525
  24.4 1.2 %collective-permute-done.8.two_ref = f32[5,32,128]{2,1,0:T(8,128)S(1)} collective-permute-done((f32[5,32,128]{2,1,0:T(8,128)S(1)}, f32[5,32,128]{2,1,0:T(8,128)S(1)}, u32[]{:S(2)}, u32[]{:S(2)}) %collective-permute-start.8) | collective-permute-done | bytes 81952 | tf_op jit(solution)/shard_map/ppermute | solution.py:525
  25.6 0.5 %collective-permute-done.9.three_ref = f32[5,32,128]{2,1,0:T(8,128)S(1)} collective-permute-done((f32[5,32,128]{2,1,0:T(8,128)S(1)}, f32[5,32,128]{2,1,0:T(8,128)S(1)}, u32[]{:S(2)}, u32[]{:S(2)}) %collective-permute-start.9) | collective-permute-done | bytes 81952 | tf_op jit(solution)/shard_map/ppermute | solution.py:525
  26.1 0.1 back.1
  26.2 0.6 %collective-permute-start.10 = (f32[2,32,128]{2,1,0:T(8,128)S(1)}, f32[2,32,128]{2,1,0:T(8,128)S(1)}, u32[]{:S(2)}, u32[]{:S(2)}) collective-permute-start(f32[2,32,128]{2,1,0:T(8,128)S(1)} %get-tuple-element.62), channel_id=1, source_target_pairs={{0,4},{4,0},{8,12},{12,8},{16,20},{20,16},{24,28},{28,24},{32,36},... | collective-permute-start | bytes 98312 | tf_op jit(solution)/shard_map/ppermute | solution.py:515
  26.8 0.9 %collective-permute-done.10.got_ref = f32[2,32,128]{2,1,0:T(8,128)S(1)} collective-permute-done((f32[2,32,128]{2,1,0:T(8,128)S(1)}, f32[2,32,128]{2,1,0:T(8,128)S(1)}, u32[]{:S(2)}, u32[]{:S(2)}) %collective-permute-start.10) | collective-permute-done | bytes 32800 | tf_op jit(solution)/shard_map/ppermute | solution.py:515
  27.7 0.4 %y_solve.1 = (f32[64,8,128]{2,1,0:T(8,128)S(1)}, f32[8,512]{1,0:T(8,128)S(1)}) custom-call(f32[2,32,128]{2,1,0:T(8,128)S(1)} %get-tuple-element.61.keep_ref, f32[2,32,128]{2,1,0:T(8,128)S(1)} %collective-permute-done.10.got_ref, f32[64,8,128]{2,1,0:T(8,128)S(1)} %get-tuple-element.63.base_ref, f32[64,8,128]{2,1,0:T(8,128)S(1)} %get-tuple-element.64.gx_ref, ...), custom_call_target="tpu_custom_call" | custom-call | bytes 2195456 | tf_op jit(solution)/shard_map/y_solve/pallas_call | solution.py:36
  28.1 3.1 %collective-permute-start.11 = (f32[8,512]{1,0:T(8,128)S(1)}, f32[8,512]{1,0:T(8,128)S(1)}, u32[]{:S(2)}, u32[]{:S(2)}) collective-permute-start(f32[8,512]{1,0:T(8,128)S(1)} %get-tuple-element.71.own_ref), channel_id=1, source_target_pairs={{0,3},{1,2},{2,1},{3,0},{4,7},{5,6},{6,5},{7,4},{8,11},{9,10},{10,... | collective-permute-start | bytes 49160 | tf_op jit(solution)/shard_map/ppermute | solution.py:515
  31.2 1.6 %collective-permute-start.12 = (f32[8,512]{1,0:T(8,128)S(1)}, f32[8,512]{1,0:T(8,128)S(1)}, u32[]{:S(2)}, u32[]{:S(2)}) collective-permute-start(f32[8,512]{1,0:T(8,128)S(1)} %get-tuple-element.71.own_ref), channel_id=1, source_target_pairs={{0,2},{1,3},{2,0},{3,1},{4,6},{5,7},{6,4},{7,5},{8,10},{9,11},{10,... | collective-permute-start | bytes 49160 | tf_op jit(solution)/shard_map/ppermute | solution.py:515
  32.8 1.4 %z_local.1.y_ref = f32[64,8,128]{2,1,0:T(8,128)S(1)} custom-call(f32[22,256,128]{2,1,0:T(8,128)S(1)} %get-tuple-element.72.f0_ref, f32[22,256,128]{2,1,0:T(8,128)S(1)} %get-tuple-element.73.f1_ref, f32[32,8,128]{2,1,0:T(8,128)S(1)} %get-tuple-element.74.u0_ref, f32[32,8,128]{2,1,0:T(8,128)S(1)} %get-tuple-element.75.u1_ref, ...), custom_call_target="tpu_custom_call" | custom-call | bytes 6553600 | tf_op jit(solution)/shard_map/z_local/pallas_call | solution.py:36
  34.2 2.3 %collective-permute-done.12.two_ref = f32[8,512]{1,0:T(8,128)S(1)} collective-permute-done((f32[8,512]{1,0:T(8,128)S(1)}, f32[8,512]{1,0:T(8,128)S(1)}, u32[]{:S(2)}, u32[]{:S(2)}) %collective-permute-start.12) | collective-permute-done | bytes 16416 | tf_op jit(solution)/shard_map/ppermute | solution.py:515
  36.5 0.0 collective-permute-done.13.three_ref
  36.5 1.1 %final.1 = f32[8,64,128]{2,1,0:T(8,128)} custom-call(f32[8,512]{1,0:T(8,128)S(1)} %get-tuple-element.71.own_ref, f32[8,512]{1,0:T(8,128)S(1)} %collective-permute-done.11.one_ref, f32[8,512]{1,0:T(8,128)S(1)} %collective-permute-done.12.two_ref, f32[8,512]{1,0:T(8,128)S(1)} %collective-permute-done.13.three_ref, f32[64,8,128]{2,1,0:T(8,128)S(1)} %z_local.1.y_ref, ...), custom_call_target="tpu_custom_call" | custom-call | bytes 1114112 | tf_op jit(solution)/shard_map/final/pallas_call | solution.py:36
  (8 shorter events, 0.1 us)
Async XLA Ops:
  1.3 5.8 %collective-permute-start.2 = (f32[64,128]{1,0:T(8,128)S(1)}, f32[64,128]{1,0:T(8,128)S(1)}, u32[]{:S(2)}, u32[]{:S(2)}) collective-permute-start(f32[64,128]{1,0:T(8,128)S(1)} %get-tuple-element.42), channel_id=1, source_target_pairs={{0,32},{4,8},{8,4},{12,16},{16,12},{20,24},{24,20},{28,60},{32,0},... | collective-permute-start | bytes 98312 | tf_op jit(solution)/shard_map/ppermute | solution.py:553
  3.4 3.7 %collective-permute-start = (f32[8,512]{1,0:T(8,128)S(1)}, f32[8,512]{1,0:T(8,128)S(1)}, u32[]{:S(2)}, u32[]{:S(2)}) collective-permute-start(f32[8,512]{1,0:T(8,128)S(1)} %get-tuple-element.41.own_ref), channel_id=1, source_target_pairs={{0,1},{1,0},{2,3},{3,2},{4,5},{5,4},{6,7},{7,6},{8,9},{9,8},{10,11... | collective-permute-start | bytes 49160 | tf_op jit(solution)/shard_map/ppermute | solution.py:515
  4.9 2.2 %collective-permute-start.1 = (f32[8,512]{1,0:T(8,128)S(1)}, f32[8,512]{1,0:T(8,128)S(1)}, u32[]{:S(2)}, u32[]{:S(2)}) collective-permute-start(f32[8,512]{1,0:T(8,128)S(1)} %get-tuple-element.41.own_ref), channel_id=1, source_target_pairs={{0,4},{1,2},{2,1},{3,7},{4,0},{5,6},{6,5},{7,3},{8,12},{9,10},{10,... | collective-permute-start | bytes 49160 | tf_op jit(solution)/shard_map/ppermute | solution.py:552
  7.4 1.4 %collective-permute-start.3 = (f32[7,32,128]{2,1,0:T(8,128)S(1)}, f32[7,32,128]{2,1,0:T(8,128)S(1)}, u32[]{:S(2)}, u32[]{:S(2)}) collective-permute-start(f32[7,32,128]{2,1,0:T(8,128)S(1)} %get-tuple-element.51), channel_id=1, source_target_pairs={{0,4},{4,0},{8,12},{12,8},{16,20},{20,16},{24,28},{28,24},{32,36},... | collective-permute-start | bytes 344072 | tf_op jit(solution)/shard_map/ppermute | solution.py:515
  8.9 7.7 %collective-permute-start.4 = (f32[6,32,128]{2,1,0:T(8,128)S(1)}, f32[6,32,128]{2,1,0:T(8,128)S(1)}, u32[]{:S(2)}, u32[]{:S(2)}) collective-permute-start(f32[6,32,128]{2,1,0:T(8,128)S(1)} %get-tuple-element.52.after_ref.own_ref), channel_id=1, source_target_pairs={{0,28},{4,16},{8,20},{12,24},{16,4},{20,8},{24,12},{28,0},{32,60},... | collective-permute-start | bytes 294920 | tf_op jit(solution)/shard_map/ppermute | solution.py:525
  10.5 6.0 %collective-permute-start.5 = (f32[6,32,128]{2,1,0:T(8,128)S(1)}, f32[6,32,128]{2,1,0:T(8,128)S(1)}, u32[]{:S(2)}, u32[]{:S(2)}) collective-permute-start(f32[6,32,128]{2,1,0:T(8,128)S(1)} %get-tuple-element.52.after_ref.own_ref), channel_id=1, source_target_pairs={{0,20},{4,24},{8,28},{12,16},{16,12},{20,0},{24,4},{28,8},{32,52},... | collective-permute-start | bytes 294920 | tf_op jit(solution)/shard_map/ppermute | solution.py:525
  10.5 6.6 %collective-permute-start.6 = (f32[6,32,128]{2,1,0:T(8,128)S(1)}, f32[6,32,128]{2,1,0:T(8,128)S(1)}, u32[]{:S(2)}, u32[]{:S(2)}) collective-permute-start(f32[6,32,128]{2,1,0:T(8,128)S(1)} %get-tuple-element.52.after_ref.own_ref), channel_id=1, source_target_pairs={{0,8},{4,12},{8,0},{12,4},{16,24},{20,28},{24,16},{28,20},{32,40},... | collective-permute-start | bytes 294920 | tf_op jit(solution)/shard_map/ppermute | solution.py:525
  17.2 7.2 %collective-permute-start.7 = (f32[5,32,128]{2,1,0:T(8,128)S(1)}, f32[5,32,128]{2,1,0:T(8,128)S(1)}, u32[]{:S(2)}, u32[]{:S(2)}) collective-permute-start(f32[5,32,128]{2,1,0:T(8,128)S(1)} %get-tuple-element.57.after_ref.own_ref), channel_id=1, source_target_pairs={{0,100},{4,64},{8,108},{12,72},{16,84},{20,112},{24,92},{28,120},{... | collective-permute-start | bytes 245768 | tf_op jit(solution)/shard_map/ppermute | solution.py:525
  20.2 5.4 %collective-permute-start.8 = (f32[5,32,128]{2,1,0:T(8,128)S(1)}, f32[5,32,128]{2,1,0:T(8,128)S(1)}, u32[]{:S(2)}, u32[]{:S(2)}) collective-permute-start(f32[5,32,128]{2,1,0:T(8,128)S(1)} %get-tuple-element.57.after_ref.own_ref), channel_id=1, source_target_pairs={{0,68},{4,96},{8,76},{12,104},{16,116},{20,80},{24,124},{28,88},{3... | collective-permute-start | bytes 245768 | tf_op jit(solution)/shard_map/ppermute | solution.py:525
  21.2 4.9 %collective-permute-start.9 = (f32[5,32,128]{2,1,0:T(8,128)S(1)}, f32[5,32,128]{2,1,0:T(8,128)S(1)}, u32[]{:S(2)}, u32[]{:S(2)}) collective-permute-start(f32[5,32,128]{2,1,0:T(8,128)S(1)} %get-tuple-element.57.after_ref.own_ref), channel_id=1, source_target_pairs={{0,32},{4,36},{8,40},{12,44},{16,48},{20,52},{24,56},{28,60},{32,0... | collective-permute-start | bytes 245768 | tf_op jit(solution)/shard_map/ppermute | solution.py:525
  26.2 1.5 %collective-permute-start.10 = (f32[2,32,128]{2,1,0:T(8,128)S(1)}, f32[2,32,128]{2,1,0:T(8,128)S(1)}, u32[]{:S(2)}, u32[]{:S(2)}) collective-permute-start(f32[2,32,128]{2,1,0:T(8,128)S(1)} %get-tuple-element.62), channel_id=1, source_target_pairs={{0,4},{4,0},{8,12},{12,8},{16,20},{20,16},{24,28},{28,24},{32,36},... | collective-permute-start | bytes 98312 | tf_op jit(solution)/shard_map/ppermute | solution.py:515
  28.1 6.0 %collective-permute-start.11 = (f32[8,512]{1,0:T(8,128)S(1)}, f32[8,512]{1,0:T(8,128)S(1)}, u32[]{:S(2)}, u32[]{:S(2)}) collective-permute-start(f32[8,512]{1,0:T(8,128)S(1)} %get-tuple-element.71.own_ref), channel_id=1, source_target_pairs={{0,3},{1,2},{2,1},{3,0},{4,7},{5,6},{6,5},{7,4},{8,11},{9,10},{10,... | collective-permute-start | bytes 49160 | tf_op jit(solution)/shard_map/ppermute | solution.py:515
  31.2 5.2 %collective-permute-start.12 = (f32[8,512]{1,0:T(8,128)S(1)}, f32[8,512]{1,0:T(8,128)S(1)}, u32[]{:S(2)}, u32[]{:S(2)}) collective-permute-start(f32[8,512]{1,0:T(8,128)S(1)} %get-tuple-element.71.own_ref), channel_id=1, source_target_pairs={{0,2},{1,3},{2,0},{3,1},{4,6},{5,7},{6,4},{7,5},{8,10},{9,11},{10,... | collective-permute-start | bytes 49160 | tf_op jit(solution)/shard_map/ppermute | solution.py:515
  32.8 3.7 %collective-permute-start.13 = (f32[8,512]{1,0:T(8,128)S(1)}, f32[8,512]{1,0:T(8,128)S(1)}, u32[]{:S(2)}, u32[]{:S(2)}) collective-permute-start(f32[8,512]{1,0:T(8,128)S(1)} %get-tuple-element.71.own_ref), channel_id=1, source_target_pairs={{0,1},{1,0},{2,3},{3,2},{4,5},{5,4},{6,7},{7,6},{8,9},{9,8},{10,11... | collective-permute-start | bytes 49160 | tf_op jit(solution)/shard_map/ppermute | solution.py:515
